TPU v7x, 512 devices: a whole 4x8x8 slice. The times are simulated.
512 devices in a mesh: hist: 16 (over z, core), items: 32 (over x, y).
Axes of the slice: x: 4, y: 8, z: 8, core: 2. Of those that a mesh axis runs over, the one named last changes fastest.
Arguments:
- history: bfloat16 [32, 2048, 512], P('items', 'hist'), may hold values from -6 to 6
- ln_gain: float32 [512], replicated, may hold values from 0.5 to 1.5
- w_in: bfloat16 [512, 2048], replicated, may hold values from -0.25 to 0.25
- w_out: bfloat16 [512, 512], replicated, may hold values from -0.25 to 0.25
- item_table: bfloat16 [131072, 512], P(('hist', 'items')), may hold values from -6 to 6
- sessions: int32 [32, 16], P('items'), may hold values from 0 to 7, never falling along the last dimension, each value on 1 to 3 neighbouring positions
- pos_owner: int32 [32, 2048, 1], P('items', 'hist'), may hold values from 0 to 511; in each aligned block of 128 rows (0 to 127, 128 to 255, ..., all dimensions but the last counted through in order) at most 2 rows name the same one
- pos_row: int32 [32, 2048], P('items', 'hist'), may hold values from 0 to 255
- neg_rows: int32 [32, 512, 1], P('items'), may hold values from 0 to 254, as said below
Outputs:
- history_grad: bfloat16 [32, 2048, 512], P('items', 'hist')
- table_grad: bfloat16 [131072, 512], P(('hist', 'items'))
Inputs may be any that keep to these rules, and one draw needn't show every extreme that they name: Within a history, sessions are numbered in order, and each session covers 1 to 3 consecutive blocks. `pos_owner`: among the 128 positions of one device, at most 2 name the same owner. `neg_rows`: entry m under owner o is a row of owner o; rows r are drawn with probability 1 / (L 2^b), b = floor(log2(r + 1)), L = floor(log2(256)).
All inputs are finite; a program needn't handle non-finite values.
Results may differ from a plain program's by a relative error of at most 0.018.
Values may be sent and summed in bfloat16 or wider, within the bound.
No kernel may reach another device: no remote copies, remote signals or barrier semaphores. Data moves between devices by JAX's collectives and lax.ppermute only.
A program may use at most 64 MiB of HBM per device.

v0:
```python
import math

import jax
import jax.numpy as jnp
from jax import lax
from jax.sharding import PartitionSpec as P

HEADS = 8
BLOCK = 128


TAU = 0.05


def passed_along(shard, axis, by):
    count = lax.axis_size(axis)
    pairs = [(i, i + by) for i in range(count) if 0 <= i + by < count]
    return lax.ppermute(shard, axis, pairs)


def for_sending(shard):

    def short(part):
        return part.astype(jnp.bfloat16) if part.dtype == jnp.float32 else part

    return jax.tree.map(short, shard)


def silu_slope(value):
    sigma = jax.nn.sigmoid(value)
    return sigma * (1.0 + value * (1.0 - sigma))


def layer_stats(values):
    center = values - jnp.mean(values, axis=-1, keepdims=True)
    scale_inv = lax.rsqrt(jnp.mean(center * center, axis=-1, keepdims=True) + 1e-05)
    return (center * scale_inv, scale_inv)


def norm_back(upstream, normed, scale_inv):
    return scale_inv * (
        upstream
        - jnp.mean(upstream, axis=-1, keepdims=True)
        - normed * jnp.mean(upstream * normed, axis=-1, keepdims=True)
    )


def item_norm(rows_in):
    values = rows_in.astype(jnp.float32)
    lengths = jnp.sqrt(jnp.sum(values * values, axis=-1, keepdims=True) + 1e-06)
    return (values / lengths, lengths)


def sample_shift(neg_flat, levels, per_owner):
    powers = jnp.left_shift(
        jnp.ones((levels - 1,), jnp.int32), jnp.arange(1, levels, dtype=jnp.int32)
    )
    exponent = jnp.sum((neg_flat[:, None] + 1 >= powers[None, :]).astype(jnp.float32), axis=1)
    return math.log(levels) - math.log(per_owner) + exponent * math.log(2.0)


def split_heads(matrix):
    return matrix.reshape(matrix.shape[0], HEADS, -1).transpose(1, 0, 2)


def merge_heads(stacked):
    return stacked.transpose(1, 0, 2).reshape(stacked.shape[1], -1)


def allowed_pairs(q_places, q_sess, k_places, k_sess):
    return (
        (k_places[None, :] <= q_places[:, None])
        & (k_sess[None, :] == q_sess[:, None])
        & (k_sess[None, :] >= 0)
    ).astype(jnp.float32)


def attend(queries, keys_in, values_in, allowed, inverse):
    score_scale = 1.0 / math.sqrt(queries.shape[1] // HEADS)

    def attend_one_head(head_parts):
        query_h, key_h, value_h = head_parts
        scores = jnp.dot(query_h, key_h.T, preferred_element_type=jnp.float32) * score_scale
        weights = (jax.nn.silu(scores) * allowed * inverse[:, None]).astype(jnp.bfloat16)
        return jnp.dot(weights, value_h, preferred_element_type=jnp.float32)

    return merge_heads(
        lax.map(
            attend_one_head, (split_heads(queries), split_heads(keys_in), split_heads(values_in))
        )
    )


def head_grads(queries, keys_in, values_in, upstream, allowed, inverse):
    score_scale = 1.0 / math.sqrt(queries.shape[1] // HEADS)

    def head_one_head(head_parts):
        query_h, key_h, value_h, grad_h = head_parts
        scores = jnp.dot(query_h, key_h.T, preferred_element_type=jnp.float32) * score_scale
        weight_grad = jnp.dot(grad_h, value_h.T, preferred_element_type=jnp.float32)
        score_grad = (
            weight_grad * silu_slope(scores) * allowed * inverse[:, None] * score_scale
        ).astype(jnp.bfloat16)
        results = []
        results.append(jnp.dot(score_grad, key_h, preferred_element_type=jnp.float32))
        weights = (jax.nn.silu(scores) * allowed * inverse[:, None]).astype(jnp.bfloat16)
        results.append(jnp.dot(score_grad.T, query_h, preferred_element_type=jnp.float32))
        results.append(jnp.dot(weights.T, grad_h, preferred_element_type=jnp.float32))
        return tuple(results)

    stacked = lax.map(
        head_one_head,
        (split_heads(queries), split_heads(keys_in), split_heads(values_in), split_heads(upstream)),
    )
    return [merge_heads(member) for member in stacked]


def on_device(history, ln_gain, w_in, w_out, item_table, sessions, pos_owner, pos_row, neg_rows):
    tok_rows = history.shape[1]
    width_d = history.shape[2]
    blocks_dev = tok_rows // BLOCK
    hist_index = lax.axis_index("hist")
    hist_count = lax.axis_size("hist")
    item_count = lax.axis_size("items")
    owner_count = hist_count * item_count
    capacity = max(2, 2 * tok_rows // owner_count)
    local_rows = item_table.shape[0]
    hist_f = history[0].astype(jnp.float32)
    normed_x, scale_x = layer_stats(hist_f)
    normed_in = (normed_x * ln_gain).astype(jnp.bfloat16)
    projected = jnp.dot(normed_in, w_in, preferred_element_type=jnp.float32)
    activated = jax.nn.silu(projected).astype(jnp.bfloat16)
    gate_u, value_v, query_q, key_k = jnp.split(activated, 4, axis=1)
    session_ids = sessions[0]
    start_blk = jnp.sum((session_ids[None, :] < session_ids[:, None]).astype(jnp.int32), axis=1)
    padded_sess = jnp.concatenate(
        [
            jnp.full((2 * blocks_dev,), -1, jnp.int32),
            session_ids,
            jnp.full((2 * blocks_dev,), -2, jnp.int32),
        ]
    )
    padded_start = jnp.concatenate(
        [
            jnp.zeros((2 * blocks_dev,), jnp.int32),
            start_blk,
            jnp.zeros((2 * blocks_dev,), jnp.int32),
        ]
    )

    def block_span(first_block, count):
        sess_blocks = lax.dynamic_slice_in_dim(padded_sess, first_block + 2 * blocks_dev, count)
        start_blocks = lax.dynamic_slice_in_dim(padded_start, first_block + 2 * blocks_dev, count)
        places = first_block * BLOCK + jnp.arange(count * BLOCK, dtype=jnp.int32)
        counts = places - BLOCK * jnp.repeat(start_blocks, BLOCK) + 1
        return (places, jnp.repeat(sess_blocks, BLOCK), counts)

    q_places, q_sess, q_counts = block_span(hist_index * blocks_dev, blocks_dev)
    inverse_q = 1.0 / q_counts.astype(jnp.float32)

    def previous(pair, depth):
        return passed_along((pair[0], pair[1]), "hist", depth)

    key_far, value_far = previous((key_k, value_v), 2)
    key_near, value_near = previous((key_k, value_v), 1)
    key_win = jnp.concatenate([key_far, key_near, key_k])
    value_win = jnp.concatenate([value_far, value_near, value_v])
    k_places, k_sess, k_unused = block_span((hist_index - 2) * blocks_dev, 3 * blocks_dev)
    allowed_q = allowed_pairs(q_places, q_sess, k_places, k_sess)
    attended = attend(query_q, key_win, value_win, allowed_q, inverse_q)
    attn_hat, scale_a = layer_stats(attended)
    gated = (attn_hat * gate_u.astype(jnp.float32)).astype(jnp.bfloat16)
    user_out = jnp.dot(gated, w_out, preferred_element_type=jnp.float32) + hist_f
    user_len = jnp.sqrt(jnp.sum(user_out * user_out, axis=-1, keepdims=True) + 1e-06)
    user_unit = user_out / user_len
    user_bf = user_unit.astype(jnp.bfloat16)
    owner_ids = pos_owner[0, :, 0]
    owner_rows = pos_row[0]
    order = jnp.arange(tok_rows, dtype=jnp.int32)
    same_owner = (owner_ids[:, None] == owner_ids[None, :]) & (order[None, :] < order[:, None])
    slot_rank = jnp.sum(same_owner.astype(jnp.int32), axis=1)
    wanted = jnp.zeros((owner_count, capacity), jnp.int32).at[owner_ids, slot_rank].set(owner_rows)
    negative_rows = neg_rows[0]
    neg_count = negative_rows.shape[1]
    asking = jnp.concatenate([wanted, negative_rows], axis=1)
    slots = asking.shape[1]
    asked = lax.all_to_all(
        lax.all_to_all(
            asking.reshape(hist_count, item_count, slots),
            "hist",
            split_axis=0,
            concat_axis=0,
            tiled=True,
        ),
        "items",
        split_axis=1,
        concat_axis=1,
        tiled=True,
    )
    served = item_table[asked]
    fetched = lax.all_to_all(
        lax.all_to_all(served, "hist", split_axis=0, concat_axis=0, tiled=True),
        "items",
        split_axis=1,
        concat_axis=1,
        tiled=True,
    ).reshape(owner_count, slots, width_d)
    pos_rows_in = fetched[owner_ids, slot_rank]
    neg_rows_in = fetched[:, capacity:].reshape(-1, width_d)
    pos_unit, pos_len = item_norm(pos_rows_in)
    neg_unit, neg_len = item_norm(neg_rows_in)
    pos_bf = pos_unit.astype(jnp.bfloat16)
    neg_bf = neg_unit.astype(jnp.bfloat16)
    levels = local_rows.bit_length() - 1
    shift_terms = sample_shift(negative_rows.reshape(-1), levels, neg_count)
    pos_logit = jnp.sum(user_bf.astype(jnp.float32) * pos_bf.astype(jnp.float32), axis=-1) / TAU
    neg_logit = (
        jnp.dot(user_bf, neg_bf.T, preferred_element_type=jnp.float32) / TAU + shift_terms[None, :]
    )
    pos_exp = jnp.exp(pos_logit)
    neg_exp = jnp.exp(neg_logit)
    denominator = pos_exp + jnp.sum(neg_exp, axis=1)
    pos_delta = pos_exp / denominator - 1.0
    neg_prob = (neg_exp / denominator[:, None]).astype(jnp.bfloat16)
    unit_grad = (
        pos_delta[:, None] * pos_bf.astype(jnp.float32)
        + jnp.dot(neg_prob, neg_bf, preferred_element_type=jnp.float32)
    ) / TAU
    user_grad = (
        unit_grad - user_unit * jnp.sum(user_unit * unit_grad, axis=-1, keepdims=True)
    ) / user_len
    raw_pos = pos_delta[:, None] * user_bf.astype(jnp.float32) / TAU
    pos_grad = (raw_pos - pos_unit * jnp.sum(pos_unit * raw_pos, axis=-1, keepdims=True)) / pos_len
    raw_neg = jnp.dot(neg_prob.T, user_bf, preferred_element_type=jnp.float32) / TAU
    neg_grad = (raw_neg - neg_unit * jnp.sum(neg_unit * raw_neg, axis=-1, keepdims=True)) / neg_len
    slot_grads = (
        jnp.zeros((owner_count, capacity, width_d), jnp.float32)
        .at[owner_ids, slot_rank]
        .set(pos_grad)
    )
    sending = jnp.concatenate(
        [slot_grads, neg_grad.reshape(owner_count, neg_count, width_d)], axis=1
    )
    returned = lax.all_to_all(
        lax.all_to_all(
            sending.reshape(hist_count, item_count, slots, width_d).astype(jnp.bfloat16),
            "hist",
            split_axis=0,
            concat_axis=0,
            tiled=True,
        ),
        "items",
        split_axis=1,
        concat_axis=1,
        tiled=True,
    ).astype(jnp.float32)
    owner_grad = jax.ops.segment_sum(
        returned.reshape(-1, width_d), asked.reshape(-1), num_segments=local_rows
    )
    table_grad = owner_grad.astype(jnp.bfloat16)
    user_grad_bf = user_grad.astype(jnp.bfloat16)
    gated_grad = jnp.dot(user_grad_bf, w_out.T, preferred_element_type=jnp.float32)
    gate_grad = gated_grad * attn_hat
    hat_grad = gated_grad * gate_u.astype(jnp.float32)
    attended_grad = norm_back(hat_grad, attn_hat, scale_a).astype(jnp.bfloat16)
    query_grad, key_grad_win, value_grad_win = head_grads(
        query_q, key_win, value_win, attended_grad, allowed_q, inverse_q
    )

    def returning(pair, depth):
        return passed_along((for_sending(pair[0]), for_sending(pair[1])), "hist", -depth)

    far_key, far_value = returning((key_grad_win[:tok_rows], value_grad_win[:tok_rows]), 2)
    near_key, near_value = returning(
        (key_grad_win[tok_rows : 2 * tok_rows], value_grad_win[tok_rows : 2 * tok_rows]), 1
    )
    key_grad = key_grad_win[2 * tok_rows :] + near_key + far_key
    value_grad = value_grad_win[2 * tok_rows :] + near_value + far_value
    act_grad = jnp.concatenate([gate_grad, value_grad, query_grad, key_grad], axis=1)
    proj_grad = (act_grad * silu_slope(projected)).astype(jnp.bfloat16)
    in_grad = jnp.dot(proj_grad, w_in.T, preferred_element_type=jnp.float32)
    history_grad = norm_back(in_grad * ln_gain, normed_x, scale_x) + user_grad
    return (history_grad.astype(jnp.bfloat16)[None], table_grad)


def solution(mesh):
    return jax.shard_map(
        on_device,
        mesh=mesh,
        in_specs=(
            P("items", "hist", None),
            P(),
            P(),
            P(),
            P(("hist", "items"), None),
            P("items", None),
            P("items", "hist", None),
            P("items", "hist"),
            P("items", None, None),
        ),
        out_specs=(P("items", "hist", None), P(("hist", "items"), None)),
        check_vma=False,
    )
```

profile of v0, /device:TPU:1, one launch (start us, length us, event | category | flops | bytes accessed | tf_op | source)
XLA Modules:
  0.0 357.3 jit_solution(16216363324880526879)
XLA Ops:
  4.2 10.9 %scatter_fusion = s32[512,2]{0,1:T(2,128)S(1)} fusion(s32[512,2]{0,1:T(2,128)S(1)} %broadcast_in_dim.30, s32[128]{0:T(128)S(1)} %get-tuple-element.360, s32[128]{0:T(128)} %bitcast.234), kind=kCustom, calls=%fused_computation.2 | custom fusion | bytes 2560 | tf_op jit(solution)/shard_map/scatter | solution.py:182
  15.2 19.0 %all_to_all.30 = s32[16,32,3]{1,2,0:T(4,128)S(1)} all-to-all(s32[16,32,3]{1,2,0:T(4,128)S(1)} %copy.143), channel_id=1, replica_groups=mesh['hist'=16,'items'=32] {'hist'}, dimensions={0} | all-to-all | bytes 12288 | tf_op jit(solution)/shard_map/all_to_all | solution.py:188
  34.3 18.3 %all_to_all.31 = s32[16,32,3]{0,2,1:T(4,128)S(1)} all-to-all(s32[16,32,3]{0,2,1:T(4,128)S(1)} %copy.144), channel_id=1, replica_groups=mesh['hist'=16,'items'=32] {'items'}, dimensions={1} | all-to-all | bytes 12288 | tf_op jit(solution)/shard_map/all_to_all | solution.py:187
  53.9 5.4 %gather_fusion = bf16[1536,512]{1,0:T(8,128)(2,1)} fusion(bf16[256,512]{1,0:T(8,128)(2,1)S(1)} %copy-done.1, s32[2048]{0:T(1024)S(1)} %pad_clamp_fusion), kind=kCustom, calls=%fused_computation | custom fusion | bytes 3151872 | tf_op jit(solution)/shard_map/gather | solution.py:200
  59.3 5.2 %reshape.253 = bf16[16,32,3,512]{3,2,1,0:T(4,128)(2,1)} reshape(bf16[1536,512]{1,0:T(8,128)(2,1)} %gather_fusion) | data formatting | bytes 3145728 | tf_op jit(solution)/shard_map/gather | solution.py:200
  64.4 3.2 copy.146
  67.7 6.1 %all-to-all-start.2 = ((bf16[16,32,3,512]{3,1,2,0:T(8,128)(2,1)}), bf16[16,32,3,512]{3,1,2,0:T(8,128)(2,1)}, u32[]{:S(2)}, u32[]{:S(2)}) async-start(bf16[16,32,3,512]{3,1,2,0:T(8,128)(2,1)} %copy.146), calls=%async_computation.2 | async-start | bytes 3145728 | tf_op jit(solution)/shard_map/all_to_all | solution.py:202
  75.7 3.5 collective-permute-start.1
  79.3 3.8 %collective-permute-start = (bf16[128,512]{1,0:T(8,128)(2,1)S(1)}, bf16[128,512]{1,0:T(8,128)(2,1)}, u32[]{:S(2)}, u32[]{:S(2)}) collective-permute-start(bf16[128,512]{1,0:T(8,128)(2,1)S(1)} %get-tuple-element.349), channel_id=1, source_target_pairs={{0,64},{32,96},{64,128},{96,160},{128,192},{160,224},{192,256},{22... | collective-permute-start | bytes 393224 | tf_op jit(solution)/shard_map/ppermute | solution.py:18
  83.0 1.9 collective-permute-start.3
  84.9 3.6 collective-permute-start.2
  93.4 17.3 %collective-permute-done.1 = bf16[128,512]{1,0:T(8,128)(2,1)} collective-permute-done((bf16[128,512]{1,0:T(8,128)(2,1)S(1)}, bf16[128,512]{1,0:T(8,128)(2,1)}, u32[]{:S(2)}, u32[]{:S(2)}) %collective-permute-start.1) | collective-permute-done | bytes 131104 | tf_op jit(solution)/shard_map/ppermute | solution.py:18
  110.7 2.8 collective-permute-done
  116.9 1.7 pad_maximum_fusion.2
  118.6 1.9 copy.138
  120.5 2.1 copy.141
  122.7 3.4 copy.147
  126.1 5.0 %all-to-all-start.3 = ((bf16[16,32,3,512]{3,0,2,1:T(8,128)(2,1)}), bf16[16,32,3,512]{3,0,2,1:T(8,128)(2,1)}, u32[]{:S(2)}, u32[]{:S(2)}) async-start(bf16[16,32,3,512]{3,0,2,1:T(8,128)(2,1)} %copy.147), calls=%async_computation.3 | async-start | bytes 3145728 | tf_op jit(solution)/shard_map/all_to_all | solution.py:201
  131.2 14.6 %while.26 = (s32[]{:T(128)}, f32[8,128,64]{1,2,0:T(8,128)S(1)}, bf16[8,128,64]{2,1,0:T(8,128)(2,1)S(1)}, bf16[8,384,64]{2,1,0:T(8,128)(2,1)S(1)}, bf16[8,384,64]...) while((s32[]{:T(128)}, f32[8,128,64]{1,2,0:T(8,128)S(1)}, ...), condition=%wide.region_4.5_spmd.clone, body=%wide.region_3.4_spmd.clone.sunk | while | flops 13124226 | bytes 268933 | solution.py:88
  150.0 19.1 %all-to-all-done.3 = bf16[16,32,3,512]{3,0,2,1:T(8,128)(2,1)} async-done(((bf16[16,32,3,512]{3,0,2,1:T(8,128)(2,1)}), bf16[16,32,3,512]{3,0,2,1:T(8,128)(2,1)}, u32[]{:S(2)}, u32[]{:S(2)}) %all-to-all-start.3) | async-done | bytes 1572896 | tf_op jit(solution)/shard_map/all_to_all | solution.py:201
  169.2 2.3 copy.148
  172.8 2.1 gather_fusion.1
  175.8 2.2 fusion.137
  179.9 1.9 broadcast_in_dim.34
  181.8 15.7 %scatter_fusion.1 = f32[512,2,512]{2,1,0:T(2,128)} fusion(f32[512,2,512]{2,1,0:T(2,128)} %broadcast_in_dim.34, s32[128]{0:T(128)S(1)} %get-tuple-element.360, f32[128,512]{1,0:T(8,128)} %fusion.98), kind=kCustom, calls=%fused_computation.3 | custom fusion | bytes 787456 | tf_op jit(solution)/shard_map/scatter | solution.py:239
  197.5 2.3 convert.20
  203.5 8.7 %all-to-all-start.4 = ((bf16[16,32,3,512]{3,1,2,0:T(8,128)(2,1)}), bf16[16,32,3,512]{3,1,2,0:T(8,128)(2,1)}, u32[]{:S(2)}, u32[]{:S(2)}) async-start(bf16[16,32,3,512]{3,1,2,0:T(8,128)(2,1)} %copy.163), calls=%async_computation.4 | async-start | bytes 3145728 | tf_op jit(solution)/shard_map/all_to_all | solution.py:245
  213.2 1.7 reshape.280
  215.0 1.6 multiply_reduce_fusion.2
  218.8 31.9 %all-to-all-done.4 = bf16[16,32,3,512]{3,1,2,0:T(8,128)(2,1)} async-done(((bf16[16,32,3,512]{3,1,2,0:T(8,128)(2,1)}), bf16[16,32,3,512]{3,1,2,0:T(8,128)(2,1)}, u32[]{:S(2)}, u32[]{:S(2)}) %all-to-all-start.4) | async-done | bytes 1572896 | tf_op jit(solution)/shard_map/all_to_all | solution.py:245
  250.7 3.4 copy.164
  254.1 6.5 %all-to-all-start.5 = ((bf16[16,32,3,512]{3,0,2,1:T(8,128)(2,1)}), bf16[16,32,3,512]{3,0,2,1:T(8,128)(2,1)}, u32[]{:S(2)}, u32[]{:S(2)}) async-start(bf16[16,32,3,512]{3,0,2,1:T(8,128)(2,1)} %copy.164), calls=%async_computation.5 | async-start | bytes 3145728 | tf_op jit(solution)/shard_map/all_to_all | solution.py:244
  260.7 44.3 %while.27 = (s32[]{:T(128)}, f32[8,128,64]{1,2,0:T(8,128)S(1)}, f32[8,384,64]{1,2,0:T(8,128)}, f32[8,384,64]{1,2,0:T(8,128)}, bf16[8,128,64]{1,2,0:T(8,128)(2,1)...) while((s32[]{:T(128)}, f32[8,128,64]{1,2,0:T(8,128)S(1)}, ...), condition=%wide.region_19.20_spmd.clone, body=%wide.region_18.19_spmd.clone.sunk | while | flops 32735872 | bytes 1521849 | solution.py:111
  264.6 1.6 fusion.181
  275.7 1.6 fusion.181
  279.7 1.6 fusion.180
  281.3 1.6 fusion.181
  309.7 1.7 slice.56
  312.5 1.7 copy.157
  314.2 1.9 collective-permute-start.6
  316.1 1.8 copy.160
  318.7 1.7 copy.156
  324.5 2.3 collective-permute-start.4
  328.6 3.3 collective-permute-done.4
  332.9 1.7 fusion.132
  335.5 4.7 %copy.165 = f32[16,32,3,512]{3,2,1,0:T(4,128)} copy(bf16[16,32,3,512]{3,0,2,1:T(8,128)(2,1)} %all-to-all-done.5) | data formatting | bytes 4718592 | tf_op jit(solution)/shard_map/reshape | solution.py:258
  340.2 6.0 %reshape.282 = f32[1536,512]{1,0:T(8,128)} reshape(f32[16,32,3,512]{3,2,1,0:T(4,128)} %copy.165) | data formatting | bytes 6291456 | tf_op jit(solution)/shard_map/reshape | solution.py:258
  346.2 10.4 %scatter_custom_fusion.2 = f32[256,512]{1,0:T(8,128)S(1)} fusion(s32[1536]{0:T(1024)} %reshape.280, f32[1536,512]{1,0:T(8,128)} %reshape.282, f32[]{:T(128)} %constant.54.clone.1), kind=kCustom, calls=%fused_computation.136 | custom fusion | flops 786432 | bytes 524800 | tf_op jit(solution)/shard_map/scatter-add | solution.py:257
  (252 shorter events, 96.6 us)
Async XLA Ops:
  0.6 73.5 %copy-start = (bf16[512,2048]{1,0:T(8,128)(2,1)S(1)}, bf16[512,2048]{1,0:T(8,128)(2,1)}, u32[]{:S(2)}) copy-start(bf16[512,2048]{1,0:T(8,128)(2,1)} %param.15) | copy-start | bytes 6291460
  0.6 53.2 %copy-start.1 = (bf16[256,512]{1,0:T(8,128)(2,1)S(1)}, bf16[256,512]{1,0:T(8,128)(2,1)}, u32[]{:S(2)}) copy-start(bf16[256,512]{1,0:T(8,128)(2,1)} %param.17) | copy-start | bytes 786436
  67.7 6.1 %copy-start.5 = (bf16[1,128,512]{2,1,0:T(8,128)(2,1)S(1)}, bf16[1,128,512]{2,1,0:T(8,128)(2,1)}, u32[]{:S(2)}) copy-start(bf16[1,128,512]{2,1,0:T(8,128)(2,1)} %param.13) | copy-start | bytes 393220
  67.7 6.4 %copy-start.38 = (f32[512]{0:T(512)S(1)}, f32[512]{0:T(512)}, u32[]{:S(2)}) copy-start(f32[512]{0:T(512)} %param.14) | copy-start | bytes 6148
  67.7 55.0 %all-to-all-start.2 = ((bf16[16,32,3,512]{3,1,2,0:T(8,128)(2,1)}), bf16[16,32,3,512]{3,1,2,0:T(8,128)(2,1)}, u32[]{:S(2)}, u32[]{:S(2)}) async-start(bf16[16,32,3,512]{3,1,2,0:T(8,128)(2,1)} %copy.146), calls=%async_computation.2 | async-start | bytes 3145728 | tf_op jit(solution)/shard_map/all_to_all | solution.py:202
  73.9 1.8 copy-start.20
  74.1 14.4 %copy-start.32 = (s32[1,16]{1,0:T(1,128)S(1)}, s32[1,16]{1,0:T(1,128)}, u32[]{:S(2)}) copy-start(s32[1,16]{1,0:T(1,128)} %param.18) | copy-start | bytes 196
  75.7 35.1 %copy-start.9 = (bf16[128,2048]{1,0:T(8,128)(2,1)}, bf16[128,2048]{1,0:T(8,128)(2,1)S(1)}, u32[]{:S(2)}) copy-start(bf16[128,2048]{1,0:T(8,128)(2,1)S(1)} %get-tuple-element.363) | copy-start | bytes 1572868
  75.7 35.0 %collective-permute-start.1 = (bf16[128,512]{1,0:T(8,128)(2,1)S(1)}, bf16[128,512]{1,0:T(8,128)(2,1)}, u32[]{:S(2)}, u32[]{:S(2)}) collective-permute-start(bf16[128,512]{1,0:T(8,128)(2,1)S(1)} %get-tuple-element.349), channel_id=1, source_target_pairs={{0,32},{32,64},{64,96},{96,128},{128,160},{160,192},{192,224},{224... | collective-permute-start | bytes 393224 | tf_op jit(solution)/shard_map/ppermute | solution.py:18
  79.3 34.3 %collective-permute-start = (bf16[128,512]{1,0:T(8,128)(2,1)S(1)}, bf16[128,512]{1,0:T(8,128)(2,1)}, u32[]{:S(2)}, u32[]{:S(2)}) collective-permute-start(bf16[128,512]{1,0:T(8,128)(2,1)S(1)} %get-tuple-element.349), channel_id=1, source_target_pairs={{0,64},{32,96},{64,128},{96,160},{128,192},{160,224},{192,256},{22... | collective-permute-start | bytes 393224 | tf_op jit(solution)/shard_map/ppermute | solution.py:18
  83.0 33.8 %collective-permute-start.3 = (bf16[128,512]{1,0:T(8,128)(2,1)S(1)}, bf16[128,512]{1,0:T(8,128)(2,1)}, u32[]{:S(2)}, u32[]{:S(2)}) collective-permute-start(bf16[128,512]{1,0:T(8,128)(2,1)S(1)} %get-tuple-element.348), channel_id=1, source_target_pairs={{0,32},{32,64},{64,96},{96,128},{128,160},{160,192},{192,224},{224... | collective-permute-start | bytes 393224 | tf_op jit(solution)/shard_map/ppermute | solution.py:18
  84.9 31.9 %collective-permute-start.2 = (bf16[128,512]{1,0:T(8,128)(2,1)S(1)}, bf16[128,512]{1,0:T(8,128)(2,1)}, u32[]{:S(2)}, u32[]{:S(2)}) collective-permute-start(bf16[128,512]{1,0:T(8,128)(2,1)S(1)} %get-tuple-element.348), channel_id=1, source_target_pairs={{0,64},{32,96},{64,128},{96,160},{128,192},{160,224},{192,256},{22... | collective-permute-start | bytes 393224 | tf_op jit(solution)/shard_map/ppermute | solution.py:18
  126.1 5.1 %copy-start.33 = (pred[384]{0:T(512)(128)(4,1)S(1)}, pred[384]{0:T(512)(128)(4,1)}, u32[]{:S(2)}) copy-start(pred[384]{0:T(512)(128)(4,1)} %get-tuple-element.576) | copy-start | bytes 1156
  126.1 43.1 %all-to-all-start.3 = ((bf16[16,32,3,512]{3,0,2,1:T(8,128)(2,1)}), bf16[16,32,3,512]{3,0,2,1:T(8,128)(2,1)}, u32[]{:S(2)}, u32[]{:S(2)}) async-start(bf16[16,32,3,512]{3,0,2,1:T(8,128)(2,1)} %copy.147), calls=%async_computation.3 | async-start | bytes 3145728 | tf_op jit(solution)/shard_map/all_to_all | solution.py:201
  203.5 8.7 %copy-start.12 = (s32[16,32,3]{0,2,1:T(4,128)S(1)}, s32[16,32,3]{0,2,1:T(4,128)}, u32[]{:S(2)}) copy-start(s32[16,32,3]{0,2,1:T(4,128)} %copy-done.11) | copy-start | bytes 18436
  203.5 11.5 %copy-start.19 = (f32[128]{0:T(128)S(1)}, f32[128]{0:T(128)}, u32[]{:S(2)}) copy-start(f32[128]{0:T(128)} %copy-done.18) | copy-start | bytes 1540
  203.5 11.5 %copy-start.22 = (f32[128]{0:T(128)S(1)}, f32[128]{0:T(128)}, u32[]{:S(2)}) copy-start(f32[128]{0:T(128)} %add_sqrt_fusion.2) | copy-start | bytes 1540
  203.5 11.5 %copy-start.37 = (f32[128]{0:T(128)S(1)}, f32[128]{0:T(128)}, u32[]{:S(2)}) copy-start(f32[128]{0:T(128)} %get-tuple-element.357) | copy-start | bytes 1540
  203.5 47.2 %all-to-all-start.4 = ((bf16[16,32,3,512]{3,1,2,0:T(8,128)(2,1)}), bf16[16,32,3,512]{3,1,2,0:T(8,128)(2,1)}, u32[]{:S(2)}, u32[]{:S(2)}) async-start(bf16[16,32,3,512]{3,1,2,0:T(8,128)(2,1)} %copy.163), calls=%async_computation.4 | async-start | bytes 3145728 | tf_op jit(solution)/shard_map/all_to_all | solution.py:245
  215.0 1.7 copy-start.4
  215.0 1.7 copy-start.10
  215.0 1.7 copy-start.13
  215.0 1.7 copy-start.25
  254.1 6.5 %copy-start.27 = (s32[384]{0:T(512)S(1)}, s32[384]{0:T(512)}, u32[]{:S(2)}) copy-start(s32[384]{0:T(512)} %copy-done.26) | copy-start | bytes 4612
  254.1 6.6 %copy-start.34 = (pred[384]{0:T(512)(128)(4,1)S(1)}, pred[384]{0:T(512)(128)(4,1)}, u32[]{:S(2)}) copy-start(pred[384]{0:T(512)(128)(4,1)} %get-tuple-element.576) | copy-start | bytes 1156
  254.1 6.6 %copy-start.35 = (pred[384]{0:T(512)(128)(4,1)S(1)}, pred[384]{0:T(512)(128)(4,1)}, u32[]{:S(2)}) copy-start(pred[384]{0:T(512)(128)(4,1)} %get-tuple-element.631) | copy-start | bytes 1156
  254.1 81.4 %all-to-all-start.5 = ((bf16[16,32,3,512]{3,0,2,1:T(8,128)(2,1)}), bf16[16,32,3,512]{3,0,2,1:T(8,128)(2,1)}, u32[]{:S(2)}, u32[]{:S(2)}) async-start(bf16[16,32,3,512]{3,0,2,1:T(8,128)(2,1)} %copy.164), calls=%async_computation.5 | async-start | bytes 3145728 | tf_op jit(solution)/shard_map/all_to_all | solution.py:244
  260.7 3.9 %copy-start.39 = (s32[128]{0:T(128)S(1)}, s32[128]{0:T(128)}, u32[]{:S(2)}) copy-start(s32[128]{0:T(128)} %get-tuple-element.603) | copy-start | bytes 1540 | tf_op jit(solution)/shard_map/while
  266.3 3.9 %copy-start.39 = (s32[128]{0:T(128)S(1)}, s32[128]{0:T(128)}, u32[]{:S(2)}) copy-start(s32[128]{0:T(128)} %get-tuple-element.603) | copy-start | bytes 1540 | tf_op jit(solution)/shard_map/while
  271.8 3.9 %copy-start.39 = (s32[128]{0:T(128)S(1)}, s32[128]{0:T(128)}, u32[]{:S(2)}) copy-start(s32[128]{0:T(128)} %get-tuple-element.603) | copy-start | bytes 1540 | tf_op jit(solution)/shard_map/while
  277.3 3.9 %copy-start.39 = (s32[128]{0:T(128)S(1)}, s32[128]{0:T(128)}, u32[]{:S(2)}) copy-start(s32[128]{0:T(128)} %get-tuple-element.603) | copy-start | bytes 1540 | tf_op jit(solution)/shard_map/while
  282.9 3.9 %copy-start.39 = (s32[128]{0:T(128)S(1)}, s32[128]{0:T(128)}, u32[]{:S(2)}) copy-start(s32[128]{0:T(128)} %get-tuple-element.603) | copy-start | bytes 1540 | tf_op jit(solution)/shard_map/while
  288.4 3.9 %copy-start.39 = (s32[128]{0:T(128)S(1)}, s32[128]{0:T(128)}, u32[]{:S(2)}) copy-start(s32[128]{0:T(128)} %get-tuple-element.603) | copy-start | bytes 1540 | tf_op jit(solution)/shard_map/while
  294.0 3.9 %copy-start.39 = (s32[128]{0:T(128)S(1)}, s32[128]{0:T(128)}, u32[]{:S(2)}) copy-start(s32[128]{0:T(128)} %get-tuple-element.603) | copy-start | bytes 1540 | tf_op jit(solution)/shard_map/while
  299.5 3.9 %copy-start.39 = (s32[128]{0:T(128)S(1)}, s32[128]{0:T(128)}, u32[]{:S(2)}) copy-start(s32[128]{0:T(128)} %get-tuple-element.603) | copy-start | bytes 1540 | tf_op jit(solution)/shard_map/while
  306.9 10.9 %copy-start.6 = (f32[8,384,64]{1,2,0:T(8,128)S(1)}, f32[8,384,64]{1,2,0:T(8,128)}, u32[]{:S(2)}) copy-start(f32[8,384,64]{1,2,0:T(8,128)} %get-tuple-element.94) | copy-start | bytes 2359300
  308.4 18.4 %collective-permute-start.7 = (bf16[128,512]{1,0:T(8,128)(2,1)}, bf16[128,512]{1,0:T(8,128)(2,1)}, u32[]{:S(2)}, u32[]{:S(2)}) collective-permute-start(bf16[128,512]{1,0:T(8,128)(2,1)} %copy.159), channel_id=1, source_target_pairs={{64,0},{96,32},{128,64},{160,96},{192,128},{224,160},{256,192},{28... | collective-permute-start | bytes 393224 | tf_op jit(solution)/shard_map/ppermute | solution.py:18
  314.2 12.7 %collective-permute-start.6 = (bf16[128,512]{1,0:T(8,128)(2,1)}, bf16[128,512]{1,0:T(8,128)(2,1)}, u32[]{:S(2)}, u32[]{:S(2)}) collective-permute-start(bf16[128,512]{1,0:T(8,128)(2,1)} %copy.157), channel_id=1, source_target_pairs={{32,0},{64,32},{96,64},{128,96},{160,128},{192,160},{224,192},{256... | collective-permute-start | bytes 393224 | tf_op jit(solution)/shard_map/ppermute | solution.py:18
  318.7 14.2 %copy-start.21 = (f32[128]{0:T(128)S(1)}, f32[128]{0:T(128)}, u32[]{:S(2)}) copy-start(f32[128]{0:T(128)} %copy-done.20) | copy-start | bytes 1540
  318.7 14.2 %copy-start.29 = (f32[128]{0:T(128)S(1)}, f32[128]{0:T(128)}, u32[]{:S(2)}) copy-start(f32[128]{0:T(128)} %copy-done.28) | copy-start | bytes 1540
  320.4 8.2 %collective-permute-start.5 = (bf16[128,512]{1,0:T(8,128)(2,1)}, bf16[128,512]{1,0:T(8,128)(2,1)}, u32[]{:S(2)}, u32[]{:S(2)}) collective-permute-start(bf16[128,512]{1,0:T(8,128)(2,1)} %copy.156), channel_id=1, source_target_pairs={{64,0},{96,32},{128,64},{160,96},{192,128},{224,160},{256,192},{28... | collective-permute-start | bytes 393224 | tf_op jit(solution)/shard_map/ppermute | solution.py:18
  324.5 8.4 %copy-start.16 = (f32[128,512]{1,0:T(8,128)S(1)}, f32[128,512]{1,0:T(8,128)}, u32[]{:S(2)}) copy-start(f32[128,512]{1,0:T(8,128)} %copy.160) | copy-start | bytes 786436
  324.5 8.4 %copy-start.17 = (f32[128,512]{1,0:T(8,128)S(1)}, f32[128,512]{1,0:T(8,128)}, u32[]{:S(2)}) copy-start(f32[128,512]{1,0:T(8,128)} %get-tuple-element.346) | copy-start | bytes 786436
  324.5 8.4 %copy-start.40 = (f32[128,2048]{1,0:T(8,128)S(1)}, f32[128,2048]{1,0:T(8,128)}, u32[]{:S(2)}) copy-start(f32[128,2048]{1,0:T(8,128)} %get-tuple-element.364) | copy-start | bytes 3145732
  324.5 7.4 %collective-permute-start.4 = (bf16[128,512]{1,0:T(8,128)(2,1)S(1)}, bf16[128,512]{1,0:T(8,128)(2,1)S(1)}, u32[]{:S(2)}, u32[]{:S(2)}) collective-permute-start(bf16[128,512]{1,0:T(8,128)(2,1)S(1)} %copy.154), channel_id=1, source_target_pairs={{32,0},{64,32},{96,64},{128,96},{160,128},{192,160},{224,192},{256... | collective-permute-start | bytes 393224 | tf_op jit(solution)/shard_map/ppermute | solution.py:18
  332.9 1.7 copy-start.15
  332.9 1.7 copy-start.23
  332.9 1.7 copy-start.31
  (13 other events, 14.2 us)
where the time goes:
time: 362 us; the launch traced here: 357 us
  local copies, waits for them, and re-layouts  98 us (27%)
  waiting for transfers between devices  75.3 us (21%)
  matrix products  63.7 us (18%)
  starting transfers between devices  45.8 us (13%)
  blocking collectives  37.3 us (10%)
  other arithmetic  34.8 us (10%)
    all_to_all x1, waiting for transfers between devices, on_device(): lax.all_to_all(sending.reshape(hist_count, item_count, slots, width_d).as...  31.9 us
    ppermute x8, waiting for transfers between devices, passed_along(): return lax.ppermute(shard, axis, pairs)  24.2 us
    ppermute x8, starting transfers between devices, passed_along(): return lax.ppermute(shard, axis, pairs)  19.5 us
    all_to_all x1, waiting for transfers between devices, on_device(): lax.all_to_all(lax.all_to_all(served, 'hist', split_axis=0, concat_axis=0...  19.1 us
    all_to_all x1, blocking collectives, on_device(): lax.all_to_all(asking.reshape(hist_count, item_count, slots), 'hist', spl...  19 us
    all_to_all x1, blocking collectives, on_device(): lax.all_to_all(lax.all_to_all(asking.reshape(hist_count, item_count, slot...  18.3 us
    scatter x1, local copies, waits for them, and re-layouts, on_device(): slot_grads = jnp.zeros((owner_count, capacity, width_d), jnp.float32).at[...  15.7 us
    gather x3, local copies, waits for them, and re-layouts, on_device(): served = item_table[asked]  13.8 us
  transfers between devices with their start and end apart: 12, of which 6 were waited for; matrix products, arithmetic and copies ran while one was open for 29% of the time, Pallas kernels for 0%

commit v1 on v0

v1 whole, which is shorter than its diff:
```python
import math

import jax
import jax.numpy as jnp
from jax import lax
from jax.experimental import pallas as pl
from jax.experimental.pallas import tpu as pltpu
from jax.sharding import PartitionSpec as P

HEADS = 8
TAU = 0.05
CAP = 2
CHUNKS = 4
LANES = 128
SLOTS = CAP + 1
PIECES = 2
NBANK = SLOTS * CHUNKS
F32 = jnp.float32
BF16 = jnp.bfloat16
VMEM = pl.BlockSpec(memory_space=pltpu.VMEM)
HBM = pl.BlockSpec(memory_space=pltpu.HBM)
SMEM = pl.BlockSpec(memory_space=pltpu.SMEM)


def call(kernel, outs, in_specs, args, flops, scratch=(), mib=60, out_specs=None):
    moved = sum(a.size * a.dtype.itemsize for a in args) + sum(
        math.prod(o.shape) * o.dtype.itemsize for o in outs
    )
    pinned = [i for i, spec in enumerate(in_specs) if spec is None]
    scratch = list(scratch)

    def body(*refs):
        refs = list(refs)
        count = len(pinned)
        if not count:
            return kernel(*refs)
        held, sems = refs[-count - 1 : -1], refs[-1]
        refs = refs[: -count - 1]
        copies = []
        for j, i in enumerate(pinned):
            copies.append(pltpu.make_async_copy(refs[i], held[j], sems.at[j]))
            copies[-1].start()
            refs[i] = held[j]

        def loaded():
            for copy in copies:
                copy.wait()

        return kernel(loaded, *refs)

    if pinned:
        scratch += [pltpu.VMEM(args[i].shape, args[i].dtype) for i in pinned]
        scratch.append(pltpu.SemaphoreType.DMA((len(pinned),)))
    return pl.pallas_call(
        body,
        out_shape=tuple(outs),
        in_specs=[HBM if spec is None else spec for spec in in_specs],
        out_specs=out_specs or tuple(VMEM for _ in outs),
        scratch_shapes=scratch,
        compiler_params=pltpu.CompilerParams(vmem_limit_bytes=mib * 2**20),
        cost_estimate=pl.CostEstimate(flops=flops, bytes_accessed=moved, transcendentals=0),
    )(
        *[
            pltpu.with_memory_space_constraint(a, pltpu.HBM) if spec is None else a
            for a, spec in zip(args, in_specs)
        ]
    )


def shaped(shape, dtype):
    return jax.ShapeDtypeStruct(shape, dtype)


def dot(a, b, contract=(1, 0)):
    return lax.dot_general(
        a, b, (((contract[0],), (contract[1],)), ((), ())), preferred_element_type=F32
    )


def layer_stats(values):
    center = values - jnp.mean(values, axis=-1, keepdims=True)
    scale_inv = lax.rsqrt(jnp.mean(center * center, axis=-1, keepdims=True) + 1e-05)
    return center * scale_inv, scale_inv


def norm_back(upstream, normed, scale_inv):
    return scale_inv * (
        upstream
        - jnp.mean(upstream, axis=-1, keepdims=True)
        - normed * jnp.mean(upstream * normed, axis=-1, keepdims=True)
    )


def item_norm(rows_in):
    values = rows_in.astype(F32)
    lengths = jnp.sqrt(jnp.sum(values * values, axis=-1, keepdims=True) + 1e-06)
    return values / lengths, lengths


def sigmoid(value):
    return 1.0 / (1.0 + jnp.exp(-value))


def ask_kernel(owner_ref, row_ref, neg_ref, ask_ref, slot_row_ref, slot_col_ref):
    n = owner_ref.shape[1]
    owners = ask_ref.shape[0]
    lead = lax.broadcasted_iota(jnp.int32, (n, n), 0)
    lane = lax.broadcasted_iota(jnp.int32, (n, n), 1)

    def column(row):
        spread = jnp.broadcast_to(row.astype(F32), (n, n))
        return jnp.sum(jnp.where(lead == lane, spread, 0.0), axis=1, keepdims=True)

    owner_r = jnp.broadcast_to(owner_ref[...].astype(F32), (n, n))
    owner_c = column(owner_ref[...])
    same = owner_r == owner_c
    rank_r = jnp.sum(jnp.where(same & (lead < lane), 1.0, 0.0), axis=0, keepdims=True)
    rank_c = jnp.sum(jnp.where(same & (lane < lead), 1.0, 0.0), axis=1, keepdims=True)
    slot_r = owner_ref[...] * CAP + rank_r.astype(jnp.int32)
    slot_row_ref[...] = slot_r
    slot_col_ref[...] = (owner_c * CAP + rank_c).astype(jnp.int32)
    rows = jnp.broadcast_to(column(row_ref[...]), (n, LANES))
    by_owner = lax.broadcasted_iota(jnp.int32, (owners, n), 0) * CAP
    asked = None
    for k in range(CAP):
        hot = jnp.where(slot_r == by_owner + k, 1.0, 0.0).astype(BF16)
        part = dot(hot, jnp.where(lane == k, rows, 0.0).astype(BF16))
        asked = part if asked is None else asked + part
    for c in range(owners // n):
        negative = column(neg_ref[:, c * n : (c + 1) * n])
        ask_ref[c * n : (c + 1) * n, :] = jnp.where(
            lane == CAP, negative, asked[c * n : (c + 1) * n]
        ).astype(jnp.int32)


def spread_slot(wide, base, k, rows):
    for c in range(CHUNKS):
        wide[pl.ds(base + k * CHUNKS + c, rows.shape[0], stride=NBANK), :] = rows[
            :, c * LANES : (c + 1) * LANES
        ]


def slot_rows(wide, base, k, count):
    return jnp.concatenate(
        [wide[pl.ds(base + k * CHUNKS + c, count, stride=NBANK), :] for c in range(CHUNKS)], axis=1
    ).astype(BF16)


def piece(ref, i):
    size = ref.shape[0] // PIECES
    return ref.at[pl.ds(i * size, size), :]


def serve_kernel(asks_ref, table_ref, out_ref, wide, narrow, sems):
    owners = asks_ref.shape[0] // PIECES
    rows = table_ref.shape[0]
    table = table_ref[...]
    row_id = lax.broadcasted_iota(jnp.int32, (owners, rows), 1)
    copies = []
    for i in range(PIECES):
        base = i * owners * NBANK
        for k in range(SLOTS):
            asked = asks_ref[i * owners : (i + 1) * owners, k : k + 1]
            hot = jnp.where(asked == row_id, 1.0, 0.0).astype(BF16)
            spread_slot(wide, base, k, dot(hot, table))
        narrow[base : base + owners * NBANK, :] = wide[base : base + owners * NBANK, :].astype(BF16)
        copies.append(pltpu.make_async_copy(piece(narrow, i), piece(out_ref, i), sems.at[i]))
        copies[-1].start()
    for copy in copies:
        copy.wait()


def pair_masks(n):
    lane = lax.broadcasted_iota(jnp.int32, (n, LANES), 1)
    return lane < (LANES // 2)


def both_heads(part, low):
    zero = jnp.zeros_like(part)
    return jnp.concatenate([jnp.where(low, part, zero), jnp.where(low, zero, part)], axis=0)


def same_before(place_ref, sess_ref, ahead):
    block = place_ref[0] + ahead
    inside = block < sess_ref.shape[1]
    block = jnp.minimum(block, sess_ref.shape[1] - 1)
    here = sess_ref[0, block]
    near = inside & (block >= 1) & (sess_ref[0, jnp.maximum(block - 1, 0)] == here)
    far = inside & (block >= 2) & (sess_ref[0, jnp.maximum(block - 2, 0)] == here)
    return jnp.where(near, 1, 0), jnp.where(far, 1, 0)


def window_scale(place_ref, sess_ref, n):
    near, far = same_before(place_ref, sess_ref, 0)
    place = lax.broadcasted_iota(jnp.int32, (n, 3 * n), 0)
    lane = lax.broadcasted_iota(jnp.int32, (n, 3 * n), 1)
    count = place + 1 + n * (near + far)
    allowed = jnp.where(
        lane < n, far, jnp.where(lane < 2 * n, near, jnp.where(lane - 2 * n <= place, 1, 0))
    )
    scale = allowed.astype(F32) * (1.0 / count.astype(F32))
    return jnp.concatenate([scale, scale], axis=0)


def forward_kernel(
    place_ref,
    sess_ref,
    far_ref,
    near_ref,
    own_ref,
    gain_ref,
    w_in_ref,
    w_out_ref,
    unit_ref,
    length_ref,
    hat_ref,
    scale_ref,
    gate_ref,
    query_ref,
    slope_gq_ref,
    slope_vk_ref,
    keys_ref,
    values_ref,
):
    n, width = own_ref.shape
    gain = gain_ref[...]
    hist_f = own_ref[...].astype(F32)

    def normed_in(values):
        return (layer_stats(values)[0] * gain).astype(BF16)

    projected = dot(normed_in(hist_f), w_in_ref[...])
    sigma = sigmoid(projected)
    slope = sigma * (1.0 + projected * (1.0 - sigma))
    slope_gq_ref[:, :width] = slope[:, :width]
    slope_vk_ref[:, :width] = slope[:, width : 2 * width]
    slope_gq_ref[:, width:] = slope[:, 2 * width : 3 * width]
    slope_vk_ref[:, width:] = slope[:, 3 * width :]
    act = (projected * sigma).astype(BF16)
    gate_ref[...] = act[:, :width]
    query_ref[...] = act[:, 2 * width : 3 * width]
    before = jnp.concatenate(
        [normed_in(far_ref[...].astype(F32)), normed_in(near_ref[...].astype(F32))], axis=0
    )
    values_before = dot(before, w_in_ref[:, width : 2 * width])
    keys_before = dot(before, w_in_ref[:, 3 * width :])
    values_ref[: 2 * n, :] = (values_before * sigmoid(values_before)).astype(BF16)
    keys_ref[: 2 * n, :] = (keys_before * sigmoid(keys_before)).astype(BF16)
    values_ref[2 * n :, :] = act[:, width : 2 * width]
    keys_ref[2 * n :, :] = act[:, 3 * width :]
    scale = window_scale(place_ref, sess_ref, n)
    low = pair_masks(n)
    score_scale = 1.0 / math.sqrt(width // HEADS)
    attended = []
    for pair in range(HEADS // 2):
        lanes = slice(pair * LANES, (pair + 1) * LANES)
        queries = both_heads(act[:, 2 * width + pair * LANES : 2 * width + (pair + 1) * LANES], low)
        scores = dot(queries, keys_ref[:, lanes], (1, 1)) * score_scale
        weights = (scores * sigmoid(scores) * scale).astype(BF16)
        both = dot(weights, values_ref[:, lanes])
        attended.append(jnp.where(low, both[:n], both[n:]))
    attn_hat, scale_a = layer_stats(jnp.concatenate(attended, axis=1))
    hat_ref[...] = attn_hat
    scale_ref[...] = jnp.broadcast_to(scale_a, scale_ref.shape)
    gated = (attn_hat * act[:, :width].astype(F32)).astype(BF16)
    user_out = dot(gated, w_out_ref[...]) + hist_f
    user_len = jnp.sqrt(jnp.sum(user_out * user_out, axis=-1, keepdims=True) + 1e-06)
    unit_ref[...] = user_out / user_len
    length_ref[...] = jnp.broadcast_to(user_len, length_ref.shape)


def softmax_kernel(
    loaded,
    fetched_ref,
    neg_row_ref,
    slot_row_ref,
    slot_col_ref,
    unit_ref,
    length_ref,
    send_ref,
    user_grad_ref,
    narrow,
    wide,
    sems,
):
    n = unit_ref.shape[0]
    owners = neg_row_ref.shape[1] // PIECES
    wide[...] = fetched_ref[...].astype(F32)
    neg_units, neg_lens, neg_bfs = [], [], []
    for i in range(PIECES):
        unit, length = item_norm(slot_rows(wide, i * owners * NBANK, CAP, owners))
        neg_units.append(unit)
        neg_lens.append(length)
        neg_bfs.append(unit.astype(BF16))
    neg_bf = jnp.concatenate(neg_bfs, axis=0)
    loaded()
    user_unit = unit_ref[...]
    user_bf = user_unit.astype(BF16)
    user_f = user_bf.astype(F32)
    neg_row = neg_row_ref[...] + 1
    exponent = jnp.zeros(neg_row.shape, F32)
    for level in range(1, 8):
        exponent = exponent + jnp.where(neg_row >= (1 << level), 1.0, 0.0)
    shift = math.log(8) + exponent * math.log(2.0)
    neg_exp = jnp.exp(dot(user_bf, neg_bf, (1, 1)) / TAU + shift)
    slot_col = slot_col_ref[...]
    lane = lax.broadcasted_iota(jnp.int32, (n, owners), 1) * CAP
    hots, rows = [], []
    for i in range(PIECES):
        for k in range(CAP):
            hots.append(jnp.where(slot_col == lane + (i * owners * CAP + k), 1.0, 0.0).astype(BF16))
            rows.append(slot_rows(wide, i * owners * NBANK, k, owners))
    pos_rows = dot(jnp.concatenate(hots, axis=1), jnp.concatenate(rows, axis=0))
    pos_unit, pos_len = item_norm(pos_rows)
    pos_bf = pos_unit.astype(BF16).astype(F32)
    pos_exp = jnp.exp(jnp.sum(user_f * pos_bf, axis=-1, keepdims=True) / TAU)
    denominator = pos_exp + jnp.sum(neg_exp, axis=-1, keepdims=True)
    pos_delta = pos_exp / denominator - 1.0
    neg_prob = (neg_exp / denominator).astype(BF16)
    raw_pos = pos_delta * user_f / TAU
    pos_grad = (raw_pos - pos_unit * jnp.sum(pos_unit * raw_pos, axis=-1, keepdims=True)) / pos_len
    pos_grad = pos_grad.astype(BF16)
    slot_row = slot_row_ref[...]
    lead = lax.broadcasted_iota(jnp.int32, (owners, n), 0) * CAP
    copies = []
    for i in range(PIECES):
        base = i * owners * NBANK
        for k in range(CAP):
            hot = jnp.where(slot_row == lead + (i * owners * CAP + k), 1.0, 0.0).astype(BF16)
            spread_slot(wide, base, k, dot(hot, pos_grad))
        raw_neg = dot(neg_prob[:, i * owners : (i + 1) * owners], user_bf, (0, 0)) / TAU
        along = jnp.sum(neg_units[i] * raw_neg, axis=-1, keepdims=True)
        spread_slot(wide, base, CAP, (raw_neg - neg_units[i] * along) / neg_lens[i])
        narrow[base : base + owners * NBANK, :] = wide[base : base + owners * NBANK, :].astype(BF16)
        copies.append(pltpu.make_async_copy(piece(narrow, i), piece(send_ref, i), sems.at[i]))
        copies[-1].start()
    unit_grad = (pos_delta * pos_bf + dot(neg_prob, neg_bf)) / TAU
    user_grad_ref[...] = (
        unit_grad - user_unit * jnp.sum(user_unit * unit_grad, axis=-1, keepdims=True)
    ) / length_ref[:, 0:1]
    for copy in copies:
        copy.wait()


def heads_back_kernel(
    place_ref,
    sess_ref,
    user_grad_ref,
    w_out_ref,
    gate_ref,
    query_ref,
    hat_ref,
    scale_ref,
    keys_ref,
    values_ref,
    slope_ref,
    w_in_ref,
    own_ref,
    near_ref,
    far_ref,
    in_part_ref,
):
    n, width = hat_ref.shape
    attn_hat = hat_ref[...]
    gated_grad = dot(user_grad_ref[...].astype(BF16), w_out_ref[...], (1, 1))
    hat_grad = gated_grad * gate_ref[...].astype(F32)
    upstream = norm_back(hat_grad, attn_hat, scale_ref[:, 0:1]).astype(BF16)
    scale = window_scale(place_ref, sess_ref, n)
    low = pair_masks(n)
    score_scale = 1.0 / math.sqrt(width // HEADS)
    query_grads = []
    for pair in range(HEADS // 2):
        first = pair * LANES
        lanes = slice(first, first + LANES)
        later = slice(width + first, width + first + LANES)
        queries = both_heads(query_ref[:, lanes], low)
        grads = both_heads(upstream[:, lanes], low)
        keys = keys_ref[:, lanes]
        scores = dot(queries, keys, (1, 1)) * score_scale
        weight_grad = dot(grads, values_ref[:, lanes], (1, 1))
        sigma = sigmoid(scores)
        weights = (scores * sigma * scale).astype(BF16)
        slope = sigma * (1.0 + scores * (1.0 - sigma))
        score_grad = (weight_grad * slope * (scale * score_scale)).astype(BF16)
        both = dot(score_grad, keys)
        query_grads.append(jnp.where(low, both[:n], both[n:]))
        key_grad = dot(score_grad, queries, (0, 0))
        value_grad = dot(weights, grads, (0, 0))
        far_ref[:, lanes] = value_grad[:n].astype(BF16)
        near_ref[:, lanes] = value_grad[n : 2 * n].astype(BF16)
        own_ref[:, lanes] = value_grad[2 * n :]
        far_ref[:, later] = key_grad[:n].astype(BF16)
        near_ref[:, later] = key_grad[n : 2 * n].astype(BF16)
        own_ref[:, later] = key_grad[2 * n :]
    gate_part = (gated_grad * attn_hat * slope_ref[:, :width]).astype(BF16)
    query_part = (jnp.concatenate(query_grads, axis=1) * slope_ref[:, width:]).astype(BF16)
    in_part_ref[...] = dot(gate_part, w_in_ref[:, :width], (1, 1)) + dot(
        query_part, w_in_ref[:, 2 * width : 3 * width], (1, 1)
    )


def last_kernel(
    loaded,
    returned_ref,
    near_ref,
    far_ref,
    asks_ref,
    own_grad_ref,
    slope_ref,
    in_part_ref,
    w_in_ref,
    gain_ref,
    hist_ref,
    user_grad_ref,
    table_grad_ref,
    history_grad_ref,
    wide,
):
    width = hist_ref.shape[1]
    owners = asks_ref.shape[0] // PIECES
    rows = table_grad_ref.shape[0]
    wide[...] = returned_ref[...].astype(F32)
    loaded()
    asks = jnp.transpose(asks_ref[...].astype(F32))
    row_id = lax.broadcasted_iota(jnp.int32, (rows, owners), 0).astype(F32)
    total = None
    for i in range(PIECES):
        hots, parts = [], []
        for k in range(SLOTS):
            asked = asks[k : k + 1, i * owners : (i + 1) * owners]
            hots.append(jnp.where(asked == row_id, 1.0, 0.0).astype(BF16))
            parts.append(slot_rows(wide, i * owners * NBANK, k, owners))
        part = dot(jnp.concatenate(hots, axis=1), jnp.concatenate(parts, axis=0))
        total = part if total is None else total + part
    table_grad_ref[...] = total.astype(BF16)
    come = near_ref[...].astype(F32) + far_ref[...].astype(F32)
    proj_grad = ((own_grad_ref[...] + come) * slope_ref[...]).astype(BF16)
    in_grad = (
        in_part_ref[...]
        + dot(proj_grad[:, :width], w_in_ref[:, width : 2 * width], (1, 1))
        + dot(proj_grad[:, width:], w_in_ref[:, 3 * width :], (1, 1))
    )
    normed_x, scale_x = layer_stats(hist_ref[...].astype(F32))
    back = norm_back(in_grad * gain_ref[...], normed_x, scale_x)
    history_grad_ref[...] = (back + user_grad_ref[...]).astype(BF16)


def passed_along(shard, axis, by):
    count = lax.axis_size(axis)
    pairs = [(i, i + by) for i in range(count) if 0 <= i + by < count]
    return lax.ppermute(shard, axis, pairs)


def on_device(history, ln_gain, w_in, w_out, item_table, sessions, pos_owner, pos_row, neg_rows):
    n, width = history.shape[1:]
    items = lax.axis_size("items")
    hists = lax.axis_size("hist")
    owners = hists * items
    rows = item_table.shape[0]
    axes = ("hist", "items")
    place = jnp.stack([lax.axis_index("hist"), lax.axis_index("items")]).astype(jnp.int32)
    own = history[0]
    gain = ln_gain.reshape(1, width)
    neg_row = neg_rows.reshape(1, owners)

    def exchange(shard, chunk):
        shape = shard.shape
        split = shard.reshape((owners,) + chunk)
        return lax.all_to_all(split, axes, split_axis=0, concat_axis=0, tiled=True).reshape(shape)

    ask, slot_row, slot_col = call(
        ask_kernel,
        [shaped((owners, LANES), jnp.int32), shaped((1, n), jnp.int32), shaped((n, 1), jnp.int32)],
        [VMEM, VMEM, VMEM],
        (pos_owner.reshape(1, n), pos_row, neg_row),
        2 * CAP * owners * n * LANES,
    )
    asks = exchange(ask, (1, LANES))
    near = passed_along(own, "hist", 1)
    far = passed_along(own, "hist", 2)

    big = owners * NBANK
    staging = [
        pltpu.VMEM((big, LANES), BF16),
        pltpu.VMEM((big, LANES), F32),
        pltpu.SemaphoreType.DMA((PIECES,)),
    ]
    outward = [staging[1], staging[0], staging[2]]
    (served,) = call(
        serve_kernel,
        [shaped((big, LANES), BF16)],
        [VMEM, VMEM],
        (asks, item_table),
        2 * SLOTS * owners * rows * width,
        outward,
        out_specs=(HBM,),
    )
    fetched = exchange(served, (SLOTS, CHUNKS, LANES))

    unit, length, attn_hat, scale_a, gate, query, slope_gq, slope_vk, keys, values = call(
        forward_kernel,
        [
            shaped((n, width), F32),
            shaped((n, LANES), F32),
            shaped((n, width), F32),
            shaped((n, LANES), F32),
            shaped((n, width), BF16),
            shaped((n, width), BF16),
            shaped((n, 2 * width), F32),
            shaped((n, 2 * width), F32),
            shaped((3 * n, width), BF16),
            shaped((3 * n, width), BF16),
        ],
        [SMEM, SMEM] + [VMEM] * 6,
        (place, sessions, far, near, own, gain, w_in, w_out),
        2 * n * width * width * 12,
    )

    send, user_grad = call(
        softmax_kernel,
        [shaped((big, LANES), BF16), shaped((n, width), F32)],
        [VMEM] + [None] * 5,
        (fetched, neg_row, slot_row, slot_col, unit, length),
        2 * n * width * owners * 7,
        staging,
        mib=40,
        out_specs=(HBM, VMEM),
    )
    returned = exchange(send, (SLOTS, CHUNKS, LANES))

    own_grad, near_grad, far_grad, in_part = call(
        heads_back_kernel,
        [
            shaped((n, 2 * width), F32),
            shaped((n, 2 * width), BF16),
            shaped((n, 2 * width), BF16),
            shaped((n, width), F32),
        ],
        [SMEM, SMEM] + [VMEM] * 10,
        (
            place,
            sessions,
            user_grad,
            w_out,
            gate,
            query,
            attn_hat,
            scale_a,
            keys,
            values,
            slope_gq,
            w_in,
        ),
        2 * n * width * width * 12,
    )
    near_back = passed_along(near_grad, "hist", -1)
    far_back = passed_along(far_grad, "hist", -2)
    table_grad, history_grad = call(
        last_kernel,
        [shaped((rows, width), BF16), shaped((n, width), BF16)],
        [VMEM] * 3 + [None] * 8,
        (
            returned,
            near_back,
            far_back,
            asks,
            own_grad,
            slope_vk,
            in_part,
            w_in,
            gain,
            own,
            user_grad,
        ),
        2 * SLOTS * owners * rows * width,
        [staging[1]],
        mib=40,
    )
    return history_grad[None], table_grad


def solution(mesh):
    return jax.shard_map(
        on_device,
        mesh=mesh,
        in_specs=(
            P("items", "hist", None),
            P(),
            P(),
            P(),
            P(("hist", "items"), None),
            P("items", None),
            P("items", "hist", None),
            P("items", "hist"),
            P("items", None, None),
        ),
        out_specs=(P("items", "hist", None), P(("hist", "items"), None)),
        check_vma=False,
    )
```

time: 362 us -> 167 us (0.46); the launches traced: 357 us -> 167 us
  local copies, waits for them, and re-layouts: 98 us -> 1.36 us
  matrix products: 63.7 us -> 0 us
  other arithmetic: 34.8 us -> 0.61 us
  Pallas kernels: 0 us -> 23.5 us
  waiting for transfers between devices: 75.3 us -> 59.5 us
  starting transfers between devices: 45.8 us -> 41.4 us
    dot_general x55 -> x0, matrix products: 63.7 us -> none  [the longest x8 12.9 us: head_one_head(): jnp.dot(weights.T, grad_h, preferred_element_type=jnp.float32)]
    all_to_all x4 -> x2, waiting for transfers between devices: 51.1 us -> 4.56 us  [exchange(): lax.all_to_all(split, axes, split_axis=0, concat_axis=0, tiled=True)]
    ppermute x8 -> x4, waiting for transfers between devices: 24.2 us -> 54.9 us  [passed_along(): return lax.ppermute(shard, axis, pairs)]
    scatter x2 -> x0, local copies, waits for them, and re-layouts: 26.6 us -> none  [the longest x1 15.7 us: on_device(): slot_grads = jnp.zeros((owner_count, capacity, width_d), jnp.float32).at[...]
    pallas_call x0 -> x6, Pallas kernels: none -> 23.5 us  [call(): pl.pallas_call(body, out_shape=tuple(outs), in_specs=[HBM if spec is None...]
    gather x4 -> x0, local copies, waits for them, and re-layouts: 15.9 us -> none  [the longest x3 13.8 us: on_device(): served = item_table[asked]]
    reshape x4 -> x0, local copies, waits for them, and re-layouts: 13.3 us -> none  [the longest x2 10.7 us: on_device(): returned.reshape(-1, width_d)]
    scatter-add x1 -> x0, other arithmetic: 10.4 us -> none  [on_device(): jax.ops.segment_sum(returned.reshape(-1, width_d), asked.reshape(-1), num...]
  transfers between devices with their start and end apart: 12 -> 6, of which waited for: 6 -> 6; matrix products, arithmetic and copies ran while one was open for 29% -> 0% of each run, Pallas kernels for 0% -> 7%
where the time goes in v1:
time: 167 us
  waiting for transfers between devices  59.5 us (36%)
  starting transfers between devices  41.4 us (25%)
  blocking collectives  39.4 us (24%)
  Pallas kernels  23.5 us (14%)
    ppermute x4, waiting for transfers between devices, passed_along(): return lax.ppermute(shard, axis, pairs)  54.9 us
    all_to_all x1, blocking collectives, exchange(): lax.all_to_all(split, axes, split_axis=0, concat_axis=0, tiled=True)  39.4 us
    all_to_all x2, starting transfers between devices, exchange(): lax.all_to_all(split, axes, split_axis=0, concat_axis=0, tiled=True)  26.2 us
    pallas_call x6, Pallas kernels, call(): pl.pallas_call(body, out_shape=tuple(outs), in_specs=[HBM if spec is None...  23.5 us
    ppermute x4, starting transfers between devices, passed_along(): return lax.ppermute(shard, axis, pairs)  15.2 us
    all_to_all x2, waiting for transfers between devices, exchange(): lax.all_to_all(split, axes, split_axis=0, concat_axis=0, tiled=True)  4.56 us
  transfers between devices with their start and end apart: 6, of which 6 were waited for; matrix products, arithmetic and copies ran while one was open for 0% of the time, Pallas kernels for 7%

profile of v1, /device:TPU:1, one launch (start us, length us, event | category | flops | bytes accessed | tf_op | source)
XLA Modules:
  0.0 166.7 jit_solution(16887177720746376975)
XLA Ops:
  0.6 1.7 %shard_map.104 = (s32[512,128]{1,0:T(8,128)}, s32[1,128]{1,0:T(1,128)}, s32[128,1]{1,0:T(8,128)}) custom-call(s32[1,128]{1,0:T(1,128)} %bitcast.30, s32[1,128]{1,0:T(1,128)} %refs_1_.4, s32[1,512]{1,0:T(1,128)} %bitcast.27), custom_call_target="tpu_custom_call" | custom-call | flops 33554432 | bytes 266240 | tf_op jit(solution)/shard_map/pallas_call | solution.py:54
  2.4 39.4 %all_to_all.15 = s32[512,1,128]{2,1,0:T(1,128)} all-to-all(s32[512,1,128]{2,1,0:T(1,128)} %bitcast.24), channel_id=1, replica_groups=mesh['hist'=16,'items'=32] {'hist','items'}, dimensions={0} | all-to-all | bytes 524288 | tf_op jit(solution)/shard_map/all_to_all | solution.py:469
  41.8 2.7 %shard_map.105 = bf16[6144,128]{1,0:T(8,128)(2,1)} custom-call(s32[512,128]{1,0:T(8,128)} %bitcast.18, bf16[256,512]{1,0:T(8,128)(2,1)} %refs_1_.5), custom_call_target="tpu_custom_call" | custom-call | flops 402653184 | bytes 2097152 | tf_op jit(solution)/shard_map/pallas_call | solution.py:54
  44.5 0.0 copy-start.1
  44.5 9.5 %all-to-all-start.1 = ((bf16[512,3,4,128]{3,2,1,0:T(4,128)(2,1)}), bf16[512,3,4,128]{3,2,1,0:T(4,128)(2,1)S(1)}, u32[]{:S(2)}, u32[]{:S(2)}) async-start(bf16[512,3,4,128]{3,2,1,0:T(4,128)(2,1)} %bitcast.17), calls=%async_computation.1 | async-start | bytes 3145728 | tf_op jit(solution)/shard_map/all_to_all | solution.py:469
  54.0 0.0 copy-done.1
  54.0 4.1 %collective-permute-start.1 = (bf16[128,512]{1,0:T(8,128)(2,1)S(1)}, bf16[128,512]{1,0:T(8,128)(2,1)S(1)}, u32[]{:S(2)}, u32[]{:S(2)}) collective-permute-start(bf16[128,512]{1,0:T(8,128)(2,1)S(1)} %bitcast.22), channel_id=1, source_target_pairs={{0,32},{32,64},{64,96},{96,128},{128,160},{160,192},{192,224},{224... | collective-permute-start | bytes 393224 | tf_op jit(solution)/shard_map/ppermute | solution.py:451
  58.1 3.6 %collective-permute-start = (bf16[128,512]{1,0:T(8,128)(2,1)S(1)}, bf16[128,512]{1,0:T(8,128)(2,1)S(1)}, u32[]{:S(2)}, u32[]{:S(2)}) collective-permute-start(bf16[128,512]{1,0:T(8,128)(2,1)S(1)} %bitcast.23), channel_id=1, source_target_pairs={{0,64},{32,96},{64,128},{96,160},{128,192},{160,224},{192,256},{22... | collective-permute-start | bytes 393224 | tf_op jit(solution)/shard_map/ppermute | solution.py:451
  61.7 0.6 pad_add_fusion.refs_0_
  62.3 24.5 %collective-permute-done.1.refs_3_ = bf16[128,512]{1,0:T(8,128)(2,1)S(1)} collective-permute-done((bf16[128,512]{1,0:T(8,128)(2,1)S(1)}, bf16[128,512]{1,0:T(8,128)(2,1)S(1)}, u32[]{:S(2)}, u32[]{:S(2)}) %collective-permute-start.1) | collective-permute-done | bytes 131104 | tf_op jit(solution)/shard_map/ppermute | solution.py:451
  86.9 0.0 copy-start.2
  86.9 4.0 %collective-permute-done.refs_2_ = bf16[128,512]{1,0:T(8,128)(2,1)S(1)} collective-permute-done((bf16[128,512]{1,0:T(8,128)(2,1)S(1)}, bf16[128,512]{1,0:T(8,128)(2,1)S(1)}, u32[]{:S(2)}, u32[]{:S(2)}) %collective-permute-start) | collective-permute-done | bytes 131104 | tf_op jit(solution)/shard_map/ppermute | solution.py:451
  90.9 0.0 copy-start.3
  90.9 0.0 copy-done.2
  90.9 0.7 copy-done.3
  91.5 5.5 %shard_map.106 = (f32[128,512]{1,0:T(8,128)}, f32[128,128]{1,0:T(8,128)}, f32[128,512]{1,0:T(8,128)}, f32[128,128]{1,0:T(8,128)}, bf16[128,512]{1,0:T(8,128)(2,1...) custom-call(s32[2]{0:T(128)} %pad_add_fusion.refs_0_, ...), custom_call_target="tpu_custom_call" | custom-call | flops 805306368 | bytes 5769288 | tf_op jit(solution)/shard_map/pallas_call | solution.py:54
  97.0 0.7 all-to-all-done.1
  97.7 3.9 %shard_map.107 = (bf16[6144,128]{1,0:T(8,128)(2,1)}, f32[128,512]{1,0:T(8,128)S(1)}) custom-call(bf16[6144,128]{1,0:T(8,128)(2,1)S(1)} %bitcast.15, s32[1,512]{1,0:T(1,128)} %bitcast.28, s32[1,128]{1,0:T(1,128)} %get-tuple-element.24.refs_2_, s32[128,1]{1,0:T(8,128)} %get-tuple-element.25.refs_3_, f32[128,512]{1,0:T(8,128)} %get-tuple-element.26.refs_4_, ...), custom_call_target="tpu_custom_call" | custom-call | flops 469762048 | bytes 3738624 | tf_op jit(solution)/shard_map/pallas_call | solution.py:54
  101.6 0.0 copy-start
  101.7 0.7 copy-done
  102.4 16.7 %all-to-all-start.2 = ((bf16[512,3,4,128]{3,2,1,0:T(4,128)(2,1)}), bf16[512,3,4,128]{3,2,1,0:T(4,128)(2,1)S(1)}, u32[]{:S(2)}, u32[]{:S(2)}) async-start(bf16[512,3,4,128]{3,2,1,0:T(4,128)(2,1)} %bitcast.11), calls=%async_computation.2 | async-start | bytes 3145728 | tf_op jit(solution)/shard_map/all_to_all | solution.py:469
  119.1 5.8 %shard_map.108 = (f32[128,1024]{1,0:T(8,128)}, bf16[128,1024]{1,0:T(8,128)(2,1)}, bf16[128,1024]{1,0:T(8,128)(2,1)}, f32[128,512]{1,0:T(8,128)}) custom-call(s32[2]{0:T(128)} %pad_add_fusion.refs_0_, s32[1,16]{1,0:T(1,128)} %refs_1_.7, f32[128,512]{1,0:T(8,128)} %copy-done, bf16[512,512]{1,0:T(8,128)(2,1)} %refs_3_.1, ...), custom_call_target="tpu_custom_call" | custom-call | flops 805306368 | bytes 6094920 | tf_op jit(solution)/shard_map/pallas_call | solution.py:54
  124.9 6.2 %collective-permute-start.2 = (bf16[128,1024]{1,0:T(8,128)(2,1)}, bf16[128,1024]{1,0:T(8,128)(2,1)S(1)}, u32[]{:S(2)}, u32[]{:S(2)}) collective-permute-start(bf16[128,1024]{1,0:T(8,128)(2,1)} %get-tuple-element.37), channel_id=1, source_target_pairs={{32,0},{64,32},{96,64},{128,96},{160,128},{192,160},{224,192},{256... | collective-permute-start | bytes 786440 | tf_op jit(solution)/shard_map/ppermute | solution.py:451
  131.1 1.3 collective-permute-start.3
  132.4 25.8 %collective-permute-done.2.refs_1_ = bf16[128,1024]{1,0:T(8,128)(2,1)S(1)} collective-permute-done((bf16[128,1024]{1,0:T(8,128)(2,1)}, bf16[128,1024]{1,0:T(8,128)(2,1)S(1)}, u32[]{:S(2)}, u32[]{:S(2)}) %collective-permute-start.2) | collective-permute-done | bytes 262176 | tf_op jit(solution)/shard_map/ppermute | solution.py:451
  158.2 0.5 collective-permute-done.3.refs_2_
  158.8 3.9 %all-to-all-done.2 = bf16[512,3,4,128]{3,2,1,0:T(4,128)(2,1)S(1)} async-done(((bf16[512,3,4,128]{3,2,1,0:T(4,128)(2,1)}), bf16[512,3,4,128]{3,2,1,0:T(4,128)(2,1)S(1)}, u32[]{:S(2)}, u32[]{:S(2)}) %all-to-all-start.2) | async-done | bytes 1572896 | tf_op jit(solution)/shard_map/all_to_all | solution.py:469
  162.6 3.9 %shard_map.109 = (bf16[256,512]{1,0:T(8,128)(2,1)}, bf16[128,512]{1,0:T(8,128)(2,1)}) custom-call(bf16[6144,128]{1,0:T(8,128)(2,1)S(1)} %bitcast.16, bf16[128,1024]{1,0:T(8,128)(2,1)S(1)} %collective-permute-done.2.refs_1_, bf16[128,1024]{1,0:T(8,128)(2,1)S(1)} %collective-permute-done.3.refs_2_, s32[512,128]{1,0:T(8,128)} %bitcast.19, ...), custom_call_target="tpu_custom_call" | custom-call | flops 402653184 | bytes 6555648 | tf_op jit(solution)/shard_map/pallas_call | solution.py:54
Async XLA Ops:
  44.5 9.5 %copy-start.1 = (bf16[1,128,512]{2,1,0:T(8,128)(2,1)S(1)}, bf16[1,128,512]{2,1,0:T(8,128)(2,1)}, u32[]{:S(2)}) copy-start(bf16[1,128,512]{2,1,0:T(8,128)(2,1)} %param.9) | copy-start | bytes 393220
  44.5 53.2 %all-to-all-start.1 = ((bf16[512,3,4,128]{3,2,1,0:T(4,128)(2,1)}), bf16[512,3,4,128]{3,2,1,0:T(4,128)(2,1)S(1)}, u32[]{:S(2)}, u32[]{:S(2)}) async-start(bf16[512,3,4,128]{3,2,1,0:T(4,128)(2,1)} %bitcast.17), calls=%async_computation.1 | async-start | bytes 3145728 | tf_op jit(solution)/shard_map/all_to_all | solution.py:469
  54.0 32.9 %collective-permute-start.1 = (bf16[128,512]{1,0:T(8,128)(2,1)S(1)}, bf16[128,512]{1,0:T(8,128)(2,1)S(1)}, u32[]{:S(2)}, u32[]{:S(2)}) collective-permute-start(bf16[128,512]{1,0:T(8,128)(2,1)S(1)} %bitcast.22), channel_id=1, source_target_pairs={{0,32},{32,64},{64,96},{96,128},{128,160},{160,192},{192,224},{224... | collective-permute-start | bytes 393224 | tf_op jit(solution)/shard_map/ppermute | solution.py:451
  58.1 32.8 %collective-permute-start = (bf16[128,512]{1,0:T(8,128)(2,1)S(1)}, bf16[128,512]{1,0:T(8,128)(2,1)S(1)}, u32[]{:S(2)}, u32[]{:S(2)}) collective-permute-start(bf16[128,512]{1,0:T(8,128)(2,1)S(1)} %bitcast.23), channel_id=1, source_target_pairs={{0,64},{32,96},{64,128},{96,160},{128,192},{160,224},{192,256},{22... | collective-permute-start | bytes 393224 | tf_op jit(solution)/shard_map/ppermute | solution.py:451
  86.9 4.0 %copy-start.2 = (bf16[128,512]{1,0:T(8,128)(2,1)}, bf16[128,512]{1,0:T(8,128)(2,1)S(1)}, u32[]{:S(2)}) copy-start(bf16[128,512]{1,0:T(8,128)(2,1)S(1)} %collective-permute-done.1.refs_3_) | copy-start | bytes 393220
  90.9 0.7 copy-start.3
  101.6 0.7 copy-start
  102.4 60.3 %all-to-all-start.2 = ((bf16[512,3,4,128]{3,2,1,0:T(4,128)(2,1)}), bf16[512,3,4,128]{3,2,1,0:T(4,128)(2,1)S(1)}, u32[]{:S(2)}, u32[]{:S(2)}) async-start(bf16[512,3,4,128]{3,2,1,0:T(4,128)(2,1)} %bitcast.11), calls=%async_computation.2 | async-start | bytes 3145728 | tf_op jit(solution)/shard_map/all_to_all | solution.py:469
  124.9 33.3 %collective-permute-start.2 = (bf16[128,1024]{1,0:T(8,128)(2,1)}, bf16[128,1024]{1,0:T(8,128)(2,1)S(1)}, u32[]{:S(2)}, u32[]{:S(2)}) collective-permute-start(bf16[128,1024]{1,0:T(8,128)(2,1)} %get-tuple-element.37), channel_id=1, source_target_pairs={{32,0},{64,32},{96,64},{128,96},{160,128},{192,160},{224,192},{256... | collective-permute-start | bytes 786440 | tf_op jit(solution)/shard_map/ppermute | solution.py:451
  131.1 27.7 %collective-permute-start.3 = (bf16[128,1024]{1,0:T(8,128)(2,1)}, bf16[128,1024]{1,0:T(8,128)(2,1)S(1)}, u32[]{:S(2)}, u32[]{:S(2)}) collective-permute-start(bf16[128,1024]{1,0:T(8,128)(2,1)} %get-tuple-element.38), channel_id=1, source_target_pairs={{64,0},{96,32},{128,64},{160,96},{192,128},{224,160},{256,192},{28... | collective-permute-start | bytes 786440 | tf_op jit(solution)/shard_map/ppermute | solution.py:451

commit v2 on v1

--- a/solution.py
+++ b/solution.py
@@ -343,6 +343,7 @@
 
 
 def heads_back_kernel(
+    loaded,
     place_ref,
     sess_ref,
     user_grad_ref,
@@ -361,6 +362,7 @@
     in_part_ref,
 ):
     n, width = hat_ref.shape
+    loaded()
     attn_hat = hat_ref[...]
     gated_grad = dot(user_grad_ref[...].astype(BF16), w_out_ref[...], (1, 1))
     hat_grad = gated_grad * gate_ref[...].astype(F32)
@@ -495,6 +497,7 @@
         outward,
         out_specs=(HBM,),
     )
+    served, near, far = lax.optimization_barrier((served, near, far))
     fetched = exchange(served, (SLOTS, CHUNKS, LANES))
 
     unit, length, attn_hat, scale_a, gate, query, slope_gq, slope_vk, keys, values = call(
@@ -518,7 +521,7 @@
 
     send, user_grad = call(
         softmax_kernel,
-        [shaped((big, LANES), BF16), shaped((n, width), F32)],
+        [shaped((big, LANES), BF16), pltpu.HBM((n, width), F32)],
         [VMEM] + [None] * 5,
         (fetched, neg_row, slot_row, slot_col, unit, length),
         2 * n * width * owners * 7,
@@ -536,7 +539,7 @@
             shaped((n, 2 * width), BF16),
             shaped((n, width), F32),
         ],
-        [SMEM, SMEM] + [VMEM] * 10,
+        [SMEM, SMEM] + [None] * 10,
         (
             place,
             sessions,

time: 167 us -> 161 us (0.964)
  blocking collectives: 39.4 us -> 0 us
  waiting for transfers between devices: 59.5 us -> 75.8 us
  starting transfers between devices: 41.4 us -> 56.9 us
    all_to_all x2 -> x3, waiting for transfers between devices: 4.56 us -> 50 us  [exchange(): lax.all_to_all(split, axes, split_axis=0, concat_axis=0, tiled=True)]
    all_to_all x1 -> x0, blocking collectives: 39.4 us -> none  [exchange(): lax.all_to_all(split, axes, split_axis=0, concat_axis=0, tiled=True)]
    ppermute x4, waiting for transfers between devices: 54.9 us -> 25.8 us  [passed_along(): return lax.ppermute(shard, axis, pairs)]
    all_to_all x2 -> x3, starting transfers between devices: 26.2 us -> 41.6 us  [exchange(): lax.all_to_all(split, axes, split_axis=0, concat_axis=0, tiled=True)]
  transfers between devices with their start and end apart: 6 -> 7, of which waited for: 6 -> 5; matrix products, arithmetic and copies ran while one was open for 0% -> 0% of each run, Pallas kernels for 7% -> 9%
where the time goes in v2:
time: 161 us
  waiting for transfers between devices  75.8 us (47%)
  starting transfers between devices  56.9 us (35%)
  Pallas kernels  25 us (16%)
    all_to_all x3, waiting for transfers between devices, exchange(): lax.all_to_all(split, axes, split_axis=0, concat_axis=0, tiled=True)  50 us
    all_to_all x3, starting transfers between devices, exchange(): lax.all_to_all(split, axes, split_axis=0, concat_axis=0, tiled=True)  41.6 us
    ppermute x4, waiting for transfers between devices, passed_along(): return lax.ppermute(shard, axis, pairs)  25.8 us
    pallas_call x6, Pallas kernels, call(): pl.pallas_call(body, out_shape=tuple(outs), in_specs=[HBM if spec is None...  25 us
    ppermute x4, starting transfers between devices, passed_along(): return lax.ppermute(shard, axis, pairs)  15.3 us
  transfers between devices with their start and end apart: 7, of which 5 were waited for; matrix products, arithmetic and copies ran while one was open for 0% of the time, Pallas kernels for 9%

profile of v2, /device:TPU:1, one launch (start us, length us, event | category | flops | bytes accessed | tf_op | source)
XLA Modules:
  0.0 160.6 jit_solution(11144983491449213792)
XLA Ops:
  0.6 1.7 %shard_map.104 = (s32[512,128]{1,0:T(8,128)}, s32[1,128]{1,0:T(1,128)}, s32[128,1]{1,0:T(8,128)}) custom-call(s32[1,128]{1,0:T(1,128)} %bitcast.30, s32[1,128]{1,0:T(1,128)} %refs_1_.4, s32[1,512]{1,0:T(1,128)} %bitcast.27), custom_call_target="tpu_custom_call" | custom-call | flops 33554432 | bytes 266240 | tf_op jit(solution)/shard_map/pallas_call | solution.py:54
  2.4 22.2 %all-to-all-start = ((s32[512,1,128]{2,1,0:T(1,128)}), s32[512,1,128]{2,1,0:T(1,128)S(1)}, u32[]{:S(2)}, u32[]{:S(2)}) async-start(s32[512,1,128]{2,1,0:T(1,128)} %bitcast.24), calls=%async_computation | async-start | bytes 524288 | tf_op jit(solution)/shard_map/all_to_all | solution.py:471
  24.5 3.7 %collective-permute-start.1 = (bf16[128,512]{1,0:T(8,128)(2,1)}, bf16[128,512]{1,0:T(8,128)(2,1)S(1)}, u32[]{:S(2)}, u32[]{:S(2)}) collective-permute-start(bf16[128,512]{1,0:T(8,128)(2,1)} %bitcast.20), channel_id=1, source_target_pairs={{0,64},{32,96},{64,128},{96,160},{128,192},{160,224},{192,256},{22... | collective-permute-start | bytes 393224 | tf_op jit(solution)/shard_map/ppermute | solution.py:453
  28.2 4.2 %collective-permute-start = (bf16[128,512]{1,0:T(8,128)(2,1)}, bf16[128,512]{1,0:T(8,128)(2,1)S(1)}, u32[]{:S(2)}, u32[]{:S(2)}) collective-permute-start(bf16[128,512]{1,0:T(8,128)(2,1)} %bitcast.21), channel_id=1, source_target_pairs={{0,32},{32,64},{64,96},{96,128},{128,160},{160,192},{192,224},{224... | collective-permute-start | bytes 393224 | tf_op jit(solution)/shard_map/ppermute | solution.py:453
  32.4 8.9 %all-to-all-done = s32[512,1,128]{2,1,0:T(1,128)S(1)} async-done(((s32[512,1,128]{2,1,0:T(1,128)}), s32[512,1,128]{2,1,0:T(1,128)S(1)}, u32[]{:S(2)}, u32[]{:S(2)}) %all-to-all-start) | async-done | bytes 262176 | tf_op jit(solution)/shard_map/all_to_all | solution.py:471
  41.3 0.0 copy-start
  41.3 0.7 copy-done
  42.0 2.7 %shard_map.105 = bf16[6144,128]{1,0:T(8,128)(2,1)} custom-call(s32[512,128]{1,0:T(8,128)} %bitcast.18, bf16[256,512]{1,0:T(8,128)(2,1)} %refs_1_.5), custom_call_target="tpu_custom_call" | custom-call | flops 402653184 | bytes 2097152 | tf_op jit(solution)/shard_map/pallas_call | solution.py:54
  44.7 0.0 collective-permute-done.1.refs_2_
  44.7 0.0 copy-start.1
  44.7 0.0 collective-permute-done.refs_3_
  44.7 0.0 copy-start.2
  44.7 0.6 copy-done.1
  45.4 0.0 copy-done.2
  45.4 9.9 %all-to-all-start.1 = ((bf16[512,3,4,128]{3,2,1,0:T(4,128)(2,1)}), bf16[512,3,4,128]{3,2,1,0:T(4,128)(2,1)S(1)}, u32[]{:S(2)}, u32[]{:S(2)}) async-start(bf16[512,3,4,128]{3,2,1,0:T(4,128)(2,1)} %bitcast.17), calls=%async_computation.1 | async-start | bytes 3145728 | tf_op jit(solution)/shard_map/all_to_all | solution.py:471
  55.3 0.7 pad_add_fusion.refs_0_
  56.0 5.5 %shard_map.106 = (f32[128,512]{1,0:T(8,128)}, f32[128,128]{1,0:T(8,128)}, f32[128,512]{1,0:T(8,128)}, f32[128,128]{1,0:T(8,128)}, bf16[128,512]{1,0:T(8,128)(2,1...) custom-call(s32[2]{0:T(128)} %pad_add_fusion.refs_0_, ...), custom_call_target="tpu_custom_call" | custom-call | flops 805306368 | bytes 5769288 | tf_op jit(solution)/shard_map/pallas_call | solution.py:54
  61.4 37.4 %all-to-all-done.1 = bf16[512,3,4,128]{3,2,1,0:T(4,128)(2,1)S(1)} async-done(((bf16[512,3,4,128]{3,2,1,0:T(4,128)(2,1)}), bf16[512,3,4,128]{3,2,1,0:T(4,128)(2,1)S(1)}, u32[]{:S(2)}, u32[]{:S(2)}) %all-to-all-start.1) | async-done | bytes 1572896 | tf_op jit(solution)/shard_map/all_to_all | solution.py:471
  98.8 4.6 %shard_map.107 = (bf16[6144,128]{1,0:T(8,128)(2,1)}, f32[128,512]{1,0:T(8,128)}) custom-call(bf16[6144,128]{1,0:T(8,128)(2,1)S(1)} %bitcast.15, s32[1,512]{1,0:T(1,128)} %bitcast.28, s32[1,128]{1,0:T(1,128)} %get-tuple-element.28.refs_2_, s32[128,1]{1,0:T(8,128)} %get-tuple-element.29.refs_3_, f32[128,512]{1,0:T(8,128)} %get-tuple-element.32.refs_4_, ...), custom_call_target="tpu_custom_call" | custom-call | flops 469762048 | bytes 3738624 | tf_op jit(solution)/shard_map/pallas_call | solution.py:54
  103.5 9.5 %all-to-all-start.2 = ((bf16[512,3,4,128]{3,2,1,0:T(4,128)(2,1)}), bf16[512,3,4,128]{3,2,1,0:T(4,128)(2,1)S(1)}, u32[]{:S(2)}, u32[]{:S(2)}) async-start(bf16[512,3,4,128]{3,2,1,0:T(4,128)(2,1)} %bitcast.11), calls=%async_computation.2 | async-start | bytes 3145728 | tf_op jit(solution)/shard_map/all_to_all | solution.py:471
  113.0 6.6 %shard_map.108 = (f32[128,1024]{1,0:T(8,128)}, bf16[128,1024]{1,0:T(8,128)(2,1)}, bf16[128,1024]{1,0:T(8,128)(2,1)}, f32[128,512]{1,0:T(8,128)}) custom-call(s32[2]{0:T(128)} %pad_add_fusion.refs_0_, s32[1,16]{1,0:T(1,128)} %refs_1_.7, f32[128,512]{1,0:T(8,128)} %get-tuple-element.35.refs_2_.refs_10_, bf16[512,512]{1,0:T(8,128)(2,1)} %refs_3_.1, ...), custom_call_target="tpu_custom_call" | custom-call | flops 805306368 | bytes 6094920 | tf_op jit(solution)/shard_map/pallas_call | solution.py:54
  119.6 6.2 %collective-permute-start.2 = (bf16[128,1024]{1,0:T(8,128)(2,1)}, bf16[128,1024]{1,0:T(8,128)(2,1)S(1)}, u32[]{:S(2)}, u32[]{:S(2)}) collective-permute-start(bf16[128,1024]{1,0:T(8,128)(2,1)} %get-tuple-element.43), channel_id=1, source_target_pairs={{32,0},{64,32},{96,64},{128,96},{160,128},{192,160},{224,192},{256... | collective-permute-start | bytes 786440 | tf_op jit(solution)/shard_map/ppermute | solution.py:453
  125.8 1.3 collective-permute-start.3
  127.1 24.8 %collective-permute-done.2.refs_1_ = bf16[128,1024]{1,0:T(8,128)(2,1)S(1)} collective-permute-done((bf16[128,1024]{1,0:T(8,128)(2,1)}, bf16[128,1024]{1,0:T(8,128)(2,1)S(1)}, u32[]{:S(2)}, u32[]{:S(2)}) %collective-permute-start.2) | collective-permute-done | bytes 262176 | tf_op jit(solution)/shard_map/ppermute | solution.py:453
  152.0 0.9 collective-permute-done.3.refs_2_
  152.9 3.7 %all-to-all-done.2 = bf16[512,3,4,128]{3,2,1,0:T(4,128)(2,1)S(1)} async-done(((bf16[512,3,4,128]{3,2,1,0:T(4,128)(2,1)}), bf16[512,3,4,128]{3,2,1,0:T(4,128)(2,1)S(1)}, u32[]{:S(2)}, u32[]{:S(2)}) %all-to-all-start.2) | async-done | bytes 1572896 | tf_op jit(solution)/shard_map/all_to_all | solution.py:471
  156.6 3.9 %shard_map.109 = (bf16[256,512]{1,0:T(8,128)(2,1)}, bf16[128,512]{1,0:T(8,128)(2,1)}) custom-call(bf16[6144,128]{1,0:T(8,128)(2,1)S(1)} %bitcast.16, bf16[128,1024]{1,0:T(8,128)(2,1)S(1)} %collective-permute-done.2.refs_1_, bf16[128,1024]{1,0:T(8,128)(2,1)S(1)} %collective-permute-done.3.refs_2_, s32[512,128]{1,0:T(8,128)} %bitcast.19, ...), custom_call_target="tpu_custom_call" | custom-call | flops 402653184 | bytes 6555648 | tf_op jit(solution)/shard_map/pallas_call | solution.py:54
Async XLA Ops:
  2.4 38.9 %all-to-all-start = ((s32[512,1,128]{2,1,0:T(1,128)}), s32[512,1,128]{2,1,0:T(1,128)S(1)}, u32[]{:S(2)}, u32[]{:S(2)}) async-start(s32[512,1,128]{2,1,0:T(1,128)} %bitcast.24), calls=%async_computation | async-start | bytes 524288 | tf_op jit(solution)/shard_map/all_to_all | solution.py:471
  24.5 20.2 %collective-permute-start.1 = (bf16[128,512]{1,0:T(8,128)(2,1)}, bf16[128,512]{1,0:T(8,128)(2,1)S(1)}, u32[]{:S(2)}, u32[]{:S(2)}) collective-permute-start(bf16[128,512]{1,0:T(8,128)(2,1)} %bitcast.20), channel_id=1, source_target_pairs={{0,64},{32,96},{64,128},{96,160},{128,192},{160,224},{192,256},{22... | collective-permute-start | bytes 393224 | tf_op jit(solution)/shard_map/ppermute | solution.py:453
  28.2 16.5 %collective-permute-start = (bf16[128,512]{1,0:T(8,128)(2,1)}, bf16[128,512]{1,0:T(8,128)(2,1)S(1)}, u32[]{:S(2)}, u32[]{:S(2)}) collective-permute-start(bf16[128,512]{1,0:T(8,128)(2,1)} %bitcast.21), channel_id=1, source_target_pairs={{0,32},{32,64},{64,96},{96,128},{128,160},{160,192},{192,224},{224... | collective-permute-start | bytes 393224 | tf_op jit(solution)/shard_map/ppermute | solution.py:453
  41.3 0.7 copy-start
  44.7 0.7 copy-start.1
  44.7 0.7 copy-start.2
  45.4 53.4 %all-to-all-start.1 = ((bf16[512,3,4,128]{3,2,1,0:T(4,128)(2,1)}), bf16[512,3,4,128]{3,2,1,0:T(4,128)(2,1)S(1)}, u32[]{:S(2)}, u32[]{:S(2)}) async-start(bf16[512,3,4,128]{3,2,1,0:T(4,128)(2,1)} %bitcast.17), calls=%async_computation.1 | async-start | bytes 3145728 | tf_op jit(solution)/shard_map/all_to_all | solution.py:471
  103.5 53.1 %all-to-all-start.2 = ((bf16[512,3,4,128]{3,2,1,0:T(4,128)(2,1)}), bf16[512,3,4,128]{3,2,1,0:T(4,128)(2,1)S(1)}, u32[]{:S(2)}, u32[]{:S(2)}) async-start(bf16[512,3,4,128]{3,2,1,0:T(4,128)(2,1)} %bitcast.11), calls=%async_computation.2 | async-start | bytes 3145728 | tf_op jit(solution)/shard_map/all_to_all | solution.py:471
  119.6 32.4 %collective-permute-start.2 = (bf16[128,1024]{1,0:T(8,128)(2,1)}, bf16[128,1024]{1,0:T(8,128)(2,1)S(1)}, u32[]{:S(2)}, u32[]{:S(2)}) collective-permute-start(bf16[128,1024]{1,0:T(8,128)(2,1)} %get-tuple-element.43), channel_id=1, source_target_pairs={{32,0},{64,32},{96,64},{128,96},{160,128},{192,160},{224,192},{256... | collective-permute-start | bytes 786440 | tf_op jit(solution)/shard_map/ppermute | solution.py:453
  125.8 27.1 %collective-permute-start.3 = (bf16[128,1024]{1,0:T(8,128)(2,1)}, bf16[128,1024]{1,0:T(8,128)(2,1)S(1)}, u32[]{:S(2)}, u32[]{:S(2)}) collective-permute-start(bf16[128,1024]{1,0:T(8,128)(2,1)} %get-tuple-element.44), channel_id=1, source_target_pairs={{64,0},{96,32},{128,64},{160,96},{192,128},{224,160},{256,192},{28... | collective-permute-start | bytes 786440 | tf_op jit(solution)/shard_map/ppermute | solution.py:453

commit v3 on v2

--- a/solution.py
+++ b/solution.py
@@ -13,7 +13,7 @@
 CHUNKS = 4
 LANES = 128
 SLOTS = CAP + 1
-PIECES = 2
+PIECES = 4
 NBANK = SLOTS * CHUNKS
 F32 = jnp.float32
 BF16 = jnp.bfloat16
@@ -42,9 +42,12 @@
             copies[-1].start()
             refs[i] = held[j]
 
-        def loaded():
-            for copy in copies:
+        waiting = list(copies)
+
+        def loaded(count=len(copies)):
+            for copy in waiting[:count]:
                 copy.wait()
+            del waiting[:count]
 
         return kernel(loaded, *refs)
 
@@ -151,9 +154,10 @@
     return ref.at[pl.ds(i * size, size), :]
 
 
-def serve_kernel(asks_ref, table_ref, out_ref, wide, narrow, sems):
+def serve_kernel(loaded, asks_ref, table_ref, out_ref, wide, narrow, sems):
     owners = asks_ref.shape[0] // PIECES
     rows = table_ref.shape[0]
+    loaded()
     table = table_ref[...]
     row_id = lax.broadcasted_iota(jnp.int32, (owners, rows), 1)
     copies = []
@@ -203,6 +207,7 @@
 
 
 def forward_kernel(
+    loaded,
     place_ref,
     sess_ref,
     far_ref,
@@ -223,6 +228,7 @@
     values_ref,
 ):
     n, width = own_ref.shape
+    loaded()
     gain = gain_ref[...]
     hist_f = own_ref[...].astype(F32)
 
@@ -282,17 +288,14 @@
     narrow,
     wide,
     sems,
+    held,
+    held_sem,
 ):
     n = unit_ref.shape[0]
-    owners = neg_row_ref.shape[1] // PIECES
+    owners = neg_row_ref.shape[1]
     wide[...] = fetched_ref[...].astype(F32)
-    neg_units, neg_lens, neg_bfs = [], [], []
-    for i in range(PIECES):
-        unit, length = item_norm(slot_rows(wide, i * owners * NBANK, CAP, owners))
-        neg_units.append(unit)
-        neg_lens.append(length)
-        neg_bfs.append(unit.astype(BF16))
-    neg_bf = jnp.concatenate(neg_bfs, axis=0)
+    neg_unit, neg_len = item_norm(slot_rows(wide, 0, CAP, owners))
+    neg_bf = neg_unit.astype(BF16)
     loaded()
     user_unit = unit_ref[...]
     user_bf = user_unit.astype(BF16)
@@ -306,10 +309,9 @@
     slot_col = slot_col_ref[...]
     lane = lax.broadcasted_iota(jnp.int32, (n, owners), 1) * CAP
     hots, rows = [], []
-    for i in range(PIECES):
-        for k in range(CAP):
-            hots.append(jnp.where(slot_col == lane + (i * owners * CAP + k), 1.0, 0.0).astype(BF16))
-            rows.append(slot_rows(wide, i * owners * NBANK, k, owners))
+    for k in range(CAP):
+        hots.append(jnp.where(slot_col == lane + k, 1.0, 0.0).astype(BF16))
+        rows.append(slot_rows(wide, 0, k, owners))
     pos_rows = dot(jnp.concatenate(hots, axis=1), jnp.concatenate(rows, axis=0))
     pos_unit, pos_len = item_norm(pos_rows)
     pos_bf = pos_unit.astype(BF16).astype(F32)
@@ -317,27 +319,30 @@
     denominator = pos_exp + jnp.sum(neg_exp, axis=-1, keepdims=True)
     pos_delta = pos_exp / denominator - 1.0
     neg_prob = (neg_exp / denominator).astype(BF16)
+    unit_grad = (pos_delta * pos_bf + dot(neg_prob, neg_bf)) / TAU
+    held[...] = (
+        unit_grad - user_unit * jnp.sum(user_unit * unit_grad, axis=-1, keepdims=True)
+    ) / length_ref[:, 0:1]
+    copies = [pltpu.make_async_copy(held, user_grad_ref, held_sem)]
+    copies[0].start()
     raw_pos = pos_delta * user_f / TAU
     pos_grad = (raw_pos - pos_unit * jnp.sum(pos_unit * raw_pos, axis=-1, keepdims=True)) / pos_len
     pos_grad = pos_grad.astype(BF16)
     slot_row = slot_row_ref[...]
+    owners = owners // PIECES
     lead = lax.broadcasted_iota(jnp.int32, (owners, n), 0) * CAP
-    copies = []
     for i in range(PIECES):
         base = i * owners * NBANK
         for k in range(CAP):
             hot = jnp.where(slot_row == lead + (i * owners * CAP + k), 1.0, 0.0).astype(BF16)
             spread_slot(wide, base, k, dot(hot, pos_grad))
-        raw_neg = dot(neg_prob[:, i * owners : (i + 1) * owners], user_bf, (0, 0)) / TAU
-        along = jnp.sum(neg_units[i] * raw_neg, axis=-1, keepdims=True)
-        spread_slot(wide, base, CAP, (raw_neg - neg_units[i] * along) / neg_lens[i])
+        own = slice(i * owners, (i + 1) * owners)
+        raw_neg = dot(neg_prob[:, own], user_bf, (0, 0)) / TAU
+        along = jnp.sum(neg_unit[own] * raw_neg, axis=-1, keepdims=True)
+        spread_slot(wide, base, CAP, (raw_neg - neg_unit[own] * along) / neg_len[own])
         narrow[base : base + owners * NBANK, :] = wide[base : base + owners * NBANK, :].astype(BF16)
         copies.append(pltpu.make_async_copy(piece(narrow, i), piece(send_ref, i), sems.at[i]))
         copies[-1].start()
-    unit_grad = (pos_delta * pos_bf + dot(neg_prob, neg_bf)) / TAU
-    user_grad_ref[...] = (
-        unit_grad - user_unit * jnp.sum(user_unit * unit_grad, axis=-1, keepdims=True)
-    ) / length_ref[:, 0:1]
     for copy in copies:
         copy.wait()
 
@@ -417,16 +422,18 @@
     table_grad_ref,
     history_grad_ref,
     wide,
+    held,
+    held_sem,
 ):
     width = hist_ref.shape[1]
-    owners = asks_ref.shape[0] // PIECES
+    owners = asks_ref.shape[0] // 2
     rows = table_grad_ref.shape[0]
     wide[...] = returned_ref[...].astype(F32)
-    loaded()
+    loaded(1)
     asks = jnp.transpose(asks_ref[...].astype(F32))
     row_id = lax.broadcasted_iota(jnp.int32, (rows, owners), 0).astype(F32)
     total = None
-    for i in range(PIECES):
+    for i in range(2):
         hots, parts = [], []
         for k in range(SLOTS):
             asked = asks[k : k + 1, i * owners : (i + 1) * owners]
@@ -434,7 +441,10 @@
             parts.append(slot_rows(wide, i * owners * NBANK, k, owners))
         part = dot(jnp.concatenate(hots, axis=1), jnp.concatenate(parts, axis=0))
         total = part if total is None else total + part
-    table_grad_ref[...] = total.astype(BF16)
+    held[...] = total.astype(BF16)
+    copy = pltpu.make_async_copy(held, table_grad_ref, held_sem)
+    copy.start()
+    loaded()
     come = near_ref[...].astype(F32) + far_ref[...].astype(F32)
     proj_grad = ((own_grad_ref[...] + come) * slope_ref[...]).astype(BF16)
     in_grad = (
@@ -445,6 +455,7 @@
     normed_x, scale_x = layer_stats(hist_ref[...].astype(F32))
     back = norm_back(in_grad * gain_ref[...], normed_x, scale_x)
     history_grad_ref[...] = (back + user_grad_ref[...]).astype(BF16)
+    copy.wait()
 
 
 def passed_along(shard, axis, by):
@@ -491,10 +502,11 @@
     (served,) = call(
         serve_kernel,
         [shaped((big, LANES), BF16)],
-        [VMEM, VMEM],
+        [VMEM, None],
         (asks, item_table),
         2 * SLOTS * owners * rows * width,
         outward,
+        mib=40,
         out_specs=(HBM,),
     )
     served, near, far = lax.optimization_barrier((served, near, far))
@@ -503,20 +515,21 @@
     unit, length, attn_hat, scale_a, gate, query, slope_gq, slope_vk, keys, values = call(
         forward_kernel,
         [
-            shaped((n, width), F32),
-            shaped((n, LANES), F32),
-            shaped((n, width), F32),
-            shaped((n, LANES), F32),
-            shaped((n, width), BF16),
-            shaped((n, width), BF16),
-            shaped((n, 2 * width), F32),
-            shaped((n, 2 * width), F32),
-            shaped((3 * n, width), BF16),
-            shaped((3 * n, width), BF16),
+            pltpu.HBM((n, width), F32),
+            pltpu.HBM((n, LANES), F32),
+            pltpu.HBM((n, width), F32),
+            pltpu.HBM((n, LANES), F32),
+            pltpu.HBM((n, width), BF16),
+            pltpu.HBM((n, width), BF16),
+            pltpu.HBM((n, 2 * width), F32),
+            pltpu.HBM((n, 2 * width), F32),
+            pltpu.HBM((3 * n, width), BF16),
+            pltpu.HBM((3 * n, width), BF16),
         ],
-        [SMEM, SMEM] + [VMEM] * 6,
+        [SMEM, SMEM, VMEM, VMEM] + [None] * 4,
         (place, sessions, far, near, own, gain, w_in, w_out),
         2 * n * width * width * 12,
+        mib=40,
     )
 
     send, user_grad = call(
@@ -525,9 +538,9 @@
         [VMEM] + [None] * 5,
         (fetched, neg_row, slot_row, slot_col, unit, length),
         2 * n * width * owners * 7,
-        staging,
+        staging + [pltpu.VMEM((n, width), F32), pltpu.SemaphoreType.DMA(())],
         mib=40,
-        out_specs=(HBM, VMEM),
+        out_specs=(HBM, HBM),
     )
     returned = exchange(send, (SLOTS, CHUNKS, LANES))
 
@@ -576,8 +589,9 @@
             user_grad,
         ),
         2 * SLOTS * owners * rows * width,
-        [staging[1]],
+        [staging[1], pltpu.VMEM((rows, width), BF16), pltpu.SemaphoreType.DMA(())],
         mib=40,
+        out_specs=(HBM, VMEM),
     )
     return history_grad[None], table_grad
 

time: 161 us -> 159 us (0.988)
  no operation moved by 1% of the time
where the time goes in v3:
time: 159 us
  waiting for transfers between devices  76 us (48%)
  starting transfers between devices  57.7 us (36%)
  Pallas kernels  24.1 us (15%)
    all_to_all x3, waiting for transfers between devices, exchange(): lax.all_to_all(split, axes, split_axis=0, concat_axis=0, tiled=True)  50.2 us
    all_to_all x3, starting transfers between devices, exchange(): lax.all_to_all(split, axes, split_axis=0, concat_axis=0, tiled=True)  42.4 us
    ppermute x4, waiting for transfers between devices, passed_along(): return lax.ppermute(shard, axis, pairs)  25.8 us
    pallas_call x6, Pallas kernels, call(): pl.pallas_call(body, out_shape=tuple(outs), in_specs=[HBM if spec is None...  24.1 us
    ppermute x4, starting transfers between devices, passed_along(): return lax.ppermute(shard, axis, pairs)  15.3 us
  transfers between devices with their start and end apart: 7, of which 5 were waited for; matrix products, arithmetic and copies ran while one was open for 0% of the time, Pallas kernels for 9%

profile of v3, /device:TPU:1, one launch (start us, length us, event | category | flops | bytes accessed | tf_op | source)
XLA Modules:
  0.0 158.8 jit_solution(15279451316958886707)
XLA Ops:
  0.6 1.7 %shard_map.104 = (s32[512,128]{1,0:T(8,128)}, s32[1,128]{1,0:T(1,128)}, s32[128,1]{1,0:T(8,128)}) custom-call(s32[1,128]{1,0:T(1,128)} %bitcast.29, s32[1,128]{1,0:T(1,128)} %refs_1_.4, s32[1,512]{1,0:T(1,128)} %bitcast.26), custom_call_target="tpu_custom_call" | custom-call | flops 33554432 | bytes 266240 | tf_op jit(solution)/shard_map/pallas_call | solution.py:57
  2.4 22.2 %all-to-all-start = ((s32[512,1,128]{2,1,0:T(1,128)}), s32[512,1,128]{2,1,0:T(1,128)S(1)}, u32[]{:S(2)}, u32[]{:S(2)}) async-start(s32[512,1,128]{2,1,0:T(1,128)} %bitcast.23), calls=%async_computation | async-start | bytes 524288 | tf_op jit(solution)/shard_map/all_to_all | solution.py:482
  24.5 3.7 %collective-permute-start.1 = (bf16[128,512]{1,0:T(8,128)(2,1)}, bf16[128,512]{1,0:T(8,128)(2,1)S(1)}, u32[]{:S(2)}, u32[]{:S(2)}) collective-permute-start(bf16[128,512]{1,0:T(8,128)(2,1)} %bitcast.19), channel_id=1, source_target_pairs={{0,64},{32,96},{64,128},{96,160},{128,192},{160,224},{192,256},{22... | collective-permute-start | bytes 393224 | tf_op jit(solution)/shard_map/ppermute | solution.py:464
  28.2 4.2 %collective-permute-start = (bf16[128,512]{1,0:T(8,128)(2,1)}, bf16[128,512]{1,0:T(8,128)(2,1)S(1)}, u32[]{:S(2)}, u32[]{:S(2)}) collective-permute-start(bf16[128,512]{1,0:T(8,128)(2,1)} %bitcast.20), channel_id=1, source_target_pairs={{0,32},{32,64},{64,96},{96,128},{128,160},{160,192},{192,224},{224... | collective-permute-start | bytes 393224 | tf_op jit(solution)/shard_map/ppermute | solution.py:464
  32.4 8.9 %all-to-all-done = s32[512,1,128]{2,1,0:T(1,128)S(1)} async-done(((s32[512,1,128]{2,1,0:T(1,128)}), s32[512,1,128]{2,1,0:T(1,128)S(1)}, u32[]{:S(2)}, u32[]{:S(2)}) %all-to-all-start) | async-done | bytes 262176 | tf_op jit(solution)/shard_map/all_to_all | solution.py:482
  41.3 0.0 copy-start
  41.3 2.6 %shard_map.105 = bf16[6144,128]{1,0:T(8,128)(2,1)} custom-call(s32[512,128]{1,0:T(8,128)S(1)} %bitcast.17, bf16[256,512]{1,0:T(8,128)(2,1)} %refs_1_.5), custom_call_target="tpu_custom_call" | custom-call | flops 402653184 | bytes 2097152 | tf_op jit(solution)/shard_map/pallas_call | solution.py:57
  43.9 0.0 collective-permute-done.1.refs_2_
  43.9 0.0 collective-permute-done.refs_3_
  43.9 0.0 copy-start.1
  43.9 0.0 copy-done
  44.0 10.7 %all-to-all-start.1 = ((bf16[512,3,4,128]{3,2,1,0:T(4,128)(2,1)}), bf16[512,3,4,128]{3,2,1,0:T(4,128)(2,1)S(1)}, u32[]{:S(2)}, u32[]{:S(2)}) async-start(bf16[512,3,4,128]{3,2,1,0:T(4,128)(2,1)} %bitcast.6), calls=%async_computation.1 | async-start | bytes 3145728 | tf_op jit(solution)/shard_map/all_to_all | solution.py:482
  54.6 0.1 pad_add_fusion.refs_0_
  54.7 0.0 copy-start.2
  54.7 0.0 copy-done.1
  54.7 5.8 %shard_map.106 = (f32[128,512]{1,0:T(8,128)}, f32[128,128]{1,0:T(8,128)}, f32[128,512]{1,0:T(8,128)}, f32[128,128]{1,0:T(8,128)}, bf16[128,512]{1,0:T(8,128)(2,1...) custom-call(s32[2]{0:T(128)S(1)} %pad_add_fusion.refs_0_, ...), custom_call_target="tpu_custom_call" | custom-call | flops 805306368 | bytes 5769288 | tf_op jit(solution)/shard_map/pallas_call | solution.py:57
  60.6 37.6 %all-to-all-done.1 = bf16[512,3,4,128]{3,2,1,0:T(4,128)(2,1)S(1)} async-done(((bf16[512,3,4,128]{3,2,1,0:T(4,128)(2,1)}), bf16[512,3,4,128]{3,2,1,0:T(4,128)(2,1)S(1)}, u32[]{:S(2)}, u32[]{:S(2)}) %all-to-all-start.1) | async-done | bytes 1572896 | tf_op jit(solution)/shard_map/all_to_all | solution.py:482
  98.2 3.9 %shard_map.107 = (bf16[6144,128]{1,0:T(8,128)(2,1)}, f32[128,512]{1,0:T(8,128)}) custom-call(bf16[6144,128]{1,0:T(8,128)(2,1)S(1)} %bitcast.15, s32[1,512]{1,0:T(1,128)} %bitcast.27, s32[1,128]{1,0:T(1,128)} %get-tuple-element.28.refs_2_, s32[128,1]{1,0:T(8,128)} %get-tuple-element.29.refs_3_, f32[128,512]{1,0:T(8,128)} %get-tuple-element.32.refs_4_, ...), custom_call_target="tpu_custom_call" | custom-call | flops 469762048 | bytes 3738624 | tf_op jit(solution)/shard_map/pallas_call | solution.py:57
  102.1 0.0 copy-done.2
  102.1 9.5 %all-to-all-start.2 = ((bf16[512,3,4,128]{3,2,1,0:T(4,128)(2,1)}), bf16[512,3,4,128]{3,2,1,0:T(4,128)(2,1)S(1)}, u32[]{:S(2)}, u32[]{:S(2)}) async-start(bf16[512,3,4,128]{3,2,1,0:T(4,128)(2,1)} %bitcast.11), calls=%async_computation.2 | async-start | bytes 3145728 | tf_op jit(solution)/shard_map/all_to_all | solution.py:482
  111.6 6.6 %shard_map.108 = (f32[128,1024]{1,0:T(8,128)}, bf16[128,1024]{1,0:T(8,128)(2,1)}, bf16[128,1024]{1,0:T(8,128)(2,1)}, f32[128,512]{1,0:T(8,128)}) custom-call(s32[2]{0:T(128)} %copy-done.2, s32[1,16]{1,0:T(1,128)} %refs_1_.7, f32[128,512]{1,0:T(8,128)} %get-tuple-element.35.refs_2_.refs_10_, bf16[512,512]{1,0:T(8,128)(2,1)} %refs_3_.1, ...), custom_call_target="tpu_custom_call" | custom-call | flops 805306368 | bytes 6094920 | tf_op jit(solution)/shard_map/pallas_call | solution.py:57
  118.2 6.2 %collective-permute-start.2 = (bf16[128,1024]{1,0:T(8,128)(2,1)}, bf16[128,1024]{1,0:T(8,128)(2,1)S(1)}, u32[]{:S(2)}, u32[]{:S(2)}) collective-permute-start(bf16[128,1024]{1,0:T(8,128)(2,1)} %get-tuple-element.43), channel_id=1, source_target_pairs={{32,0},{64,32},{96,64},{128,96},{160,128},{192,160},{224,192},{256... | collective-permute-start | bytes 786440 | tf_op jit(solution)/shard_map/ppermute | solution.py:464
  124.4 1.3 collective-permute-start.3
  125.7 24.9 %collective-permute-done.2.refs_1_ = bf16[128,1024]{1,0:T(8,128)(2,1)S(1)} collective-permute-done((bf16[128,1024]{1,0:T(8,128)(2,1)}, bf16[128,1024]{1,0:T(8,128)(2,1)S(1)}, u32[]{:S(2)}, u32[]{:S(2)}) %collective-permute-start.2) | collective-permute-done | bytes 262176 | tf_op jit(solution)/shard_map/ppermute | solution.py:464
  150.6 0.9 collective-permute-done.3.refs_2_
  151.5 3.7 %all-to-all-done.2 = bf16[512,3,4,128]{3,2,1,0:T(4,128)(2,1)S(1)} async-done(((bf16[512,3,4,128]{3,2,1,0:T(4,128)(2,1)}), bf16[512,3,4,128]{3,2,1,0:T(4,128)(2,1)S(1)}, u32[]{:S(2)}, u32[]{:S(2)}) %all-to-all-start.2) | async-done | bytes 1572896 | tf_op jit(solution)/shard_map/all_to_all | solution.py:482
  155.2 3.4 %shard_map.109 = (bf16[256,512]{1,0:T(8,128)(2,1)}, bf16[128,512]{1,0:T(8,128)(2,1)}) custom-call(bf16[6144,128]{1,0:T(8,128)(2,1)S(1)} %bitcast.16, bf16[128,1024]{1,0:T(8,128)(2,1)S(1)} %collective-permute-done.2.refs_1_, bf16[128,1024]{1,0:T(8,128)(2,1)S(1)} %collective-permute-done.3.refs_2_, s32[512,128]{1,0:T(8,128)} %bitcast.18, ...), custom_call_target="tpu_custom_call" | custom-call | flops 402653184 | bytes 6555648 | tf_op jit(solution)/shard_map/pallas_call | solution.py:57
Async XLA Ops:
  2.4 38.9 %all-to-all-start = ((s32[512,1,128]{2,1,0:T(1,128)}), s32[512,1,128]{2,1,0:T(1,128)S(1)}, u32[]{:S(2)}, u32[]{:S(2)}) async-start(s32[512,1,128]{2,1,0:T(1,128)} %bitcast.23), calls=%async_computation | async-start | bytes 524288 | tf_op jit(solution)/shard_map/all_to_all | solution.py:482
  24.5 19.4 %collective-permute-start.1 = (bf16[128,512]{1,0:T(8,128)(2,1)}, bf16[128,512]{1,0:T(8,128)(2,1)S(1)}, u32[]{:S(2)}, u32[]{:S(2)}) collective-permute-start(bf16[128,512]{1,0:T(8,128)(2,1)} %bitcast.19), channel_id=1, source_target_pairs={{0,64},{32,96},{64,128},{96,160},{128,192},{160,224},{192,256},{22... | collective-permute-start | bytes 393224 | tf_op jit(solution)/shard_map/ppermute | solution.py:464
  28.2 15.7 %collective-permute-start = (bf16[128,512]{1,0:T(8,128)(2,1)}, bf16[128,512]{1,0:T(8,128)(2,1)S(1)}, u32[]{:S(2)}, u32[]{:S(2)}) collective-permute-start(bf16[128,512]{1,0:T(8,128)(2,1)} %bitcast.20), channel_id=1, source_target_pairs={{0,32},{32,64},{64,96},{96,128},{128,160},{160,192},{192,224},{224... | collective-permute-start | bytes 393224 | tf_op jit(solution)/shard_map/ppermute | solution.py:464
  41.3 2.7 %copy-start = (s32[512,1,128]{2,1,0:T(1,128)}, s32[512,1,128]{2,1,0:T(1,128)S(1)}, u32[]{:S(2)}) copy-start(s32[512,1,128]{2,1,0:T(1,128)S(1)} %all-to-all-done) | copy-start | bytes 786436
  43.9 10.8 %copy-start.1 = (s32[1,16]{1,0:T(1,128)S(1)}, s32[1,16]{1,0:T(1,128)}, u32[]{:S(2)}) copy-start(s32[1,16]{1,0:T(1,128)} %refs_1_.7) | copy-start | bytes 196
  44.0 54.2 %all-to-all-start.1 = ((bf16[512,3,4,128]{3,2,1,0:T(4,128)(2,1)}), bf16[512,3,4,128]{3,2,1,0:T(4,128)(2,1)S(1)}, u32[]{:S(2)}, u32[]{:S(2)}) async-start(bf16[512,3,4,128]{3,2,1,0:T(4,128)(2,1)} %bitcast.6), calls=%async_computation.1 | async-start | bytes 3145728 | tf_op jit(solution)/shard_map/all_to_all | solution.py:482
  54.7 47.4 %copy-start.2 = (s32[2]{0:T(128)}, s32[2]{0:T(128)S(1)}, u32[]{:S(2)}) copy-start(s32[2]{0:T(128)S(1)} %pad_add_fusion.refs_0_) | copy-start | bytes 28
  102.1 53.1 %all-to-all-start.2 = ((bf16[512,3,4,128]{3,2,1,0:T(4,128)(2,1)}), bf16[512,3,4,128]{3,2,1,0:T(4,128)(2,1)S(1)}, u32[]{:S(2)}, u32[]{:S(2)}) async-start(bf16[512,3,4,128]{3,2,1,0:T(4,128)(2,1)} %bitcast.11), calls=%async_computation.2 | async-start | bytes 3145728 | tf_op jit(solution)/shard_map/all_to_all | solution.py:482
  118.2 32.4 %collective-permute-start.2 = (bf16[128,1024]{1,0:T(8,128)(2,1)}, bf16[128,1024]{1,0:T(8,128)(2,1)S(1)}, u32[]{:S(2)}, u32[]{:S(2)}) collective-permute-start(bf16[128,1024]{1,0:T(8,128)(2,1)} %get-tuple-element.43), channel_id=1, source_target_pairs={{32,0},{64,32},{96,64},{128,96},{160,128},{192,160},{224,192},{256... | collective-permute-start | bytes 786440 | tf_op jit(solution)/shard_map/ppermute | solution.py:464
  124.4 27.1 %collective-permute-start.3 = (bf16[128,1024]{1,0:T(8,128)(2,1)}, bf16[128,1024]{1,0:T(8,128)(2,1)S(1)}, u32[]{:S(2)}, u32[]{:S(2)}) collective-permute-start(bf16[128,1024]{1,0:T(8,128)(2,1)} %get-tuple-element.44), channel_id=1, source_target_pairs={{64,0},{96,32},{128,64},{160,96},{192,128},{224,160},{256,192},{28... | collective-permute-start | bytes 786440 | tf_op jit(solution)/shard_map/ppermute | solution.py:464

commit v4 on v3

--- a/solution.py
+++ b/solution.py
@@ -1,3 +1,4 @@
+import functools
 import math
 
 import jax
@@ -104,9 +105,12 @@
     return 1.0 / (1.0 + jnp.exp(-value))
 
 
-def ask_kernel(owner_ref, row_ref, neg_ref, ask_ref, slot_row_ref, slot_col_ref):
+def ask_kernel(
+    items, hists, owner_ref, row_ref, neg_ref, ask_ref, slot_row_ref, slot_col_ref, neg_row_ref
+):
     n = owner_ref.shape[1]
     owners = ask_ref.shape[0]
+    item_bits, hist_bits = items.bit_length() - 1, hists.bit_length() - 1
     lead = lax.broadcasted_iota(jnp.int32, (n, n), 0)
     lane = lax.broadcasted_iota(jnp.int32, (n, n), 1)
 
@@ -114,14 +118,15 @@
         spread = jnp.broadcast_to(row.astype(F32), (n, n))
         return jnp.sum(jnp.where(lead == lane, spread, 0.0), axis=1, keepdims=True)
 
-    owner_r = jnp.broadcast_to(owner_ref[...].astype(F32), (n, n))
-    owner_c = column(owner_ref[...])
-    same = owner_r == owner_c
+    place = ((owner_ref[...] & (items - 1)) << hist_bits) + (owner_ref[...] >> item_bits)
+    place_r = jnp.broadcast_to(place.astype(F32), (n, n))
+    place_c = column(place)
+    same = place_r == place_c
     rank_r = jnp.sum(jnp.where(same & (lead < lane), 1.0, 0.0), axis=0, keepdims=True)
     rank_c = jnp.sum(jnp.where(same & (lane < lead), 1.0, 0.0), axis=1, keepdims=True)
-    slot_r = owner_ref[...] * CAP + rank_r.astype(jnp.int32)
+    slot_r = place * CAP + rank_r.astype(jnp.int32)
     slot_row_ref[...] = slot_r
-    slot_col_ref[...] = (owner_c * CAP + rank_c).astype(jnp.int32)
+    slot_col_ref[...] = (place_c * CAP + rank_c).astype(jnp.int32)
     rows = jnp.broadcast_to(column(row_ref[...]), (n, LANES))
     by_owner = lax.broadcasted_iota(jnp.int32, (owners, n), 0) * CAP
     asked = None
@@ -129,10 +134,16 @@
         hot = jnp.where(slot_r == by_owner + k, 1.0, 0.0).astype(BF16)
         part = dot(hot, jnp.where(lane == k, rows, 0.0).astype(BF16))
         asked = part if asked is None else asked + part
+    neg_all = jnp.broadcast_to(neg_ref[...].astype(F32), (n, owners))
+    at = lax.broadcasted_iota(jnp.int32, (n, owners), 0)
+    named = lax.broadcasted_iota(jnp.int32, (n, owners), 1)
     for c in range(owners // n):
-        negative = column(neg_ref[:, c * n : (c + 1) * n])
-        ask_ref[c * n : (c + 1) * n, :] = jnp.where(
-            lane == CAP, negative, asked[c * n : (c + 1) * n]
+        own = slice(c * n, (c + 1) * n)
+        owner = (((at + c * n) & (hists - 1)) << item_bits) + ((at + c * n) >> hist_bits)
+        negative = jnp.sum(jnp.where(owner == named, neg_all, 0.0), axis=1, keepdims=True)
+        ask_ref[own, :] = jnp.where(lane == CAP, negative, asked[own]).astype(jnp.int32)
+        neg_row_ref[:, own] = jnp.sum(
+            jnp.where(lead == lane, negative, 0.0), axis=0, keepdims=True
         ).astype(jnp.int32)
 
 
@@ -470,7 +481,7 @@
     hists = lax.axis_size("hist")
     owners = hists * items
     rows = item_table.shape[0]
-    axes = ("hist", "items")
+    axes = ("items", "hist")
     place = jnp.stack([lax.axis_index("hist"), lax.axis_index("items")]).astype(jnp.int32)
     own = history[0]
     gain = ln_gain.reshape(1, width)
@@ -481,9 +492,14 @@
         split = shard.reshape((owners,) + chunk)
         return lax.all_to_all(split, axes, split_axis=0, concat_axis=0, tiled=True).reshape(shape)
 
-    ask, slot_row, slot_col = call(
-        ask_kernel,
-        [shaped((owners, LANES), jnp.int32), shaped((1, n), jnp.int32), shaped((n, 1), jnp.int32)],
+    ask, slot_row, slot_col, neg_row = call(
+        functools.partial(ask_kernel, items, hists),
+        [
+            shaped((owners, LANES), jnp.int32),
+            shaped((1, n), jnp.int32),
+            shaped((n, 1), jnp.int32),
+            shaped((1, owners), jnp.int32),
+        ],
         [VMEM, VMEM, VMEM],
         (pos_owner.reshape(1, n), pos_row, neg_row),
         2 * CAP * owners * n * LANES,

time: 159 us -> 159 us (level)
  no operation moved by 1% of the time
where the time goes in v4:
time: 159 us; the launch traced here: 158 us
  waiting for transfers between devices  75.2 us (47%)
  starting transfers between devices  57.9 us (36%)
  Pallas kernels  24.1 us (15%)
    all_to_all x3, waiting for transfers between devices, exchange(): lax.all_to_all(split, axes, split_axis=0, concat_axis=0, tiled=True)  49.7 us
    all_to_all x3, starting transfers between devices, exchange(): lax.all_to_all(split, axes, split_axis=0, concat_axis=0, tiled=True)  42.6 us
    ppermute x4, waiting for transfers between devices, passed_along(): return lax.ppermute(shard, axis, pairs)  25.5 us
    pallas_call x6, Pallas kernels, call(): pl.pallas_call(body, out_shape=tuple(outs), in_specs=[HBM if spec is None...  24.1 us
    ppermute x4, starting transfers between devices, passed_along(): return lax.ppermute(shard, axis, pairs)  15.3 us
  transfers between devices with their start and end apart: 7, of which 5 were waited for; matrix products, arithmetic and copies ran while one was open for 0% of the time, Pallas kernels for 9%

profile of v4, /device:TPU:1, one launch (start us, length us, event | category | flops | bytes accessed | tf_op | source)
XLA Modules:
  0.0 158.3 jit_solution(12057053553839890225)
XLA Ops:
  0.6 1.8 %shard_map.104 = (s32[512,128]{1,0:T(8,128)}, s32[1,128]{1,0:T(1,128)}, s32[128,1]{1,0:T(8,128)}, s32[1,512]{1,0:T(1,128)}) custom-call(s32[1,128]{1,0:T(1,128)} %bitcast.28, s32[1,128]{1,0:T(1,128)} %refs_1_.4, s32[1,512]{1,0:T(1,128)} %bitcast.27), custom_call_target="tpu_custom_call" | custom-call | flops 33554432 | bytes 268288 | tf_op jit(solution)/shard_map/pallas_call | solution.py:58
  2.4 22.2 %all-to-all-start = ((s32[512,1,128]{2,1,0:T(1,128)}), s32[512,1,128]{2,1,0:T(1,128)S(1)}, u32[]{:S(2)}, u32[]{:S(2)}) async-start(s32[512,1,128]{2,1,0:T(1,128)} %bitcast.23), calls=%async_computation | async-start | bytes 524288 | tf_op jit(solution)/shard_map/all_to_all | solution.py:493
  24.6 3.7 %collective-permute-start.1 = (bf16[128,512]{1,0:T(8,128)(2,1)}, bf16[128,512]{1,0:T(8,128)(2,1)S(1)}, u32[]{:S(2)}, u32[]{:S(2)}) collective-permute-start(bf16[128,512]{1,0:T(8,128)(2,1)} %bitcast.19), channel_id=1, source_target_pairs={{0,64},{32,96},{64,128},{96,160},{128,192},{160,224},{192,256},{22... | collective-permute-start | bytes 393224 | tf_op jit(solution)/shard_map/ppermute | solution.py:475
  28.3 4.2 %collective-permute-start = (bf16[128,512]{1,0:T(8,128)(2,1)}, bf16[128,512]{1,0:T(8,128)(2,1)S(1)}, u32[]{:S(2)}, u32[]{:S(2)}) collective-permute-start(bf16[128,512]{1,0:T(8,128)(2,1)} %bitcast.20), channel_id=1, source_target_pairs={{0,32},{32,64},{64,96},{96,128},{128,160},{160,192},{192,224},{224... | collective-permute-start | bytes 393224 | tf_op jit(solution)/shard_map/ppermute | solution.py:475
  32.5 8.9 %all-to-all-done = s32[512,1,128]{2,1,0:T(1,128)S(1)} async-done(((s32[512,1,128]{2,1,0:T(1,128)}), s32[512,1,128]{2,1,0:T(1,128)S(1)}, u32[]{:S(2)}, u32[]{:S(2)}) %all-to-all-start) | async-done | bytes 262176 | tf_op jit(solution)/shard_map/all_to_all | solution.py:493
  41.4 0.0 copy-start
  41.4 2.6 %shard_map.105 = bf16[6144,128]{1,0:T(8,128)(2,1)} custom-call(s32[512,128]{1,0:T(8,128)S(1)} %bitcast.17, bf16[256,512]{1,0:T(8,128)(2,1)} %refs_1_.5), custom_call_target="tpu_custom_call" | custom-call | flops 402653184 | bytes 2097152 | tf_op jit(solution)/shard_map/pallas_call | solution.py:58
  44.0 0.0 collective-permute-done.1.refs_2_
  44.0 0.0 collective-permute-done.refs_3_
  44.0 0.0 copy-start.1
  44.1 0.0 copy-done
  44.1 10.6 %all-to-all-start.1 = ((bf16[512,3,4,128]{3,2,1,0:T(4,128)(2,1)}), bf16[512,3,4,128]{3,2,1,0:T(4,128)(2,1)S(1)}, u32[]{:S(2)}, u32[]{:S(2)}) async-start(bf16[512,3,4,128]{3,2,1,0:T(4,128)(2,1)} %bitcast.6), calls=%async_computation.1 | async-start | bytes 3145728 | tf_op jit(solution)/shard_map/all_to_all | solution.py:493
  54.7 0.1 pad_add_fusion.refs_0_
  54.8 0.0 copy-start.2
  54.8 0.0 copy-done.1
  54.8 5.8 %shard_map.106 = (f32[128,512]{1,0:T(8,128)}, f32[128,128]{1,0:T(8,128)}, f32[128,512]{1,0:T(8,128)}, f32[128,128]{1,0:T(8,128)}, bf16[128,512]{1,0:T(8,128)(2,1...) custom-call(s32[2]{0:T(128)S(1)} %pad_add_fusion.refs_0_, ...), custom_call_target="tpu_custom_call" | custom-call | flops 805306368 | bytes 5769288 | tf_op jit(solution)/shard_map/pallas_call | solution.py:58
  60.6 37.2 %all-to-all-done.1 = bf16[512,3,4,128]{3,2,1,0:T(4,128)(2,1)S(1)} async-done(((bf16[512,3,4,128]{3,2,1,0:T(4,128)(2,1)}), bf16[512,3,4,128]{3,2,1,0:T(4,128)(2,1)S(1)}, u32[]{:S(2)}, u32[]{:S(2)}) %all-to-all-start.1) | async-done | bytes 1572896 | tf_op jit(solution)/shard_map/all_to_all | solution.py:493
  97.9 3.9 %shard_map.107 = (bf16[6144,128]{1,0:T(8,128)(2,1)}, f32[128,512]{1,0:T(8,128)}) custom-call(bf16[6144,128]{1,0:T(8,128)(2,1)S(1)} %bitcast.15, s32[1,512]{1,0:T(1,128)} %get-tuple-element.29.refs_1_, s32[1,128]{1,0:T(1,128)} %get-tuple-element.30.refs_2_, s32[128,1]{1,0:T(8,128)} %get-tuple-element.31.refs_3_, f32[128,512]{1,0:T(8,128)} %get-tuple-element.34.refs_4_, ...), custom_call_target="tpu_custom_call" | custom-call | flops 469762048 | bytes 3738624 | tf_op jit(solution)/shard_map/pallas_call | solution.py:58
  101.7 0.0 copy-done.2
  101.7 9.8 %all-to-all-start.2 = ((bf16[512,3,4,128]{3,2,1,0:T(4,128)(2,1)}), bf16[512,3,4,128]{3,2,1,0:T(4,128)(2,1)S(1)}, u32[]{:S(2)}, u32[]{:S(2)}) async-start(bf16[512,3,4,128]{3,2,1,0:T(4,128)(2,1)} %bitcast.11), calls=%async_computation.2 | async-start | bytes 3145728 | tf_op jit(solution)/shard_map/all_to_all | solution.py:493
  111.5 6.6 %shard_map.108 = (f32[128,1024]{1,0:T(8,128)}, bf16[128,1024]{1,0:T(8,128)(2,1)}, bf16[128,1024]{1,0:T(8,128)(2,1)}, f32[128,512]{1,0:T(8,128)}) custom-call(s32[2]{0:T(128)} %copy-done.2, s32[1,16]{1,0:T(1,128)} %refs_1_.7, f32[128,512]{1,0:T(8,128)} %get-tuple-element.37.refs_2_.refs_10_, bf16[512,512]{1,0:T(8,128)(2,1)} %refs_3_.1, ...), custom_call_target="tpu_custom_call" | custom-call | flops 805306368 | bytes 6094920 | tf_op jit(solution)/shard_map/pallas_call | solution.py:58
  118.1 6.2 %collective-permute-start.2 = (bf16[128,1024]{1,0:T(8,128)(2,1)}, bf16[128,1024]{1,0:T(8,128)(2,1)S(1)}, u32[]{:S(2)}, u32[]{:S(2)}) collective-permute-start(bf16[128,1024]{1,0:T(8,128)(2,1)} %get-tuple-element.45), channel_id=1, source_target_pairs={{32,0},{64,32},{96,64},{128,96},{160,128},{192,160},{224,192},{256... | collective-permute-start | bytes 786440 | tf_op jit(solution)/shard_map/ppermute | solution.py:475
  124.3 1.3 collective-permute-start.3
  125.6 25.1 %collective-permute-done.2.refs_1_ = bf16[128,1024]{1,0:T(8,128)(2,1)S(1)} collective-permute-done((bf16[128,1024]{1,0:T(8,128)(2,1)}, bf16[128,1024]{1,0:T(8,128)(2,1)S(1)}, u32[]{:S(2)}, u32[]{:S(2)}) %collective-permute-start.2) | collective-permute-done | bytes 262176 | tf_op jit(solution)/shard_map/ppermute | solution.py:475
  150.8 0.3 collective-permute-done.3.refs_2_
  151.1 3.6 %all-to-all-done.2 = bf16[512,3,4,128]{3,2,1,0:T(4,128)(2,1)S(1)} async-done(((bf16[512,3,4,128]{3,2,1,0:T(4,128)(2,1)}), bf16[512,3,4,128]{3,2,1,0:T(4,128)(2,1)S(1)}, u32[]{:S(2)}, u32[]{:S(2)}) %all-to-all-start.2) | async-done | bytes 1572896 | tf_op jit(solution)/shard_map/all_to_all | solution.py:493
  154.7 3.4 %shard_map.109 = (bf16[256,512]{1,0:T(8,128)(2,1)}, bf16[128,512]{1,0:T(8,128)(2,1)}) custom-call(bf16[6144,128]{1,0:T(8,128)(2,1)S(1)} %bitcast.16, bf16[128,1024]{1,0:T(8,128)(2,1)S(1)} %collective-permute-done.2.refs_1_, bf16[128,1024]{1,0:T(8,128)(2,1)S(1)} %collective-permute-done.3.refs_2_, s32[512,128]{1,0:T(8,128)} %bitcast.18, ...), custom_call_target="tpu_custom_call" | custom-call | flops 402653184 | bytes 6555648 | tf_op jit(solution)/shard_map/pallas_call | solution.py:58
Async XLA Ops:
  2.4 39.0 %all-to-all-start = ((s32[512,1,128]{2,1,0:T(1,128)}), s32[512,1,128]{2,1,0:T(1,128)S(1)}, u32[]{:S(2)}, u32[]{:S(2)}) async-start(s32[512,1,128]{2,1,0:T(1,128)} %bitcast.23), calls=%async_computation | async-start | bytes 524288 | tf_op jit(solution)/shard_map/all_to_all | solution.py:493
  24.6 19.4 %collective-permute-start.1 = (bf16[128,512]{1,0:T(8,128)(2,1)}, bf16[128,512]{1,0:T(8,128)(2,1)S(1)}, u32[]{:S(2)}, u32[]{:S(2)}) collective-permute-start(bf16[128,512]{1,0:T(8,128)(2,1)} %bitcast.19), channel_id=1, source_target_pairs={{0,64},{32,96},{64,128},{96,160},{128,192},{160,224},{192,256},{22... | collective-permute-start | bytes 393224 | tf_op jit(solution)/shard_map/ppermute | solution.py:475
  28.3 15.7 %collective-permute-start = (bf16[128,512]{1,0:T(8,128)(2,1)}, bf16[128,512]{1,0:T(8,128)(2,1)S(1)}, u32[]{:S(2)}, u32[]{:S(2)}) collective-permute-start(bf16[128,512]{1,0:T(8,128)(2,1)} %bitcast.20), channel_id=1, source_target_pairs={{0,32},{32,64},{64,96},{96,128},{128,160},{160,192},{192,224},{224... | collective-permute-start | bytes 393224 | tf_op jit(solution)/shard_map/ppermute | solution.py:475
  41.4 2.7 %copy-start = (s32[512,1,128]{2,1,0:T(1,128)}, s32[512,1,128]{2,1,0:T(1,128)S(1)}, u32[]{:S(2)}) copy-start(s32[512,1,128]{2,1,0:T(1,128)S(1)} %all-to-all-done) | copy-start | bytes 786436
  44.0 10.7 %copy-start.1 = (s32[1,16]{1,0:T(1,128)S(1)}, s32[1,16]{1,0:T(1,128)}, u32[]{:S(2)}) copy-start(s32[1,16]{1,0:T(1,128)} %refs_1_.7) | copy-start | bytes 196
  44.1 53.8 %all-to-all-start.1 = ((bf16[512,3,4,128]{3,2,1,0:T(4,128)(2,1)}), bf16[512,3,4,128]{3,2,1,0:T(4,128)(2,1)S(1)}, u32[]{:S(2)}, u32[]{:S(2)}) async-start(bf16[512,3,4,128]{3,2,1,0:T(4,128)(2,1)} %bitcast.6), calls=%async_computation.1 | async-start | bytes 3145728 | tf_op jit(solution)/shard_map/all_to_all | solution.py:493
  54.8 47.0 %copy-start.2 = (s32[2]{0:T(128)}, s32[2]{0:T(128)S(1)}, u32[]{:S(2)}) copy-start(s32[2]{0:T(128)S(1)} %pad_add_fusion.refs_0_) | copy-start | bytes 28
  101.7 52.9 %all-to-all-start.2 = ((bf16[512,3,4,128]{3,2,1,0:T(4,128)(2,1)}), bf16[512,3,4,128]{3,2,1,0:T(4,128)(2,1)S(1)}, u32[]{:S(2)}, u32[]{:S(2)}) async-start(bf16[512,3,4,128]{3,2,1,0:T(4,128)(2,1)} %bitcast.11), calls=%async_computation.2 | async-start | bytes 3145728 | tf_op jit(solution)/shard_map/all_to_all | solution.py:493
  118.1 32.6 %collective-permute-start.2 = (bf16[128,1024]{1,0:T(8,128)(2,1)}, bf16[128,1024]{1,0:T(8,128)(2,1)S(1)}, u32[]{:S(2)}, u32[]{:S(2)}) collective-permute-start(bf16[128,1024]{1,0:T(8,128)(2,1)} %get-tuple-element.45), channel_id=1, source_target_pairs={{32,0},{64,32},{96,64},{128,96},{160,128},{192,160},{224,192},{256... | collective-permute-start | bytes 786440 | tf_op jit(solution)/shard_map/ppermute | solution.py:475
  124.3 26.8 %collective-permute-start.3 = (bf16[128,1024]{1,0:T(8,128)(2,1)}, bf16[128,1024]{1,0:T(8,128)(2,1)S(1)}, u32[]{:S(2)}, u32[]{:S(2)}) collective-permute-start(bf16[128,1024]{1,0:T(8,128)(2,1)} %get-tuple-element.46), channel_id=1, source_target_pairs={{64,0},{96,32},{128,64},{160,96},{192,128},{224,160},{256,192},{28... | collective-permute-start | bytes 786440 | tf_op jit(solution)/shard_map/ppermute | solution.py:475

commit v5 on v3

--- a/solution.py
+++ b/solution.py
@@ -1,3 +1,4 @@
+import functools
 import math
 
 import jax
@@ -13,8 +14,9 @@
 CHUNKS = 4
 LANES = 128
 SLOTS = CAP + 1
-PIECES = 4
-NBANK = SLOTS * CHUNKS
+SEATS = 2 * CAP + 1
+PIECES = 2
+NBANK = SEATS * CHUNKS
 F32 = jnp.float32
 BF16 = jnp.bfloat16
 VMEM = pl.BlockSpec(memory_space=pltpu.VMEM)
@@ -154,20 +156,34 @@
     return ref.at[pl.ds(i * size, size), :]
 
 
-def serve_kernel(loaded, asks_ref, table_ref, out_ref, wide, narrow, sems):
-    owners = asks_ref.shape[0] // PIECES
+def by_chip(asks_ref, core, items):
+    count = asks_ref.shape[0] // (2 * items)
+    return jnp.concatenate(
+        [
+            asks_ref[(2 * z + core) * items : (2 * z + core + 1) * items, :]
+            for z in range(count)
+        ],
+        axis=0,
+    )
+
+
+def serve_kernel(items, loaded, asks_ref, table_ref, out_ref, wide, narrow, sems):
+    chips = asks_ref.shape[0] // 2
+    part = chips // PIECES
     rows = table_ref.shape[0]
+    asks = [by_chip(asks_ref, core, items) for core in range(2)]
     loaded()
     table = table_ref[...]
-    row_id = lax.broadcasted_iota(jnp.int32, (owners, rows), 1)
+    row_id = lax.broadcasted_iota(jnp.int32, (part, rows), 1)
     copies = []
     for i in range(PIECES):
-        base = i * owners * NBANK
-        for k in range(SLOTS):
-            asked = asks_ref[i * owners : (i + 1) * owners, k : k + 1]
+        base = i * part * NBANK
+        for seat in range(SEATS):
+            core, k = (0, CAP) if seat == 2 * CAP else divmod(seat, CAP)
+            asked = asks[core][i * part : (i + 1) * part, k : k + 1]
             hot = jnp.where(asked == row_id, 1.0, 0.0).astype(BF16)
-            spread_slot(wide, base, k, dot(hot, table))
-        narrow[base : base + owners * NBANK, :] = wide[base : base + owners * NBANK, :].astype(BF16)
+            spread_slot(wide, base, seat, dot(hot, table))
+        narrow[base : base + part * NBANK, :] = wide[base : base + part * NBANK, :].astype(BF16)
         copies.append(pltpu.make_async_copy(piece(narrow, i), piece(out_ref, i), sems.at[i]))
         copies[-1].start()
     for copy in copies:
@@ -226,6 +242,7 @@
     slope_vk_ref,
     keys_ref,
     values_ref,
+    user_ref,
 ):
     n, width = own_ref.shape
     loaded()
@@ -271,76 +288,144 @@
     gated = (attn_hat * act[:, :width].astype(F32)).astype(BF16)
     user_out = dot(gated, w_out_ref[...]) + hist_f
     user_len = jnp.sqrt(jnp.sum(user_out * user_out, axis=-1, keepdims=True) + 1e-06)
-    unit_ref[...] = user_out / user_len
+    user_unit = user_out / user_len
+    unit_ref[...] = user_unit
+    user_ref[...] = user_unit.astype(BF16)
     length_ref[...] = jnp.broadcast_to(user_len, length_ref.shape)
 
 
+def local_slots(slots, core, items):
+    bits = items.bit_length() - 1
+    owner = slots >> 1
+    local = ((owner >> (bits + 1)) << bits) + (owner & (items - 1))
+    return jnp.where(((owner >> bits) & 1) == core, local * CAP + (slots & 1), -1)
+
+
+def as_column(row):
+    n = row.shape[1]
+    lead = lax.broadcasted_iota(jnp.int32, (n, n), 0)
+    lane = lax.broadcasted_iota(jnp.int32, (n, n), 1)
+    spread = jnp.broadcast_to(row.astype(F32), (n, n))
+    return jnp.sum(jnp.where(lead == lane, spread, 0.0), axis=1, keepdims=True).astype(jnp.int32)
+
+
 def softmax_kernel(
+    items,
     loaded,
+    place_ref,
     fetched_ref,
     neg_row_ref,
-    slot_row_ref,
-    slot_col_ref,
-    unit_ref,
-    length_ref,
-    send_ref,
-    user_grad_ref,
-    narrow,
+    slots_ref,
+    users_ref,
+    den_ref,
+    pos_exp_ref,
+    neg_exp_ref,
+    neg_rows_ref,
+    pos_rows_ref,
     wide,
-    sems,
-    held,
-    held_sem,
 ):
-    n = unit_ref.shape[0]
-    owners = neg_row_ref.shape[1]
+    chips = neg_row_ref.shape[1]
+    n = users_ref.shape[0] // 2
     wide[...] = fetched_ref[...].astype(F32)
-    neg_unit, neg_len = item_norm(slot_rows(wide, 0, CAP, owners))
-    neg_bf = neg_unit.astype(BF16)
+    neg_rows = slot_rows(wide, 0, 2 * CAP, chips)
+    neg_rows_ref[...] = neg_rows
+    neg_bf = item_norm(neg_rows)[0].astype(BF16)
     loaded()
-    user_unit = unit_ref[...]
-    user_bf = user_unit.astype(BF16)
-    user_f = user_bf.astype(F32)
+    users = users_ref[...]
     neg_row = neg_row_ref[...] + 1
     exponent = jnp.zeros(neg_row.shape, F32)
     for level in range(1, 8):
         exponent = exponent + jnp.where(neg_row >= (1 << level), 1.0, 0.0)
     shift = math.log(8) + exponent * math.log(2.0)
-    neg_exp = jnp.exp(dot(user_bf, neg_bf, (1, 1)) / TAU + shift)
-    slot_col = slot_col_ref[...]
-    lane = lax.broadcasted_iota(jnp.int32, (n, owners), 1) * CAP
-    hots, rows = [], []
-    for k in range(CAP):
-        hots.append(jnp.where(slot_col == lane + k, 1.0, 0.0).astype(BF16))
-        rows.append(slot_rows(wide, 0, k, owners))
-    pos_rows = dot(jnp.concatenate(hots, axis=1), jnp.concatenate(rows, axis=0))
-    pos_unit, pos_len = item_norm(pos_rows)
+    neg_exp = jnp.exp(dot(users, neg_bf, (1, 1)) / TAU + shift)
+    neg_exp_ref[...] = neg_exp
+    slots = local_slots(slots_ref[...], place_ref[1], items)
+    lane = lax.broadcasted_iota(jnp.int32, (n, chips), 1) * CAP
+    pos_rows, here = [], []
+    for core in range(2):
+        column = as_column(slots[:, core * n : (core + 1) * n])
+        here.append(jnp.where(column >= 0, 1.0, 0.0))
+        hots = [jnp.where(column == lane + k, 1.0, 0.0).astype(BF16) for k in range(CAP)]
+        rows = [slot_rows(wide, 0, core * CAP + k, chips) for k in range(CAP)]
+        pos_rows.append(dot(jnp.concatenate(hots, axis=1), jnp.concatenate(rows, axis=0)))
+    pos_rows = jnp.concatenate(pos_rows, axis=0)
+    pos_rows_ref[...] = pos_rows.astype(BF16)
+    pos_bf = item_norm(pos_rows)[0].astype(BF16).astype(F32)
+    along = jnp.sum(users.astype(F32) * pos_bf, axis=-1, keepdims=True)
+    pos_exp = jnp.concatenate(here, axis=0) * jnp.exp(along / TAU)
+    pos_exp_ref[...] = jnp.broadcast_to(pos_exp, pos_exp_ref.shape)
+    den_ref[...] = jnp.broadcast_to(
+        pos_exp + jnp.sum(neg_exp, axis=-1, keepdims=True), den_ref.shape
+    )
+
+
+def send_kernel(
+    items,
+    loaded,
+    place_ref,
+    den_ref,
+    den_other_ref,
+    pos_exp_ref,
+    neg_exp_ref,
+    neg_rows_ref,
+    pos_rows_ref,
+    users_ref,
+    slots_ref,
+    send_ref,
+    own_part_ref,
+    other_part_ref,
+    wide,
+    narrow,
+    sems,
+    held,
+    held_sems,
+):
+    chips = neg_rows_ref.shape[0]
+    n = users_ref.shape[0] // 2
+    core_here = place_ref[1]
+    loaded()
+    users = users_ref[...]
+    user_f = users.astype(F32)
+    neg_unit, neg_len = item_norm(neg_rows_ref[...])
+    neg_bf = neg_unit.astype(BF16)
+    pos_unit, pos_len = item_norm(pos_rows_ref[...])
     pos_bf = pos_unit.astype(BF16).astype(F32)
-    pos_exp = jnp.exp(jnp.sum(user_f * pos_bf, axis=-1, keepdims=True) / TAU)
-    denominator = pos_exp + jnp.sum(neg_exp, axis=-1, keepdims=True)
-    pos_delta = pos_exp / denominator - 1.0
-    neg_prob = (neg_exp / denominator).astype(BF16)
-    unit_grad = (pos_delta * pos_bf + dot(neg_prob, neg_bf)) / TAU
-    held[...] = (
-        unit_grad - user_unit * jnp.sum(user_unit * unit_grad, axis=-1, keepdims=True)
-    ) / length_ref[:, 0:1]
-    copies = [pltpu.make_async_copy(held, user_grad_ref, held_sem)]
-    copies[0].start()
+    slots = local_slots(slots_ref[...], core_here, items)
+    here = jnp.concatenate(
+        [jnp.where(as_column(slots[:, c * n : (c + 1) * n]) >= 0, 1.0, 0.0) for c in range(2)],
+        axis=0,
+    )
+    denominator = den_ref[:, 0:1] + den_other_ref[:, 0:1]
+    pos_delta = here * (pos_exp_ref[:, 0:1] / denominator - 1.0)
+    neg_prob = (neg_exp_ref[...] / denominator).astype(BF16)
     raw_pos = pos_delta * user_f / TAU
     pos_grad = (raw_pos - pos_unit * jnp.sum(pos_unit * raw_pos, axis=-1, keepdims=True)) / pos_len
     pos_grad = pos_grad.astype(BF16)
-    slot_row = slot_row_ref[...]
-    owners = owners // PIECES
-    lead = lax.broadcasted_iota(jnp.int32, (owners, n), 0) * CAP
+    unit_part = (pos_delta * pos_bf + dot(neg_prob, neg_bf)) / TAU
+    first = core_here == 0
+    held[:n, :] = jnp.where(first, unit_part[:n], unit_part[n:])
+    held[n:, :] = jnp.where(first, unit_part[n:], unit_part[:n])
+    copies = [
+        pltpu.make_async_copy(held.at[pl.ds(n, n), :], other_part_ref, held_sems.at[0]),
+        pltpu.make_async_copy(held.at[pl.ds(0, n), :], own_part_ref, held_sems.at[1]),
+    ]
+    for copy in copies:
+        copy.start()
+    part = chips // PIECES
+    lead = lax.broadcasted_iota(jnp.int32, (part, n), 0) * CAP
     for i in range(PIECES):
-        base = i * owners * NBANK
-        for k in range(CAP):
-            hot = jnp.where(slot_row == lead + (i * owners * CAP + k), 1.0, 0.0).astype(BF16)
-            spread_slot(wide, base, k, dot(hot, pos_grad))
-        own = slice(i * owners, (i + 1) * owners)
-        raw_neg = dot(neg_prob[:, own], user_bf, (0, 0)) / TAU
+        base = i * part * NBANK
+        for core in range(2):
+            row = slots[:, core * n : (core + 1) * n]
+            for k in range(CAP):
+                hot = jnp.where(row == lead + (i * part * CAP + k), 1.0, 0.0).astype(BF16)
+                placed = dot(hot, pos_grad[core * n : (core + 1) * n])
+                spread_slot(wide, base, core * CAP + k, placed)
+        own = slice(i * part, (i + 1) * part)
+        raw_neg = dot(neg_prob[:, own], users, (0, 0)) / TAU
         along = jnp.sum(neg_unit[own] * raw_neg, axis=-1, keepdims=True)
-        spread_slot(wide, base, CAP, (raw_neg - neg_unit[own] * along) / neg_len[own])
-        narrow[base : base + owners * NBANK, :] = wide[base : base + owners * NBANK, :].astype(BF16)
+        spread_slot(wide, base, 2 * CAP, (raw_neg - neg_unit[own] * along) / neg_len[own])
+        narrow[base : base + part * NBANK, :] = wide[base : base + part * NBANK, :].astype(BF16)
         copies.append(pltpu.make_async_copy(piece(narrow, i), piece(send_ref, i), sems.at[i]))
         copies[-1].start()
     for copy in copies:
@@ -351,7 +436,10 @@
     loaded,
     place_ref,
     sess_ref,
-    user_grad_ref,
+    own_part_ref,
+    other_part_ref,
+    unit_ref,
+    length_ref,
     w_out_ref,
     gate_ref,
     query_ref,
@@ -365,11 +453,18 @@
     near_ref,
     far_ref,
     in_part_ref,
+    user_grad_ref,
 ):
     n, width = hat_ref.shape
     loaded()
     attn_hat = hat_ref[...]
-    gated_grad = dot(user_grad_ref[...].astype(BF16), w_out_ref[...], (1, 1))
+    user_unit = unit_ref[...]
+    unit_grad = own_part_ref[...] + other_part_ref[...]
+    user_grad = (
+        unit_grad - user_unit * jnp.sum(user_unit * unit_grad, axis=-1, keepdims=True)
+    ) / length_ref[:, 0:1]
+    user_grad_ref[...] = user_grad
+    gated_grad = dot(user_grad.astype(BF16), w_out_ref[...], (1, 1))
     hat_grad = gated_grad * gate_ref[...].astype(F32)
     upstream = norm_back(hat_grad, attn_hat, scale_ref[:, 0:1]).astype(BF16)
     scale = window_scale(place_ref, sess_ref, n)
@@ -407,6 +502,7 @@
 
 
 def last_kernel(
+    items,
     loaded,
     returned_ref,
     near_ref,
@@ -426,21 +522,18 @@
     held_sem,
 ):
     width = hist_ref.shape[1]
-    owners = asks_ref.shape[0] // 2
+    chips = asks_ref.shape[0] // 2
     rows = table_grad_ref.shape[0]
     wide[...] = returned_ref[...].astype(F32)
     loaded(1)
-    asks = jnp.transpose(asks_ref[...].astype(F32))
-    row_id = lax.broadcasted_iota(jnp.int32, (rows, owners), 0).astype(F32)
-    total = None
-    for i in range(2):
-        hots, parts = [], []
-        for k in range(SLOTS):
-            asked = asks[k : k + 1, i * owners : (i + 1) * owners]
-            hots.append(jnp.where(asked == row_id, 1.0, 0.0).astype(BF16))
-            parts.append(slot_rows(wide, i * owners * NBANK, k, owners))
-        part = dot(jnp.concatenate(hots, axis=1), jnp.concatenate(parts, axis=0))
-        total = part if total is None else total + part
+    asks = [jnp.transpose(by_chip(asks_ref, core, items).astype(F32)) for core in range(2)]
+    row_id = lax.broadcasted_iota(jnp.int32, (rows, chips), 0).astype(F32)
+    hots, parts = [], []
+    for seat in range(SEATS):
+        core, k = (0, CAP) if seat == 2 * CAP else divmod(seat, CAP)
+        hots.append(jnp.where(asks[core][k : k + 1] == row_id, 1.0, 0.0).astype(BF16))
+        parts.append(slot_rows(wide, 0, seat, chips))
+    total = dot(jnp.concatenate(hots, axis=1), jnp.concatenate(parts, axis=0))
     held[...] = total.astype(BF16)
     copy = pltpu.make_async_copy(held, table_grad_ref, held_sem)
     copy.start()
@@ -458,28 +551,40 @@
     copy.wait()
 
 
-def passed_along(shard, axis, by):
-    count = lax.axis_size(axis)
+def passed_along(shard, by):
+    axes = ("z", "core")
+    count = lax.axis_size(axes)
     pairs = [(i, i + by) for i in range(count) if 0 <= i + by < count]
-    return lax.ppermute(shard, axis, pairs)
+    return lax.ppermute(shard, axes, pairs)
+
+
+def swapped(shard):
+    return lax.ppermute(shard, "core", [(0, 1), (1, 0)])
 
 
 def on_device(history, ln_gain, w_in, w_out, item_table, sessions, pos_owner, pos_row, neg_rows):
     n, width = history.shape[1:]
     items = lax.axis_size("items")
-    hists = lax.axis_size("hist")
-    owners = hists * items
+    chips = lax.axis_size("z") * items
+    owners = 2 * chips
     rows = item_table.shape[0]
-    axes = ("hist", "items")
-    place = jnp.stack([lax.axis_index("hist"), lax.axis_index("items")]).astype(jnp.int32)
+    core = lax.axis_index("core")
+    place = jnp.stack([2 * lax.axis_index("z") + core, core]).astype(jnp.int32)
     own = history[0]
     gain = ln_gain.reshape(1, width)
     neg_row = neg_rows.reshape(1, owners)
 
-    def exchange(shard, chunk):
+    def exchange(shard, axes, chunk):
         shape = shard.shape
-        split = shard.reshape((owners,) + chunk)
+        split = shard.reshape((-1,) + chunk)
         return lax.all_to_all(split, axes, split_axis=0, concat_axis=0, tiled=True).reshape(shape)
+
+    def by_core(mine, other, axis):
+        return jnp.where(
+            core == 0,
+            jnp.concatenate([mine, other], axis=axis),
+            jnp.concatenate([other, mine], axis=axis),
+        )
 
     ask, slot_row, slot_col = call(
         ask_kernel,
@@ -488,11 +593,11 @@
         (pos_owner.reshape(1, n), pos_row, neg_row),
         2 * CAP * owners * n * LANES,
     )
-    asks = exchange(ask, (1, LANES))
-    near = passed_along(own, "hist", 1)
-    far = passed_along(own, "hist", 2)
-
-    big = owners * NBANK
+    asks = exchange(ask, ("z", "core", "items"), (1, LANES))
+    near = passed_along(own, 1)
+    far = passed_along(own, 2)
+
+    big = chips * NBANK
     staging = [
         pltpu.VMEM((big, LANES), BF16),
         pltpu.VMEM((big, LANES), F32),
@@ -500,19 +605,19 @@
     ]
     outward = [staging[1], staging[0], staging[2]]
     (served,) = call(
-        serve_kernel,
+        functools.partial(serve_kernel, items),
         [shaped((big, LANES), BF16)],
         [VMEM, None],
         (asks, item_table),
-        2 * SLOTS * owners * rows * width,
+        2 * SEATS * chips * rows * width,
         outward,
         mib=40,
         out_specs=(HBM,),
     )
     served, near, far = lax.optimization_barrier((served, near, far))
-    fetched = exchange(served, (SLOTS, CHUNKS, LANES))
-
-    unit, length, attn_hat, scale_a, gate, query, slope_gq, slope_vk, keys, values = call(
+    fetched = exchange(served, ("z", "items"), (SEATS, CHUNKS, LANES))
+
+    unit, length, attn_hat, scale_a, gate, query, slope_gq, slope_vk, keys, values, user = call(
         forward_kernel,
         [
             pltpu.HBM((n, width), F32),
@@ -525,6 +630,7 @@
             pltpu.HBM((n, 2 * width), F32),
             pltpu.HBM((3 * n, width), BF16),
             pltpu.HBM((3 * n, width), BF16),
+            pltpu.HBM((n, width), BF16),
         ],
         [SMEM, SMEM, VMEM, VMEM] + [None] * 4,
         (place, sessions, far, near, own, gain, w_in, w_out),
@@ -532,31 +638,55 @@
         mib=40,
     )
 
-    send, user_grad = call(
-        softmax_kernel,
-        [shaped((big, LANES), BF16), pltpu.HBM((n, width), F32)],
-        [VMEM] + [None] * 5,
-        (fetched, neg_row, slot_row, slot_col, unit, length),
-        2 * n * width * owners * 7,
-        staging + [pltpu.VMEM((n, width), F32), pltpu.SemaphoreType.DMA(())],
+    users = by_core(user, swapped(user), 0)
+    slots = by_core(slot_row, swapped(slot_row), 1)
+    neg_here = lax.dynamic_index_in_dim(
+        neg_rows.reshape(chips // items, 2, items), core, axis=1, keepdims=False
+    ).reshape(1, chips)
+    den, pos_exp, neg_exp, neg_kept, pos_kept = call(
+        functools.partial(softmax_kernel, items),
+        [
+            pltpu.HBM((2 * n, LANES), F32),
+            pltpu.HBM((2 * n, LANES), F32),
+            pltpu.HBM((2 * n, chips), F32),
+            pltpu.HBM((chips, width), BF16),
+            pltpu.HBM((2 * n, width), BF16),
+        ],
+        [SMEM, VMEM] + [None] * 3,
+        (place, fetched, neg_here, slots, users),
+        2 * n * width * owners * 3,
+        [staging[1]],
         mib=40,
-        out_specs=(HBM, HBM),
-    )
-    returned = exchange(send, (SLOTS, CHUNKS, LANES))
-
-    own_grad, near_grad, far_grad, in_part = call(
+    )
+    send, own_part, other_part = call(
+        functools.partial(send_kernel, items),
+        [shaped((big, LANES), BF16), pltpu.HBM((n, width), F32), pltpu.HBM((n, width), F32)],
+        [SMEM, None, VMEM] + [None] * 6,
+        (place, den, swapped(den), pos_exp, neg_exp, neg_kept, pos_kept, users, slots),
+        2 * n * width * owners * 4,
+        outward + [pltpu.VMEM((2 * n, width), F32), pltpu.SemaphoreType.DMA((2,))],
+        mib=40,
+        out_specs=(HBM, HBM, HBM),
+    )
+    returned = exchange(send, ("z", "items"), (SEATS, CHUNKS, LANES))
+
+    own_grad, near_grad, far_grad, in_part, user_grad = call(
         heads_back_kernel,
         [
             shaped((n, 2 * width), F32),
             shaped((n, 2 * width), BF16),
             shaped((n, 2 * width), BF16),
             shaped((n, width), F32),
+            shaped((n, width), F32),
         ],
-        [SMEM, SMEM] + [None] * 10,
+        [SMEM, SMEM] + [None] * 13,
         (
             place,
             sessions,
-            user_grad,
+            own_part,
+            swapped(other_part),
+            unit,
+            length,
             w_out,
             gate,
             query,
@@ -569,10 +699,10 @@
         ),
         2 * n * width * width * 12,
     )
-    near_back = passed_along(near_grad, "hist", -1)
-    far_back = passed_along(far_grad, "hist", -2)
+    near_back = passed_along(near_grad, -1)
+    far_back = passed_along(far_grad, -2)
     table_grad, history_grad = call(
-        last_kernel,
+        functools.partial(last_kernel, items),
         [shaped((rows, width), BF16), shaped((n, width), BF16)],
         [VMEM] * 3 + [None] * 8,
         (
@@ -588,7 +718,7 @@
             own,
             user_grad,
         ),
-        2 * SLOTS * owners * rows * width,
+        2 * SEATS * chips * rows * width,
         [staging[1], pltpu.VMEM((rows, width), BF16), pltpu.SemaphoreType.DMA(())],
         mib=40,
         out_specs=(HBM, VMEM),
@@ -597,20 +727,24 @@
 
 
 def solution(mesh):
+    hist, items = mesh.shape["hist"], mesh.shape["items"]
+    split = jax.sharding.Mesh(
+        mesh.devices.reshape(hist // 2, 2, items), ("z", "core", "items")
+    )
     return jax.shard_map(
         on_device,
-        mesh=mesh,
+        mesh=split,
         in_specs=(
-            P("items", "hist", None),
+            P("items", ("z", "core"), None),
             P(),
             P(),
             P(),
-            P(("hist", "items"), None),
+            P(("z", "core", "items"), None),
             P("items", None),
-            P("items", "hist", None),
-            P("items", "hist"),
+            P("items", ("z", "core"), None),
+            P("items", ("z", "core")),
             P("items", None, None),
         ),
-        out_specs=(P("items", "hist", None), P(("hist", "items"), None)),
+        out_specs=(P("items", ("z", "core"), None), P(("z", "core", "items"), None)),
         check_vma=False,
     )

time: 159 us -> 153 us (0.962)
  waiting for transfers between devices: 76 us -> 49.4 us
  starting transfers between devices: 57.7 us -> 68.8 us
  Pallas kernels: 24.1 us -> 28.2 us
  other arithmetic: 0.08 us -> 3.01 us
  local copies, waits for them, and re-layouts: 0.01 us -> 1.98 us
    all_to_all x3, waiting for transfers between devices: 50.2 us -> 27.3 us  [exchange(): lax.all_to_all(split, axes, split_axis=0, concat_axis=0, tiled=True)]
    ppermute x4 -> x8, starting transfers between devices: 15.3 us -> 27.3 us  [the longest x4 15.9 us: swapped(): return lax.ppermute(shard, 'core', [(0, 1), (1, 0)])]
    pallas_call x6 -> x7, Pallas kernels: 24.1 us -> 28.2 us  [call(): pl.pallas_call(body, out_shape=tuple(outs), in_specs=[HBM if spec is None...]
    ppermute x4 -> x8, waiting for transfers between devices: 25.8 us -> 22.1 us  [the longest x4 19.6 us: passed_along(): return lax.ppermute(shard, axes, pairs)]
    select_n x0 -> x2, other arithmetic: none -> 2.27 us  [by_core(): jnp.where(core == 0, jnp.concatenate([mine, other], axis=axis), jnp.conca...]
  transfers between devices with their start and end apart: 7 -> 11, of which waited for: 5 -> 8; matrix products, arithmetic and copies ran while one was open for 0% -> 3% of each run, Pallas kernels for 9% -> 10%
where the time goes in v5:
time: 153 us; the launch traced here: 152 us
  starting transfers between devices  68.8 us (45%)
  waiting for transfers between devices  49.4 us (32%)
  Pallas kernels  28.2 us (18%)
  other arithmetic  3.01 us (2%)
  local copies, waits for them, and re-layouts  1.98 us (1%)
    all_to_all x3, starting transfers between devices, exchange(): lax.all_to_all(split, axes, split_axis=0, concat_axis=0, tiled=True)  41.5 us
    pallas_call x7, Pallas kernels, call(): pl.pallas_call(body, out_shape=tuple(outs), in_specs=[HBM if spec is None...  28.2 us
    all_to_all x3, waiting for transfers between devices, exchange(): lax.all_to_all(split, axes, split_axis=0, concat_axis=0, tiled=True)  27.3 us
    ppermute x4, waiting for transfers between devices, passed_along(): return lax.ppermute(shard, axes, pairs)  19.6 us
    ppermute x4, starting transfers between devices, swapped(): return lax.ppermute(shard, 'core', [(0, 1), (1, 0)])  15.9 us
    ppermute x4, starting transfers between devices, passed_along(): return lax.ppermute(shard, axes, pairs)  11.4 us
  transfers between devices with their start and end apart: 11, of which 8 were waited for; matrix products, arithmetic and copies ran while one was open for 3% of the time, Pallas kernels for 10%

profile of v5, /device:TPU:1, one launch (start us, length us, event | category | flops | bytes accessed | tf_op | source)
XLA Modules:
  0.0 152.4 jit_solution(13551455722251442665)
XLA Ops:
  0.6 1.7 %shard_map.104 = (s32[512,128]{1,0:T(8,128)}, s32[1,128]{1,0:T(1,128)}, s32[128,1]{1,0:T(8,128)}) custom-call(s32[1,128]{1,0:T(1,128)} %bitcast.33, s32[1,128]{1,0:T(1,128)} %refs_1_.4, s32[1,512]{1,0:T(1,128)} %bitcast.31), custom_call_target="tpu_custom_call" | custom-call | flops 33554432 | bytes 266240 | tf_op jit(solution)/shard_map/pallas_call | solution.py:59
  2.4 22.2 %all-to-all-start = ((s32[512,1,128]{2,1,0:T(1,128)}), s32[512,1,128]{2,1,0:T(1,128)S(1)}, u32[]{:S(2)}, u32[]{:S(2)}) async-start(s32[512,1,128]{2,1,0:T(1,128)} %bitcast.27), calls=%async_computation | async-start | bytes 524288 | tf_op jit(solution)/shard_map/all_to_all | solution.py:580
  24.5 3.7 %collective-permute-start.1 = (bf16[128,512]{1,0:T(8,128)(2,1)}, bf16[128,512]{1,0:T(8,128)(2,1)S(1)}, u32[]{:S(2)}, u32[]{:S(2)}) collective-permute-start(bf16[128,512]{1,0:T(8,128)(2,1)} %bitcast.23), channel_id=1, source_target_pairs={{0,64},{32,96},{64,128},{96,160},{128,192},{160,224},{192,256},{22... | collective-permute-start | bytes 393224 | tf_op jit(solution)/shard_map/ppermute | solution.py:558
  28.2 4.2 %collective-permute-start = (bf16[128,512]{1,0:T(8,128)(2,1)}, bf16[128,512]{1,0:T(8,128)(2,1)S(1)}, u32[]{:S(2)}, u32[]{:S(2)}) collective-permute-start(bf16[128,512]{1,0:T(8,128)(2,1)} %bitcast.24), channel_id=1, source_target_pairs={{0,32},{32,64},{64,96},{96,128},{128,160},{160,192},{192,224},{224... | collective-permute-start | bytes 393224 | tf_op jit(solution)/shard_map/ppermute | solution.py:558
  32.4 8.9 %all-to-all-done = s32[512,1,128]{2,1,0:T(1,128)S(1)} async-done(((s32[512,1,128]{2,1,0:T(1,128)}), s32[512,1,128]{2,1,0:T(1,128)S(1)}, u32[]{:S(2)}, u32[]{:S(2)}) %all-to-all-start) | async-done | bytes 262176 | tf_op jit(solution)/shard_map/all_to_all | solution.py:580
  41.3 0.0 copy-start
  41.3 2.6 %shard_map.105 = bf16[5120,128]{1,0:T(8,128)(2,1)} custom-call(s32[512,128]{1,0:T(8,128)S(1)} %bitcast.21, bf16[256,512]{1,0:T(8,128)(2,1)} %refs_1_.5), custom_call_target="tpu_custom_call" | custom-call | flops 335544320 | bytes 1835008 | tf_op jit(solution)/shard_map/pallas_call | solution.py:59
  43.9 0.0 collective-permute-done.1.refs_2_
  43.9 0.0 collective-permute-done.refs_3_
  43.9 0.0 copy-start.5
  43.9 0.0 copy-start.4
  43.9 0.0 copy-start.2
  44.0 0.0 copy-done
  44.0 10.0 %all-to-all-start.1 = ((bf16[256,5,4,128]{3,2,1,0:T(4,128)(2,1)}), bf16[256,5,4,128]{3,2,1,0:T(4,128)(2,1)S(1)}, u32[]{:S(2)}, u32[]{:S(2)}) async-start(bf16[256,5,4,128]{3,2,1,0:T(4,128)(2,1)} %bitcast.8), calls=%async_computation.1 | async-start | bytes 2621440 | tf_op jit(solution)/shard_map/all_to_all | solution.py:580
  54.0 0.0 copy-done.5
  54.0 4.7 %collective-permute-start.2 = (s32[1,128]{1,0:T(1,128)S(1)}, s32[1,128]{1,0:T(1,128)S(1)}, u32[]{:S(2)}, u32[]{:S(2)}) collective-permute-start(s32[1,128]{1,0:T(1,128)S(1)} %copy-done.5), channel_id=1, source_target_pairs={{0,32},{32,0},{1,33},{33,1},{2,34},{34,2},{3,35},{35,3},{4,36},{36... | collective-permute-start | bytes 1544 | tf_op jit(solution)/shard_map/ppermute | solution.py:562
  58.7 0.5 broadcast.11
  59.2 0.0 copy-done.4
  59.2 0.7 reduce.3
  59.9 0.1 reshape.96
  60.0 0.1 pad_add_fusion.refs_0_
  60.1 0.0 copy-done.2
  60.1 5.9 %shard_map.106 = (f32[128,512]{1,0:T(8,128)}, f32[128,128]{1,0:T(8,128)}, f32[128,512]{1,0:T(8,128)}, f32[128,128]{1,0:T(8,128)}, bf16[128,512]{1,0:T(8,128)(2,1...) custom-call(s32[2]{0:T(128)S(1)} %pad_add_fusion.refs_0_, ...), custom_call_target="tpu_custom_call" | custom-call | flops 805306368 | bytes 5900360 | tf_op jit(solution)/shard_map/pallas_call | solution.py:59
  65.9 1.9 %collective-permute-start.3 = (bf16[128,512]{1,0:T(8,128)(2,1)}, bf16[128,512]{1,0:T(8,128)(2,1)S(1)}, u32[]{:S(2)}, u32[]{:S(2)}) collective-permute-start(bf16[128,512]{1,0:T(8,128)(2,1)} %get-tuple-element.38), channel_id=1, source_target_pairs={{0,32},{32,0},{1,33},{33,1},{2,34},{34,2},{3,35},{35,3},{4,36},{36... | collective-permute-start | bytes 393224 | tf_op jit(solution)/shard_map/ppermute | solution.py:562
  67.9 0.6 reshape.97.refs_2_
  68.5 0.0 collective-permute-done.2
  68.5 0.5 broadcast_select_fusion.refs_3_.refs_8_
  69.0 0.4 collective-permute-done.3
  69.4 1.8 %maximum_select_fusion.refs_4_.refs_7_ = bf16[256,512]{1,0:T(8,128)(2,1)} fusion(bf16[128,512]{1,0:T(8,128)(2,1)S(1)} %collective-permute-done.3, bf16[128,512]{1,0:T(8,128)(2,1)} %get-tuple-element.38, pred[]{:T(512)S(6)} %eq.4), kind=kLoop, calls=%fused_computation | loop fusion | flops 1179648 | bytes 524289 | tf_op jit(solution)/shard_map/jit(_where)/select_n | solution.py:583
  71.1 16.5 %all-to-all-done.1 = bf16[256,5,4,128]{3,2,1,0:T(4,128)(2,1)S(1)} async-done(((bf16[256,5,4,128]{3,2,1,0:T(4,128)(2,1)}), bf16[256,5,4,128]{3,2,1,0:T(4,128)(2,1)S(1)}, u32[]{:S(2)}, u32[]{:S(2)}) %all-to-all-start.1) | async-done | bytes 1310752 | tf_op jit(solution)/shard_map/all_to_all | solution.py:580
  87.6 3.5 %shard_map.107 = (f32[256,128]{1,0:T(8,128)}, f32[256,128]{1,0:T(8,128)}, f32[256,256]{1,0:T(8,128)}, bf16[256,512]{1,0:T(8,128)(2,1)}, bf16[256,512]{1,0:T(8,128)(2,1)}) custom-call(s32[2]{0:T(128)S(1)} %pad_add_fusion.refs_0_, bf16[5120,128]{1,0:T(8,128)(2,1)S(1)} %bitcast.19, s32[1,256]{1,0:T(1,128)} %reshape.97.refs_2_, ...), custom_call_target="tpu_custom_call" | custom-call | flops 201326592 | bytes 2623496 | tf_op jit(solution)/shard_map/pallas_call | solution.py:59
  91.1 7.0 %collective-permute-start.4 = (f32[256,128]{1,0:T(8,128)}, f32[256,128]{1,0:T(8,128)S(1)}, u32[]{:S(2)}, u32[]{:S(2)}) collective-permute-start(f32[256,128]{1,0:T(8,128)} %get-tuple-element.39.refs_1_), channel_id=1, source_target_pairs={{0,32},{32,0},{1,33},{33,1},{2,34},{34,2},{3,35},{35,3},{4,36},{36... | collective-permute-start | bytes 393224 | tf_op jit(solution)/shard_map/ppermute | solution.py:562
  98.1 1.0 collective-permute-done.4.refs_2_
  99.1 0.0 copy-done.1
  99.1 4.2 %shard_map.108 = (bf16[5120,128]{1,0:T(8,128)(2,1)}, f32[128,512]{1,0:T(8,128)}, f32[128,512]{1,0:T(8,128)}) custom-call(s32[2]{0:T(128)S(1)} %pad_add_fusion.refs_0_, f32[256,128]{1,0:T(8,128)} %get-tuple-element.39.refs_1_, f32[256,128]{1,0:T(8,128)S(1)} %collective-permute-done.4.refs_2_, f32[256,128]{1,0:T(8,128)} %get-tuple-element.40.refs_3_, ...), custom_call_target="tpu_custom_call" | custom-call | flops 268435456 | bytes 3277832 | tf_op jit(solution)/shard_map/pallas_call | solution.py:59
  103.2 0.0 copy-start.6
  103.2 9.3 %all-to-all-start.2 = ((bf16[256,5,4,128]{3,2,1,0:T(4,128)(2,1)}), bf16[256,5,4,128]{3,2,1,0:T(4,128)(2,1)S(1)}, u32[]{:S(2)}, u32[]{:S(2)}) async-start(bf16[256,5,4,128]{3,2,1,0:T(4,128)(2,1)} %bitcast.11), calls=%async_computation.2 | async-start | bytes 2621440 | tf_op jit(solution)/shard_map/all_to_all | solution.py:580
  112.6 0.0 copy-done.6
  112.6 2.3 %collective-permute-start.5 = (f32[128,512]{1,0:T(8,128)S(1)}, f32[128,512]{1,0:T(8,128)S(1)}, u32[]{:S(2)}, u32[]{:S(2)}) collective-permute-start(f32[128,512]{1,0:T(8,128)S(1)} %copy-done.6), channel_id=1, source_target_pairs={{0,32},{32,0},{1,33},{33,1},{2,34},{34,2},{3,35},{35,3},{4,36},{36... | collective-permute-start | bytes 786440 | tf_op jit(solution)/shard_map/ppermute | solution.py:562
  114.8 1.2 collective-permute-done.5.refs_3_
  116.0 0.7 copy-done.3
  116.7 7.0 %shard_map.109 = (f32[128,1024]{1,0:T(8,128)}, bf16[128,1024]{1,0:T(8,128)(2,1)}, bf16[128,1024]{1,0:T(8,128)(2,1)}, f32[128,512]{1,0:T(8,128)}, f32[128,512]{1,0:T(8,128)}) custom-call(s32[2]{0:T(128)} %copy-done.1, s32[1,16]{1,0:T(1,128)} %refs_1_.7, f32[128,512]{1,0:T(8,128)} %get-tuple-element.45.refs_2_, f32[128,512]{1,0:T(8,128)} %copy-done.3, ...), custom_call_target="tpu_custom_call" | custom-call | flops 805306368 | bytes 6946888 | tf_op jit(solution)/shard_map/pallas_call | solution.py:59
  123.7 2.3 %collective-permute-start.6 = (bf16[128,1024]{1,0:T(8,128)(2,1)}, bf16[128,1024]{1,0:T(8,128)(2,1)S(1)}, u32[]{:S(2)}, u32[]{:S(2)}) collective-permute-start(bf16[128,1024]{1,0:T(8,128)(2,1)} %get-tuple-element.56), channel_id=1, source_target_pairs={{32,0},{64,32},{96,64},{128,96},{160,128},{192,160},{224,192},{256... | collective-permute-start | bytes 786440 | tf_op jit(solution)/shard_map/ppermute | solution.py:558
  126.0 1.3 collective-permute-start.7
  127.3 19.1 %collective-permute-done.6.refs_1_ = bf16[128,1024]{1,0:T(8,128)(2,1)S(1)} collective-permute-done((bf16[128,1024]{1,0:T(8,128)(2,1)}, bf16[128,1024]{1,0:T(8,128)(2,1)S(1)}, u32[]{:S(2)}, u32[]{:S(2)}) %collective-permute-start.6) | collective-permute-done | bytes 262176 | tf_op jit(solution)/shard_map/ppermute | solution.py:558
  146.4 0.4 collective-permute-done.7.refs_2_
  146.9 2.0 %all-to-all-done.2 = bf16[256,5,4,128]{3,2,1,0:T(4,128)(2,1)S(1)} async-done(((bf16[256,5,4,128]{3,2,1,0:T(4,128)(2,1)}), bf16[256,5,4,128]{3,2,1,0:T(4,128)(2,1)S(1)}, u32[]{:S(2)}, u32[]{:S(2)}) %all-to-all-start.2) | async-done | bytes 1310752 | tf_op jit(solution)/shard_map/all_to_all | solution.py:580
  148.8 3.4 %shard_map.110 = (bf16[256,512]{1,0:T(8,128)(2,1)}, bf16[128,512]{1,0:T(8,128)(2,1)}) custom-call(bf16[5120,128]{1,0:T(8,128)(2,1)S(1)} %bitcast.20, bf16[128,1024]{1,0:T(8,128)(2,1)S(1)} %collective-permute-done.6.refs_1_, bf16[128,1024]{1,0:T(8,128)(2,1)S(1)} %collective-permute-done.7.refs_2_, s32[512,128]{1,0:T(8,128)} %bitcast.22, ...), custom_call_target="tpu_custom_call" | custom-call | flops 335544320 | bytes 6293504 | tf_op jit(solution)/shard_map/pallas_call | solution.py:59
  (3 shorter events, 0.0 us)
Async XLA Ops:
  2.4 38.9 %all-to-all-start = ((s32[512,1,128]{2,1,0:T(1,128)}), s32[512,1,128]{2,1,0:T(1,128)S(1)}, u32[]{:S(2)}, u32[]{:S(2)}) async-start(s32[512,1,128]{2,1,0:T(1,128)} %bitcast.27), calls=%async_computation | async-start | bytes 524288 | tf_op jit(solution)/shard_map/all_to_all | solution.py:580
  24.5 19.4 %collective-permute-start.1 = (bf16[128,512]{1,0:T(8,128)(2,1)}, bf16[128,512]{1,0:T(8,128)(2,1)S(1)}, u32[]{:S(2)}, u32[]{:S(2)}) collective-permute-start(bf16[128,512]{1,0:T(8,128)(2,1)} %bitcast.23), channel_id=1, source_target_pairs={{0,64},{32,96},{64,128},{96,160},{128,192},{160,224},{192,256},{22... | collective-permute-start | bytes 393224 | tf_op jit(solution)/shard_map/ppermute | solution.py:558
  28.2 15.7 %collective-permute-start = (bf16[128,512]{1,0:T(8,128)(2,1)}, bf16[128,512]{1,0:T(8,128)(2,1)S(1)}, u32[]{:S(2)}, u32[]{:S(2)}) collective-permute-start(bf16[128,512]{1,0:T(8,128)(2,1)} %bitcast.24), channel_id=1, source_target_pairs={{0,32},{32,64},{64,96},{96,128},{128,160},{160,192},{192,224},{224... | collective-permute-start | bytes 393224 | tf_op jit(solution)/shard_map/ppermute | solution.py:558
  41.3 2.7 %copy-start = (s32[512,1,128]{2,1,0:T(1,128)}, s32[512,1,128]{2,1,0:T(1,128)S(1)}, u32[]{:S(2)}) copy-start(s32[512,1,128]{2,1,0:T(1,128)S(1)} %all-to-all-done) | copy-start | bytes 786436
  43.9 10.1 %copy-start.5 = (s32[1,128]{1,0:T(1,128)S(1)}, s32[1,128]{1,0:T(1,128)}, u32[]{:S(2)}) copy-start(s32[1,128]{1,0:T(1,128)} %get-tuple-element.35) | copy-start | bytes 1540
  43.9 15.3 %copy-start.4 = (s32[1,512,1]{1,2,0:T(1,128)S(1)}, s32[1,512,1]{1,2,0:T(1,128)}, u32[]{:S(2)}) copy-start(s32[1,512,1]{1,2,0:T(1,128)} %param.17) | copy-start | bytes 6148
  43.9 16.1 %copy-start.2 = (s32[1,16]{1,0:T(1,128)S(1)}, s32[1,16]{1,0:T(1,128)}, u32[]{:S(2)}) copy-start(s32[1,16]{1,0:T(1,128)} %refs_1_.7) | copy-start | bytes 196
  44.0 43.6 %all-to-all-start.1 = ((bf16[256,5,4,128]{3,2,1,0:T(4,128)(2,1)}), bf16[256,5,4,128]{3,2,1,0:T(4,128)(2,1)S(1)}, u32[]{:S(2)}, u32[]{:S(2)}) async-start(bf16[256,5,4,128]{3,2,1,0:T(4,128)(2,1)} %bitcast.8), calls=%async_computation.1 | async-start | bytes 2621440 | tf_op jit(solution)/shard_map/all_to_all | solution.py:580
  54.0 14.5 %collective-permute-start.2 = (s32[1,128]{1,0:T(1,128)S(1)}, s32[1,128]{1,0:T(1,128)S(1)}, u32[]{:S(2)}, u32[]{:S(2)}) collective-permute-start(s32[1,128]{1,0:T(1,128)S(1)} %copy-done.5), channel_id=1, source_target_pairs={{0,32},{32,0},{1,33},{33,1},{2,34},{34,2},{3,35},{35,3},{4,36},{36... | collective-permute-start | bytes 1544 | tf_op jit(solution)/shard_map/ppermute | solution.py:562
  60.1 39.0 %copy-start.1 = (s32[2]{0:T(128)}, s32[2]{0:T(128)S(1)}, u32[]{:S(2)}) copy-start(s32[2]{0:T(128)S(1)} %pad_add_fusion.refs_0_) | copy-start | bytes 28
  65.9 3.5 %collective-permute-start.3 = (bf16[128,512]{1,0:T(8,128)(2,1)}, bf16[128,512]{1,0:T(8,128)(2,1)S(1)}, u32[]{:S(2)}, u32[]{:S(2)}) collective-permute-start(bf16[128,512]{1,0:T(8,128)(2,1)} %get-tuple-element.38), channel_id=1, source_target_pairs={{0,32},{32,0},{1,33},{33,1},{2,34},{34,2},{3,35},{35,3},{4,36},{36... | collective-permute-start | bytes 393224 | tf_op jit(solution)/shard_map/ppermute | solution.py:562
  91.1 8.0 %collective-permute-start.4 = (f32[256,128]{1,0:T(8,128)}, f32[256,128]{1,0:T(8,128)S(1)}, u32[]{:S(2)}, u32[]{:S(2)}) collective-permute-start(f32[256,128]{1,0:T(8,128)} %get-tuple-element.39.refs_1_), channel_id=1, source_target_pairs={{0,32},{32,0},{1,33},{33,1},{2,34},{34,2},{3,35},{35,3},{4,36},{36... | collective-permute-start | bytes 393224 | tf_op jit(solution)/shard_map/ppermute | solution.py:562
  103.2 9.3 %copy-start.6 = (f32[128,512]{1,0:T(8,128)S(1)}, f32[128,512]{1,0:T(8,128)}, u32[]{:S(2)}) copy-start(f32[128,512]{1,0:T(8,128)} %get-tuple-element.46) | copy-start | bytes 786436
  103.2 45.6 %all-to-all-start.2 = ((bf16[256,5,4,128]{3,2,1,0:T(4,128)(2,1)}), bf16[256,5,4,128]{3,2,1,0:T(4,128)(2,1)S(1)}, u32[]{:S(2)}, u32[]{:S(2)}) async-start(bf16[256,5,4,128]{3,2,1,0:T(4,128)(2,1)} %bitcast.11), calls=%async_computation.2 | async-start | bytes 2621440 | tf_op jit(solution)/shard_map/all_to_all | solution.py:580
  112.6 3.4 %collective-permute-start.5 = (f32[128,512]{1,0:T(8,128)S(1)}, f32[128,512]{1,0:T(8,128)S(1)}, u32[]{:S(2)}, u32[]{:S(2)}) collective-permute-start(f32[128,512]{1,0:T(8,128)S(1)} %copy-done.6), channel_id=1, source_target_pairs={{0,32},{32,0},{1,33},{33,1},{2,34},{34,2},{3,35},{35,3},{4,36},{36... | collective-permute-start | bytes 786440 | tf_op jit(solution)/shard_map/ppermute | solution.py:562
  116.0 0.7 copy-start.3
  123.7 22.7 %collective-permute-start.6 = (bf16[128,1024]{1,0:T(8,128)(2,1)}, bf16[128,1024]{1,0:T(8,128)(2,1)S(1)}, u32[]{:S(2)}, u32[]{:S(2)}) collective-permute-start(bf16[128,1024]{1,0:T(8,128)(2,1)} %get-tuple-element.56), channel_id=1, source_target_pairs={{32,0},{64,32},{96,64},{128,96},{160,128},{192,160},{224,192},{256... | collective-permute-start | bytes 786440 | tf_op jit(solution)/shard_map/ppermute | solution.py:558
  126.0 20.9 %collective-permute-start.7 = (bf16[128,1024]{1,0:T(8,128)(2,1)}, bf16[128,1024]{1,0:T(8,128)(2,1)S(1)}, u32[]{:S(2)}, u32[]{:S(2)}) collective-permute-start(bf16[128,1024]{1,0:T(8,128)(2,1)} %get-tuple-element.57), channel_id=1, source_target_pairs={{64,0},{96,32},{128,64},{160,96},{192,128},{224,160},{256,192},{28... | collective-permute-start | bytes 786440 | tf_op jit(solution)/shard_map/ppermute | solution.py:558

commit v6 on v5

--- a/solution.py
+++ b/solution.py
@@ -305,8 +305,21 @@
     n = row.shape[1]
     lead = lax.broadcasted_iota(jnp.int32, (n, n), 0)
     lane = lax.broadcasted_iota(jnp.int32, (n, n), 1)
-    spread = jnp.broadcast_to(row.astype(F32), (n, n))
-    return jnp.sum(jnp.where(lead == lane, spread, 0.0), axis=1, keepdims=True).astype(jnp.int32)
+    spread = jnp.broadcast_to(row, (n, n))
+    return jnp.sum(jnp.where(lead == lane, spread, 0.0), axis=1, keepdims=True)
+
+
+def as_row(column):
+    n = column.shape[0]
+    lead = lax.broadcasted_iota(jnp.int32, (n, n), 0)
+    lane = lax.broadcasted_iota(jnp.int32, (n, n), 1)
+    return jnp.sum(jnp.where(lead == lane, column, 0.0), axis=0, keepdims=True)
+
+
+def halves(convert, values, axis):
+    n = values.shape[axis] // 2
+    first, second = (values[:, :n], values[:, n:]) if axis else (values[:n], values[n:])
+    return jnp.concatenate([convert(first), convert(second)], axis=1 - axis)
 
 
 def softmax_kernel(
@@ -317,18 +330,28 @@
     neg_row_ref,
     slots_ref,
     users_ref,
-    den_ref,
-    pos_exp_ref,
+    stats_ref,
     neg_exp_ref,
     neg_rows_ref,
     pos_rows_ref,
     wide,
+    held_rows,
+    held_exp,
+    held_sems,
 ):
     chips = neg_row_ref.shape[1]
     n = users_ref.shape[0] // 2
     wide[...] = fetched_ref[...].astype(F32)
     neg_rows = slot_rows(wide, 0, 2 * CAP, chips)
-    neg_rows_ref[...] = neg_rows
+    held_rows[:chips, :] = neg_rows
+    copies = [
+        pltpu.make_async_copy(held_rows.at[pl.ds(0, chips), :], neg_rows_ref, held_sems.at[0]),
+        pltpu.make_async_copy(held_exp, neg_exp_ref, held_sems.at[1]),
+        pltpu.make_async_copy(
+            held_rows.at[pl.ds(chips, 2 * n), :], pos_rows_ref, held_sems.at[2]
+        ),
+    ]
+    copies[0].start()
     neg_bf = item_norm(neg_rows)[0].astype(BF16)
     loaded()
     users = users_ref[...]
@@ -338,39 +361,41 @@
         exponent = exponent + jnp.where(neg_row >= (1 << level), 1.0, 0.0)
     shift = math.log(8) + exponent * math.log(2.0)
     neg_exp = jnp.exp(dot(users, neg_bf, (1, 1)) / TAU + shift)
-    neg_exp_ref[...] = neg_exp
+    held_exp[...] = neg_exp
+    copies[1].start()
     slots = local_slots(slots_ref[...], place_ref[1], items)
     lane = lax.broadcasted_iota(jnp.int32, (n, chips), 1) * CAP
     pos_rows, here = [], []
     for core in range(2):
-        column = as_column(slots[:, core * n : (core + 1) * n])
+        column = as_column(slots[:, core * n : (core + 1) * n].astype(F32)).astype(jnp.int32)
         here.append(jnp.where(column >= 0, 1.0, 0.0))
         hots = [jnp.where(column == lane + k, 1.0, 0.0).astype(BF16) for k in range(CAP)]
         rows = [slot_rows(wide, 0, core * CAP + k, chips) for k in range(CAP)]
         pos_rows.append(dot(jnp.concatenate(hots, axis=1), jnp.concatenate(rows, axis=0)))
     pos_rows = jnp.concatenate(pos_rows, axis=0)
-    pos_rows_ref[...] = pos_rows.astype(BF16)
+    held_rows[chips:, :] = pos_rows.astype(BF16)
+    copies[2].start()
     pos_bf = item_norm(pos_rows)[0].astype(BF16).astype(F32)
     along = jnp.sum(users.astype(F32) * pos_bf, axis=-1, keepdims=True)
     pos_exp = jnp.concatenate(here, axis=0) * jnp.exp(along / TAU)
-    pos_exp_ref[...] = jnp.broadcast_to(pos_exp, pos_exp_ref.shape)
-    den_ref[...] = jnp.broadcast_to(
-        pos_exp + jnp.sum(neg_exp, axis=-1, keepdims=True), den_ref.shape
-    )
+    total = pos_exp + jnp.sum(neg_exp, axis=-1, keepdims=True)
+    stats_ref[0:1, :] = halves(as_row, total, 0)
+    stats_ref[1:2, :] = halves(as_row, pos_exp, 0)
+    for copy in copies:
+        copy.wait()
 
 
 def send_kernel(
     items,
     loaded,
     place_ref,
-    den_ref,
-    den_other_ref,
-    pos_exp_ref,
-    neg_exp_ref,
+    stats_ref,
+    stats_other_ref,
     neg_rows_ref,
     pos_rows_ref,
     users_ref,
     slots_ref,
+    neg_exp_ref,
     send_ref,
     own_part_ref,
     other_part_ref,
@@ -383,20 +408,19 @@
     chips = neg_rows_ref.shape[0]
     n = users_ref.shape[0] // 2
     core_here = place_ref[1]
-    loaded()
-    users = users_ref[...]
-    user_f = users.astype(F32)
+    loaded(2)
     neg_unit, neg_len = item_norm(neg_rows_ref[...])
     neg_bf = neg_unit.astype(BF16)
     pos_unit, pos_len = item_norm(pos_rows_ref[...])
     pos_bf = pos_unit.astype(BF16).astype(F32)
+    loaded()
+    users = users_ref[...]
+    user_f = users.astype(F32)
     slots = local_slots(slots_ref[...], core_here, items)
-    here = jnp.concatenate(
-        [jnp.where(as_column(slots[:, c * n : (c + 1) * n]) >= 0, 1.0, 0.0) for c in range(2)],
-        axis=0,
-    )
-    denominator = den_ref[:, 0:1] + den_other_ref[:, 0:1]
-    pos_delta = here * (pos_exp_ref[:, 0:1] / denominator - 1.0)
+    total = stats_ref[0:1, :] + stats_other_ref[0:1, :]
+    denominator = halves(as_column, total, 1)
+    delta = jnp.where(slots >= 0, stats_ref[1:2, :] / total - 1.0, 0.0)
+    pos_delta = halves(as_column, delta, 1)
     neg_prob = (neg_exp_ref[...] / denominator).astype(BF16)
     raw_pos = pos_delta * user_f / TAU
     pos_grad = (raw_pos - pos_unit * jnp.sum(pos_unit * raw_pos, axis=-1, keepdims=True)) / pos_len
@@ -643,11 +667,10 @@
     neg_here = lax.dynamic_index_in_dim(
         neg_rows.reshape(chips // items, 2, items), core, axis=1, keepdims=False
     ).reshape(1, chips)
-    den, pos_exp, neg_exp, neg_kept, pos_kept = call(
+    stats, neg_exp, neg_kept, pos_kept = call(
         functools.partial(softmax_kernel, items),
         [
-            pltpu.HBM((2 * n, LANES), F32),
-            pltpu.HBM((2 * n, LANES), F32),
+            shaped((2, 2 * n), F32),
             pltpu.HBM((2 * n, chips), F32),
             pltpu.HBM((chips, width), BF16),
             pltpu.HBM((2 * n, width), BF16),
@@ -655,14 +678,20 @@
         [SMEM, VMEM] + [None] * 3,
         (place, fetched, neg_here, slots, users),
         2 * n * width * owners * 3,
-        [staging[1]],
+        [
+            staging[1],
+            pltpu.VMEM((chips + 2 * n, width), BF16),
+            pltpu.VMEM((2 * n, chips), F32),
+            pltpu.SemaphoreType.DMA((3,)),
+        ],
         mib=40,
+        out_specs=(VMEM, HBM, HBM, HBM),
     )
     send, own_part, other_part = call(
         functools.partial(send_kernel, items),
         [shaped((big, LANES), BF16), pltpu.HBM((n, width), F32), pltpu.HBM((n, width), F32)],
-        [SMEM, None, VMEM] + [None] * 6,
-        (place, den, swapped(den), pos_exp, neg_exp, neg_kept, pos_kept, users, slots),
+        [SMEM, VMEM, VMEM] + [None] * 5,
+        (place, stats, swapped(stats), neg_kept, pos_kept, users, slots, neg_exp),
         2 * n * width * owners * 4,
         outward + [pltpu.VMEM((2 * n, width), F32), pltpu.SemaphoreType.DMA((2,))],
         mib=40,

time: 153 us -> 152 us (level)
  no operation moved by 1% of the time
where the time goes in v6:
time: 152 us; the launch traced here: 151 us
  starting transfers between devices  68.7 us (45%)
  waiting for transfers between devices  49 us (32%)
  Pallas kernels  27.3 us (18%)
  other arithmetic  3.09 us (2%)
  local copies, waits for them, and re-layouts  2.02 us (1%)
    all_to_all x3, starting transfers between devices, exchange(): lax.all_to_all(split, axes, split_axis=0, concat_axis=0, tiled=True)  41.5 us
    all_to_all x3, waiting for transfers between devices, exchange(): lax.all_to_all(split, axes, split_axis=0, concat_axis=0, tiled=True)  27.4 us
    pallas_call x7, Pallas kernels, call(): pl.pallas_call(body, out_shape=tuple(outs), in_specs=[HBM if spec is None...  27.3 us
    ppermute x4, waiting for transfers between devices, passed_along(): return lax.ppermute(shard, axes, pairs)  19.6 us
    ppermute x4, starting transfers between devices, swapped(): return lax.ppermute(shard, 'core', [(0, 1), (1, 0)])  15.9 us
    ppermute x4, starting transfers between devices, passed_along(): return lax.ppermute(shard, axes, pairs)  11.4 us
  transfers between devices with their start and end apart: 11, of which 8 were waited for; matrix products, arithmetic and copies ran while one was open for 3% of the time, Pallas kernels for 10%

profile of v6, /device:TPU:1, one launch (start us, length us, event | category | flops | bytes accessed | tf_op | source)
XLA Modules:
  0.0 151.1 jit_solution(1899062287802408252)
XLA Ops:
  0.6 1.7 %shard_map.104 = (s32[512,128]{1,0:T(8,128)}, s32[1,128]{1,0:T(1,128)}, s32[128,1]{1,0:T(8,128)}) custom-call(s32[1,128]{1,0:T(1,128)} %bitcast.33, s32[1,128]{1,0:T(1,128)} %refs_1_.4, s32[1,512]{1,0:T(1,128)} %bitcast.31), custom_call_target="tpu_custom_call" | custom-call | flops 33554432 | bytes 266240 | tf_op jit(solution)/shard_map/pallas_call | solution.py:59
  2.4 22.2 %all-to-all-start = ((s32[512,1,128]{2,1,0:T(1,128)}), s32[512,1,128]{2,1,0:T(1,128)S(1)}, u32[]{:S(2)}, u32[]{:S(2)}) async-start(s32[512,1,128]{2,1,0:T(1,128)} %bitcast.27), calls=%async_computation | async-start | bytes 524288 | tf_op jit(solution)/shard_map/all_to_all | solution.py:604
  24.5 3.7 %collective-permute-start.1 = (bf16[128,512]{1,0:T(8,128)(2,1)}, bf16[128,512]{1,0:T(8,128)(2,1)S(1)}, u32[]{:S(2)}, u32[]{:S(2)}) collective-permute-start(bf16[128,512]{1,0:T(8,128)(2,1)} %bitcast.23), channel_id=1, source_target_pairs={{0,64},{32,96},{64,128},{96,160},{128,192},{160,224},{192,256},{22... | collective-permute-start | bytes 393224 | tf_op jit(solution)/shard_map/ppermute | solution.py:582
  28.2 4.2 %collective-permute-start = (bf16[128,512]{1,0:T(8,128)(2,1)}, bf16[128,512]{1,0:T(8,128)(2,1)S(1)}, u32[]{:S(2)}, u32[]{:S(2)}) collective-permute-start(bf16[128,512]{1,0:T(8,128)(2,1)} %bitcast.24), channel_id=1, source_target_pairs={{0,32},{32,64},{64,96},{96,128},{128,160},{160,192},{192,224},{224... | collective-permute-start | bytes 393224 | tf_op jit(solution)/shard_map/ppermute | solution.py:582
  32.4 8.9 %all-to-all-done = s32[512,1,128]{2,1,0:T(1,128)S(1)} async-done(((s32[512,1,128]{2,1,0:T(1,128)}), s32[512,1,128]{2,1,0:T(1,128)S(1)}, u32[]{:S(2)}, u32[]{:S(2)}) %all-to-all-start) | async-done | bytes 262176 | tf_op jit(solution)/shard_map/all_to_all | solution.py:604
  41.3 0.0 copy-start
  41.3 2.6 %shard_map.105 = bf16[5120,128]{1,0:T(8,128)(2,1)} custom-call(s32[512,128]{1,0:T(8,128)S(1)} %bitcast.21, bf16[256,512]{1,0:T(8,128)(2,1)} %refs_1_.5), custom_call_target="tpu_custom_call" | custom-call | flops 335544320 | bytes 1835008 | tf_op jit(solution)/shard_map/pallas_call | solution.py:59
  43.9 0.0 collective-permute-done.1.refs_2_
  43.9 0.0 collective-permute-done.refs_3_
  43.9 0.0 copy-start.5
  43.9 0.0 copy-start.4
  43.9 0.0 copy-start.2
  44.0 0.0 copy-done
  44.0 10.0 %all-to-all-start.1 = ((bf16[256,5,4,128]{3,2,1,0:T(4,128)(2,1)}), bf16[256,5,4,128]{3,2,1,0:T(4,128)(2,1)S(1)}, u32[]{:S(2)}, u32[]{:S(2)}) async-start(bf16[256,5,4,128]{3,2,1,0:T(4,128)(2,1)} %bitcast.8), calls=%async_computation.1 | async-start | bytes 2621440 | tf_op jit(solution)/shard_map/all_to_all | solution.py:604
  54.0 0.0 copy-done.5
  54.0 4.7 %collective-permute-start.2 = (s32[1,128]{1,0:T(1,128)S(1)}, s32[1,128]{1,0:T(1,128)S(1)}, u32[]{:S(2)}, u32[]{:S(2)}) collective-permute-start(s32[1,128]{1,0:T(1,128)S(1)} %copy-done.5), channel_id=1, source_target_pairs={{0,32},{32,0},{1,33},{33,1},{2,34},{34,2},{3,35},{35,3},{4,36},{36... | collective-permute-start | bytes 1544 | tf_op jit(solution)/shard_map/ppermute | solution.py:586
  58.7 0.5 broadcast.11
  59.2 0.0 copy-done.4
  59.2 0.7 reduce.3
  59.9 0.1 reshape.96
  60.0 0.1 pad_add_fusion.refs_0_
  60.1 0.0 copy-done.2
  60.1 5.9 %shard_map.106 = (f32[128,512]{1,0:T(8,128)}, f32[128,128]{1,0:T(8,128)}, f32[128,512]{1,0:T(8,128)}, f32[128,128]{1,0:T(8,128)}, bf16[128,512]{1,0:T(8,128)(2,1...) custom-call(s32[2]{0:T(128)S(1)} %pad_add_fusion.refs_0_, ...), custom_call_target="tpu_custom_call" | custom-call | flops 805306368 | bytes 5900360 | tf_op jit(solution)/shard_map/pallas_call | solution.py:59
  65.9 1.9 %collective-permute-start.3 = (bf16[128,512]{1,0:T(8,128)(2,1)}, bf16[128,512]{1,0:T(8,128)(2,1)S(1)}, u32[]{:S(2)}, u32[]{:S(2)}) collective-permute-start(bf16[128,512]{1,0:T(8,128)(2,1)} %get-tuple-element.37), channel_id=1, source_target_pairs={{0,32},{32,0},{1,33},{33,1},{2,34},{34,2},{3,35},{35,3},{4,36},{36... | collective-permute-start | bytes 393224 | tf_op jit(solution)/shard_map/ppermute | solution.py:586
  67.9 0.7 reshape.97.refs_2_
  68.5 0.0 collective-permute-done.2
  68.5 0.6 broadcast_select_fusion.refs_3_.refs_6_
  69.1 0.2 collective-permute-done.3
  69.4 1.8 %maximum_select_fusion.refs_4_.refs_5_ = bf16[256,512]{1,0:T(8,128)(2,1)} fusion(bf16[128,512]{1,0:T(8,128)(2,1)S(1)} %collective-permute-done.3, bf16[128,512]{1,0:T(8,128)(2,1)} %get-tuple-element.37, pred[]{:T(512)S(6)} %eq.4), kind=kLoop, calls=%fused_computation | loop fusion | flops 1179648 | bytes 524289 | tf_op jit(solution)/shard_map/jit(_where)/select_n | solution.py:607
  71.1 16.5 %all-to-all-done.1 = bf16[256,5,4,128]{3,2,1,0:T(4,128)(2,1)S(1)} async-done(((bf16[256,5,4,128]{3,2,1,0:T(4,128)(2,1)}), bf16[256,5,4,128]{3,2,1,0:T(4,128)(2,1)S(1)}, u32[]{:S(2)}, u32[]{:S(2)}) %all-to-all-start.1) | async-done | bytes 1310752 | tf_op jit(solution)/shard_map/all_to_all | solution.py:604
  87.6 2.7 %shard_map.107 = (f32[2,256]{1,0:T(2,128)S(1)}, f32[256,256]{1,0:T(8,128)}, bf16[256,512]{1,0:T(8,128)(2,1)}, bf16[256,512]{1,0:T(8,128)(2,1)}) custom-call(s32[2]{0:T(128)S(1)} %pad_add_fusion.refs_0_, bf16[5120,128]{1,0:T(8,128)(2,1)S(1)} %bitcast.19, s32[1,256]{1,0:T(1,128)} %reshape.97.refs_2_, s32[1,256]{1,0:T(1,128)} %broadcast_select_fusion.refs_3_.refs_6_, ...), custom_call_target="tpu_custom_call" | custom-call | flops 201326592 | bytes 2363400 | tf_op jit(solution)/shard_map/pallas_call | solution.py:59
  90.3 7.0 %collective-permute-start.4 = (f32[2,256]{1,0:T(2,128)S(1)}, f32[2,256]{1,0:T(2,128)S(1)}, u32[]{:S(2)}, u32[]{:S(2)}) collective-permute-start(f32[2,256]{1,0:T(2,128)S(1)} %get-tuple-element.38.refs_1_), channel_id=1, source_target_pairs={{0,32},{32,0},{1,33},{33,1},{2,34},{34,2},{3,35},{35,3},{4,36},{36... | collective-permute-start | bytes 6152 | tf_op jit(solution)/shard_map/ppermute | solution.py:586
  97.3 0.6 collective-permute-done.4.refs_2_
  97.9 0.0 copy-done.1
  97.9 3.9 %shard_map.108 = (bf16[5120,128]{1,0:T(8,128)(2,1)}, f32[128,512]{1,0:T(8,128)}, f32[128,512]{1,0:T(8,128)}) custom-call(s32[2]{0:T(128)S(1)} %pad_add_fusion.refs_0_, f32[2,256]{1,0:T(2,128)S(1)} %get-tuple-element.38.refs_1_, f32[2,256]{1,0:T(2,128)S(1)} %collective-permute-done.4.refs_2_, bf16[256,512]{1,0:T(8,128)(2,1)} %get-tuple-element.39.refs_3_, ...), custom_call_target="tpu_custom_call" | custom-call | flops 268435456 | bytes 2888712 | tf_op jit(solution)/shard_map/pallas_call | solution.py:59
  101.9 0.0 copy-start.6
  101.9 9.3 %all-to-all-start.2 = ((bf16[256,5,4,128]{3,2,1,0:T(4,128)(2,1)}), bf16[256,5,4,128]{3,2,1,0:T(4,128)(2,1)S(1)}, u32[]{:S(2)}, u32[]{:S(2)}) async-start(bf16[256,5,4,128]{3,2,1,0:T(4,128)(2,1)} %bitcast.11), calls=%async_computation.2 | async-start | bytes 2621440 | tf_op jit(solution)/shard_map/all_to_all | solution.py:604
  111.2 0.0 copy-done.6
  111.2 2.2 %collective-permute-start.5 = (f32[128,512]{1,0:T(8,128)S(1)}, f32[128,512]{1,0:T(8,128)S(1)}, u32[]{:S(2)}, u32[]{:S(2)}) collective-permute-start(f32[128,512]{1,0:T(8,128)S(1)} %copy-done.6), channel_id=1, source_target_pairs={{0,32},{32,0},{1,33},{33,1},{2,34},{34,2},{3,35},{35,3},{4,36},{36... | collective-permute-start | bytes 786440 | tf_op jit(solution)/shard_map/ppermute | solution.py:586
  113.5 1.2 collective-permute-done.5.refs_3_
  114.7 0.7 copy-done.3
  115.4 7.0 %shard_map.109 = (f32[128,1024]{1,0:T(8,128)}, bf16[128,1024]{1,0:T(8,128)(2,1)}, bf16[128,1024]{1,0:T(8,128)(2,1)}, f32[128,512]{1,0:T(8,128)}, f32[128,512]{1,0:T(8,128)}) custom-call(s32[2]{0:T(128)} %copy-done.1, s32[1,16]{1,0:T(1,128)} %refs_1_.7, f32[128,512]{1,0:T(8,128)} %get-tuple-element.43.refs_2_, f32[128,512]{1,0:T(8,128)} %copy-done.3, ...), custom_call_target="tpu_custom_call" | custom-call | flops 805306368 | bytes 6946888 | tf_op jit(solution)/shard_map/pallas_call | solution.py:59
  122.4 2.2 %collective-permute-start.6 = (bf16[128,1024]{1,0:T(8,128)(2,1)}, bf16[128,1024]{1,0:T(8,128)(2,1)S(1)}, u32[]{:S(2)}, u32[]{:S(2)}) collective-permute-start(bf16[128,1024]{1,0:T(8,128)(2,1)} %get-tuple-element.54), channel_id=1, source_target_pairs={{32,0},{64,32},{96,64},{128,96},{160,128},{192,160},{224,192},{256... | collective-permute-start | bytes 786440 | tf_op jit(solution)/shard_map/ppermute | solution.py:582
  124.6 1.3 collective-permute-start.7
  125.9 19.2 %collective-permute-done.6.refs_1_ = bf16[128,1024]{1,0:T(8,128)(2,1)S(1)} collective-permute-done((bf16[128,1024]{1,0:T(8,128)(2,1)}, bf16[128,1024]{1,0:T(8,128)(2,1)S(1)}, u32[]{:S(2)}, u32[]{:S(2)}) %collective-permute-start.6) | collective-permute-done | bytes 262176 | tf_op jit(solution)/shard_map/ppermute | solution.py:582
  145.2 0.4 collective-permute-done.7.refs_2_
  145.5 2.0 %all-to-all-done.2 = bf16[256,5,4,128]{3,2,1,0:T(4,128)(2,1)S(1)} async-done(((bf16[256,5,4,128]{3,2,1,0:T(4,128)(2,1)}), bf16[256,5,4,128]{3,2,1,0:T(4,128)(2,1)S(1)}, u32[]{:S(2)}, u32[]{:S(2)}) %all-to-all-start.2) | async-done | bytes 1310752 | tf_op jit(solution)/shard_map/all_to_all | solution.py:604
  147.5 3.4 %shard_map.110 = (bf16[256,512]{1,0:T(8,128)(2,1)}, bf16[128,512]{1,0:T(8,128)(2,1)}) custom-call(bf16[5120,128]{1,0:T(8,128)(2,1)S(1)} %bitcast.20, bf16[128,1024]{1,0:T(8,128)(2,1)S(1)} %collective-permute-done.6.refs_1_, bf16[128,1024]{1,0:T(8,128)(2,1)S(1)} %collective-permute-done.7.refs_2_, s32[512,128]{1,0:T(8,128)} %bitcast.22, ...), custom_call_target="tpu_custom_call" | custom-call | flops 335544320 | bytes 6293504 | tf_op jit(solution)/shard_map/pallas_call | solution.py:59
  (3 shorter events, 0.0 us)
Async XLA Ops:
  2.4 38.9 %all-to-all-start = ((s32[512,1,128]{2,1,0:T(1,128)}), s32[512,1,128]{2,1,0:T(1,128)S(1)}, u32[]{:S(2)}, u32[]{:S(2)}) async-start(s32[512,1,128]{2,1,0:T(1,128)} %bitcast.27), calls=%async_computation | async-start | bytes 524288 | tf_op jit(solution)/shard_map/all_to_all | solution.py:604
  24.5 19.4 %collective-permute-start.1 = (bf16[128,512]{1,0:T(8,128)(2,1)}, bf16[128,512]{1,0:T(8,128)(2,1)S(1)}, u32[]{:S(2)}, u32[]{:S(2)}) collective-permute-start(bf16[128,512]{1,0:T(8,128)(2,1)} %bitcast.23), channel_id=1, source_target_pairs={{0,64},{32,96},{64,128},{96,160},{128,192},{160,224},{192,256},{22... | collective-permute-start | bytes 393224 | tf_op jit(solution)/shard_map/ppermute | solution.py:582
  28.2 15.7 %collective-permute-start = (bf16[128,512]{1,0:T(8,128)(2,1)}, bf16[128,512]{1,0:T(8,128)(2,1)S(1)}, u32[]{:S(2)}, u32[]{:S(2)}) collective-permute-start(bf16[128,512]{1,0:T(8,128)(2,1)} %bitcast.24), channel_id=1, source_target_pairs={{0,32},{32,64},{64,96},{96,128},{128,160},{160,192},{192,224},{224... | collective-permute-start | bytes 393224 | tf_op jit(solution)/shard_map/ppermute | solution.py:582
  41.3 2.7 %copy-start = (s32[512,1,128]{2,1,0:T(1,128)}, s32[512,1,128]{2,1,0:T(1,128)S(1)}, u32[]{:S(2)}) copy-start(s32[512,1,128]{2,1,0:T(1,128)S(1)} %all-to-all-done) | copy-start | bytes 786436
  43.9 10.1 %copy-start.5 = (s32[1,128]{1,0:T(1,128)S(1)}, s32[1,128]{1,0:T(1,128)}, u32[]{:S(2)}) copy-start(s32[1,128]{1,0:T(1,128)} %get-tuple-element.34) | copy-start | bytes 1540
  43.9 15.3 %copy-start.4 = (s32[1,512,1]{1,2,0:T(1,128)S(1)}, s32[1,512,1]{1,2,0:T(1,128)}, u32[]{:S(2)}) copy-start(s32[1,512,1]{1,2,0:T(1,128)} %param.17) | copy-start | bytes 6148
  43.9 16.1 %copy-start.2 = (s32[1,16]{1,0:T(1,128)S(1)}, s32[1,16]{1,0:T(1,128)}, u32[]{:S(2)}) copy-start(s32[1,16]{1,0:T(1,128)} %refs_1_.7) | copy-start | bytes 196
  44.0 43.6 %all-to-all-start.1 = ((bf16[256,5,4,128]{3,2,1,0:T(4,128)(2,1)}), bf16[256,5,4,128]{3,2,1,0:T(4,128)(2,1)S(1)}, u32[]{:S(2)}, u32[]{:S(2)}) async-start(bf16[256,5,4,128]{3,2,1,0:T(4,128)(2,1)} %bitcast.8), calls=%async_computation.1 | async-start | bytes 2621440 | tf_op jit(solution)/shard_map/all_to_all | solution.py:604
  54.0 14.6 %collective-permute-start.2 = (s32[1,128]{1,0:T(1,128)S(1)}, s32[1,128]{1,0:T(1,128)S(1)}, u32[]{:S(2)}, u32[]{:S(2)}) collective-permute-start(s32[1,128]{1,0:T(1,128)S(1)} %copy-done.5), channel_id=1, source_target_pairs={{0,32},{32,0},{1,33},{33,1},{2,34},{34,2},{3,35},{35,3},{4,36},{36... | collective-permute-start | bytes 1544 | tf_op jit(solution)/shard_map/ppermute | solution.py:586
  60.1 37.9 %copy-start.1 = (s32[2]{0:T(128)}, s32[2]{0:T(128)S(1)}, u32[]{:S(2)}) copy-start(s32[2]{0:T(128)S(1)} %pad_add_fusion.refs_0_) | copy-start | bytes 28
  65.9 3.5 %collective-permute-start.3 = (bf16[128,512]{1,0:T(8,128)(2,1)}, bf16[128,512]{1,0:T(8,128)(2,1)S(1)}, u32[]{:S(2)}, u32[]{:S(2)}) collective-permute-start(bf16[128,512]{1,0:T(8,128)(2,1)} %get-tuple-element.37), channel_id=1, source_target_pairs={{0,32},{32,0},{1,33},{33,1},{2,34},{34,2},{3,35},{35,3},{4,36},{36... | collective-permute-start | bytes 393224 | tf_op jit(solution)/shard_map/ppermute | solution.py:586
  90.3 7.6 %collective-permute-start.4 = (f32[2,256]{1,0:T(2,128)S(1)}, f32[2,256]{1,0:T(2,128)S(1)}, u32[]{:S(2)}, u32[]{:S(2)}) collective-permute-start(f32[2,256]{1,0:T(2,128)S(1)} %get-tuple-element.38.refs_1_), channel_id=1, source_target_pairs={{0,32},{32,0},{1,33},{33,1},{2,34},{34,2},{3,35},{35,3},{4,36},{36... | collective-permute-start | bytes 6152 | tf_op jit(solution)/shard_map/ppermute | solution.py:586
  101.9 9.3 %copy-start.6 = (f32[128,512]{1,0:T(8,128)S(1)}, f32[128,512]{1,0:T(8,128)}, u32[]{:S(2)}) copy-start(f32[128,512]{1,0:T(8,128)} %get-tuple-element.44) | copy-start | bytes 786436
  101.9 45.6 %all-to-all-start.2 = ((bf16[256,5,4,128]{3,2,1,0:T(4,128)(2,1)}), bf16[256,5,4,128]{3,2,1,0:T(4,128)(2,1)S(1)}, u32[]{:S(2)}, u32[]{:S(2)}) async-start(bf16[256,5,4,128]{3,2,1,0:T(4,128)(2,1)} %bitcast.11), calls=%async_computation.2 | async-start | bytes 2621440 | tf_op jit(solution)/shard_map/all_to_all | solution.py:604
  111.2 3.4 %collective-permute-start.5 = (f32[128,512]{1,0:T(8,128)S(1)}, f32[128,512]{1,0:T(8,128)S(1)}, u32[]{:S(2)}, u32[]{:S(2)}) collective-permute-start(f32[128,512]{1,0:T(8,128)S(1)} %copy-done.6), channel_id=1, source_target_pairs={{0,32},{32,0},{1,33},{33,1},{2,34},{34,2},{3,35},{35,3},{4,36},{36... | collective-permute-start | bytes 786440 | tf_op jit(solution)/shard_map/ppermute | solution.py:586
  114.7 0.7 copy-start.3
  122.4 22.8 %collective-permute-start.6 = (bf16[128,1024]{1,0:T(8,128)(2,1)}, bf16[128,1024]{1,0:T(8,128)(2,1)S(1)}, u32[]{:S(2)}, u32[]{:S(2)}) collective-permute-start(bf16[128,1024]{1,0:T(8,128)(2,1)} %get-tuple-element.54), channel_id=1, source_target_pairs={{32,0},{64,32},{96,64},{128,96},{160,128},{192,160},{224,192},{256... | collective-permute-start | bytes 786440 | tf_op jit(solution)/shard_map/ppermute | solution.py:582
  124.6 20.9 %collective-permute-start.7 = (bf16[128,1024]{1,0:T(8,128)(2,1)}, bf16[128,1024]{1,0:T(8,128)(2,1)S(1)}, u32[]{:S(2)}, u32[]{:S(2)}) collective-permute-start(bf16[128,1024]{1,0:T(8,128)(2,1)} %get-tuple-element.55), channel_id=1, source_target_pairs={{64,0},{96,32},{128,64},{160,96},{192,128},{224,160},{256,192},{28... | collective-permute-start | bytes 786440 | tf_op jit(solution)/shard_map/ppermute | solution.py:582

commit v7 on v6

--- a/solution.py
+++ b/solution.py
@@ -13,7 +13,6 @@
 CAP = 2
 CHUNKS = 4
 LANES = 128
-SLOTS = CAP + 1
 SEATS = 2 * CAP + 1
 PIECES = 2
 NBANK = SEATS * CHUNKS
@@ -106,36 +105,50 @@
     return 1.0 / (1.0 + jnp.exp(-value))
 
 
-def ask_kernel(owner_ref, row_ref, neg_ref, ask_ref, slot_row_ref, slot_col_ref):
+def slots_kernel(owner_ref, row_ref, out_ref):
     n = owner_ref.shape[1]
-    owners = ask_ref.shape[0]
     lead = lax.broadcasted_iota(jnp.int32, (n, n), 0)
     lane = lax.broadcasted_iota(jnp.int32, (n, n), 1)
-
-    def column(row):
-        spread = jnp.broadcast_to(row.astype(F32), (n, n))
-        return jnp.sum(jnp.where(lead == lane, spread, 0.0), axis=1, keepdims=True)
-
     owner_r = jnp.broadcast_to(owner_ref[...].astype(F32), (n, n))
-    owner_c = column(owner_ref[...])
-    same = owner_r == owner_c
-    rank_r = jnp.sum(jnp.where(same & (lead < lane), 1.0, 0.0), axis=0, keepdims=True)
-    rank_c = jnp.sum(jnp.where(same & (lane < lead), 1.0, 0.0), axis=1, keepdims=True)
-    slot_r = owner_ref[...] * CAP + rank_r.astype(jnp.int32)
-    slot_row_ref[...] = slot_r
-    slot_col_ref[...] = (owner_c * CAP + rank_c).astype(jnp.int32)
-    rows = jnp.broadcast_to(column(row_ref[...]), (n, LANES))
-    by_owner = lax.broadcasted_iota(jnp.int32, (owners, n), 0) * CAP
+    owner_c = as_column(owner_ref[...].astype(F32))
+    before = jnp.where((owner_r == owner_c) & (lead < lane), 1.0, 0.0)
+    rank = jnp.sum(before, axis=0, keepdims=True)
+    out_ref[0:1, :] = owner_ref[...] * CAP + rank.astype(jnp.int32)
+    out_ref[1:2, :] = row_ref[...]
+
+
+def ask_kernel(
+    items, loaded, place_ref, mine_ref, other_ref, neg_ref, ask_ref, slots_ref, neg_row_ref
+):
+    n = mine_ref.shape[1]
+    chips = ask_ref.shape[0]
+    bits = items.bit_length() - 1
+    core_here = place_ref[1]
+    first = core_here == 0
+    lane = lax.broadcasted_iota(jnp.int32, (n, LANES), 1)
+    by_owner = lax.broadcasted_iota(jnp.int32, (chips, n), 0) * CAP
+    loaded()
     asked = None
-    for k in range(CAP):
-        hot = jnp.where(slot_r == by_owner + k, 1.0, 0.0).astype(BF16)
-        part = dot(hot, jnp.where(lane == k, rows, 0.0).astype(BF16))
-        asked = part if asked is None else asked + part
-    for c in range(owners // n):
-        negative = column(neg_ref[:, c * n : (c + 1) * n])
-        ask_ref[c * n : (c + 1) * n, :] = jnp.where(
-            lane == CAP, negative, asked[c * n : (c + 1) * n]
-        ).astype(jnp.int32)
+    for core in range(2):
+        own, sibling = mine_ref[...], other_ref[...]
+        named = jnp.where(first, own, sibling) if core == 0 else jnp.where(first, sibling, own)
+        slots_ref[:, core * n : (core + 1) * n] = named[0:1, :]
+        slots = local_slots(named[0:1, :], core_here, items)
+        rows = as_column(named[1:2, :].astype(F32))
+        for k in range(CAP):
+            hot = jnp.where(slots == by_owner + k, 1.0, 0.0).astype(BF16)
+            part = dot(hot, jnp.where(lane == core * CAP + k, rows, 0.0).astype(BF16))
+            asked = part if asked is None else asked + part
+    neg_all = jnp.broadcast_to(neg_ref[...].astype(F32), (n, 2 * chips))
+    at = lax.broadcasted_iota(jnp.int32, (n, 2 * chips), 0)
+    owner = lax.broadcasted_iota(jnp.int32, (n, 2 * chips), 1)
+    for c in range(chips // n):
+        own = slice(c * n, (c + 1) * n)
+        local = at + c * n
+        wanted = ((local >> bits) << (bits + 1)) + (core_here << bits) + (local & (items - 1))
+        negative = jnp.sum(jnp.where(owner == wanted, neg_all, 0.0), axis=1, keepdims=True)
+        ask_ref[own, :] = jnp.where(lane == 2 * CAP, negative, asked[own]).astype(jnp.int32)
+        neg_row_ref[:, own] = as_row(negative).astype(jnp.int32)
 
 
 def spread_slot(wide, base, k, rows):
@@ -156,22 +169,10 @@
     return ref.at[pl.ds(i * size, size), :]
 
 
-def by_chip(asks_ref, core, items):
-    count = asks_ref.shape[0] // (2 * items)
-    return jnp.concatenate(
-        [
-            asks_ref[(2 * z + core) * items : (2 * z + core + 1) * items, :]
-            for z in range(count)
-        ],
-        axis=0,
-    )
-
-
-def serve_kernel(items, loaded, asks_ref, table_ref, out_ref, wide, narrow, sems):
-    chips = asks_ref.shape[0] // 2
+def serve_kernel(loaded, asks_ref, table_ref, out_ref, wide, narrow, sems):
+    chips = asks_ref.shape[0]
     part = chips // PIECES
     rows = table_ref.shape[0]
-    asks = [by_chip(asks_ref, core, items) for core in range(2)]
     loaded()
     table = table_ref[...]
     row_id = lax.broadcasted_iota(jnp.int32, (part, rows), 1)
@@ -179,8 +180,7 @@
     for i in range(PIECES):
         base = i * part * NBANK
         for seat in range(SEATS):
-            core, k = (0, CAP) if seat == 2 * CAP else divmod(seat, CAP)
-            asked = asks[core][i * part : (i + 1) * part, k : k + 1]
+            asked = asks_ref[i * part : (i + 1) * part, seat : seat + 1]
             hot = jnp.where(asked == row_id, 1.0, 0.0).astype(BF16)
             spread_slot(wide, base, seat, dot(hot, table))
         narrow[base : base + part * NBANK, :] = wide[base : base + part * NBANK, :].astype(BF16)
@@ -526,7 +526,6 @@
 
 
 def last_kernel(
-    items,
     loaded,
     returned_ref,
     near_ref,
@@ -546,16 +545,15 @@
     held_sem,
 ):
     width = hist_ref.shape[1]
-    chips = asks_ref.shape[0] // 2
+    chips = asks_ref.shape[0]
     rows = table_grad_ref.shape[0]
     wide[...] = returned_ref[...].astype(F32)
     loaded(1)
-    asks = [jnp.transpose(by_chip(asks_ref, core, items).astype(F32)) for core in range(2)]
+    asks = jnp.transpose(asks_ref[...].astype(F32))
     row_id = lax.broadcasted_iota(jnp.int32, (rows, chips), 0).astype(F32)
     hots, parts = [], []
     for seat in range(SEATS):
-        core, k = (0, CAP) if seat == 2 * CAP else divmod(seat, CAP)
-        hots.append(jnp.where(asks[core][k : k + 1] == row_id, 1.0, 0.0).astype(BF16))
+        hots.append(jnp.where(asks[seat : seat + 1] == row_id, 1.0, 0.0).astype(BF16))
         parts.append(slot_rows(wide, 0, seat, chips))
     total = dot(jnp.concatenate(hots, axis=1), jnp.concatenate(parts, axis=0))
     held[...] = total.astype(BF16)
@@ -610,14 +608,26 @@
             jnp.concatenate([other, mine], axis=axis),
         )
 
-    ask, slot_row, slot_col = call(
-        ask_kernel,
-        [shaped((owners, LANES), jnp.int32), shaped((1, n), jnp.int32), shaped((n, 1), jnp.int32)],
-        [VMEM, VMEM, VMEM],
-        (pos_owner.reshape(1, n), pos_row, neg_row),
-        2 * CAP * owners * n * LANES,
-    )
-    asks = exchange(ask, ("z", "core", "items"), (1, LANES))
+    (mine,) = call(
+        slots_kernel,
+        [shaped((2, n), jnp.int32)],
+        [VMEM, VMEM],
+        (pos_owner.reshape(1, n), pos_row),
+        n * n,
+    )
+    ask, slots, neg_here = call(
+        functools.partial(ask_kernel, items),
+        [
+            pltpu.HBM((chips, LANES), jnp.int32),
+            pltpu.HBM((1, 2 * n), jnp.int32),
+            pltpu.HBM((1, chips), jnp.int32),
+        ],
+        [SMEM, None, VMEM, None],
+        (place, mine, swapped(mine), neg_row),
+        4 * CAP * chips * n * LANES,
+        mib=40,
+    )
+    asks = exchange(ask, ("z", "items"), (1, LANES))
     near = passed_along(own, 1)
     far = passed_along(own, 2)
 
@@ -629,7 +639,7 @@
     ]
     outward = [staging[1], staging[0], staging[2]]
     (served,) = call(
-        functools.partial(serve_kernel, items),
+        serve_kernel,
         [shaped((big, LANES), BF16)],
         [VMEM, None],
         (asks, item_table),
@@ -663,10 +673,6 @@
     )
 
     users = by_core(user, swapped(user), 0)
-    slots = by_core(slot_row, swapped(slot_row), 1)
-    neg_here = lax.dynamic_index_in_dim(
-        neg_rows.reshape(chips // items, 2, items), core, axis=1, keepdims=False
-    ).reshape(1, chips)
     stats, neg_exp, neg_kept, pos_kept = call(
         functools.partial(softmax_kernel, items),
         [
@@ -731,7 +737,7 @@
     near_back = passed_along(near_grad, -1)
     far_back = passed_along(far_grad, -2)
     table_grad, history_grad = call(
-        functools.partial(last_kernel, items),
+        last_kernel,
         [shaped((rows, width), BF16), shaped((n, width), BF16)],
         [VMEM] * 3 + [None] * 8,
         (

time: 152 us -> 155 us (1.020)
  waiting for transfers between devices: 49 us -> 51.2 us
  Pallas kernels: 27.3 us -> 29.1 us
  starting transfers between devices: 68.7 us -> 70.5 us
    ppermute x4, starting transfers between devices: 15.9 us -> 23.2 us  [swapped(): return lax.ppermute(shard, 'core', [(0, 1), (1, 0)])]
    all_to_all x3, starting transfers between devices: 41.5 us -> 37.6 us  [exchange(): lax.all_to_all(split, axes, split_axis=0, concat_axis=0, tiled=True)]
    pallas_call x7 -> x8, Pallas kernels: 27.3 us -> 29.1 us  [call(): pl.pallas_call(body, out_shape=tuple(outs), in_specs=[HBM if spec is None...]
    ppermute x4, waiting for transfers between devices: 2.04 us -> 3.89 us  [swapped(): return lax.ppermute(shard, 'core', [(0, 1), (1, 0)])]
    ppermute x4, starting transfers between devices: 11.4 us -> 9.6 us  [passed_along(): return lax.ppermute(shard, axes, pairs)]
  transfers between devices with their start and end apart: 11 -> 11, of which waited for: 8 -> 9; matrix products, arithmetic and copies ran while one was open for 3% -> 1% of each run, Pallas kernels for 10% -> 10%
where the time goes in v7:
time: 155 us; the launch traced here: 154 us
  starting transfers between devices  70.5 us (45%)
  waiting for transfers between devices  51.2 us (33%)
  Pallas kernels  29.1 us (19%)
  other arithmetic  1.83 us (1%)
    all_to_all x3, starting transfers between devices, exchange(): lax.all_to_all(split, axes, split_axis=0, concat_axis=0, tiled=True)  37.6 us
    pallas_call x8, Pallas kernels, call(): pl.pallas_call(body, out_shape=tuple(outs), in_specs=[HBM if spec is None...  29.1 us
    all_to_all x3, waiting for transfers between devices, exchange(): lax.all_to_all(split, axes, split_axis=0, concat_axis=0, tiled=True)  27.7 us
    ppermute x4, starting transfers between devices, swapped(): return lax.ppermute(shard, 'core', [(0, 1), (1, 0)])  23.2 us
    ppermute x4, waiting for transfers between devices, passed_along(): return lax.ppermute(shard, axes, pairs)  19.6 us
    ppermute x4, starting transfers between devices, passed_along(): return lax.ppermute(shard, axes, pairs)  9.6 us
    ppermute x4, waiting for transfers between devices, swapped(): return lax.ppermute(shard, 'core', [(0, 1), (1, 0)])  3.89 us
  transfers between devices with their start and end apart: 11, of which 9 were waited for; matrix products, arithmetic and copies ran while one was open for 1% of the time, Pallas kernels for 10%

profile of v7, /device:TPU:1, one launch (start us, length us, event | category | flops | bytes accessed | tf_op | source)
XLA Modules:
  0.0 154.4 jit_solution(15547830734417817643)
XLA Ops:
  0.6 1.3 shard_map.104.refs_1_
  2.0 8.8 %collective-permute-start = (s32[2,128]{1,0:T(2,128)}, s32[2,128]{1,0:T(2,128)S(1)}, u32[]{:S(2)}, u32[]{:S(2)}) collective-permute-start(s32[2,128]{1,0:T(2,128)} %shard_map.104.refs_1_), channel_id=1, source_target_pairs={{0,32},{32,0},{1,33},{33,1},{2,34},{34,2},{3,35},{35,3},{4,36},{36... | collective-permute-start | bytes 3080 | tf_op jit(solution)/shard_map/ppermute | solution.py:584
  10.8 0.1 pad_add_fusion.refs_0_
  10.8 0.0 copy-start.1
  10.8 0.9 collective-permute-done.refs_2_
  11.8 2.2 %shard_map.105 = (s32[256,128]{1,0:T(8,128)}, s32[1,256]{1,0:T(1,128)}, s32[1,256]{1,0:T(1,128)}) custom-call(s32[2]{0:T(128)S(1)} %pad_add_fusion.refs_0_, s32[2,128]{1,0:T(2,128)} %shard_map.104.refs_1_, s32[2,128]{1,0:T(2,128)S(1)} %collective-permute-done.refs_2_, s32[1,512]{1,0:T(1,128)} %bitcast.28), custom_call_target="tpu_custom_call" | custom-call | flops 33554432 | bytes 137224 | tf_op jit(solution)/shard_map/pallas_call | solution.py:58
  14.0 17.0 %all-to-all-start = ((s32[256,1,128]{2,1,0:T(1,128)}), s32[256,1,128]{2,1,0:T(1,128)S(1)}, u32[]{:S(2)}, u32[]{:S(2)}) async-start(s32[256,1,128]{2,1,0:T(1,128)} %bitcast.23), calls=%async_computation | async-start | bytes 262144 | tf_op jit(solution)/shard_map/all_to_all | solution.py:602
  31.0 1.7 %collective-permute-start.2 = (bf16[128,512]{1,0:T(8,128)(2,1)}, bf16[128,512]{1,0:T(8,128)(2,1)S(1)}, u32[]{:S(2)}, u32[]{:S(2)}) collective-permute-start(bf16[128,512]{1,0:T(8,128)(2,1)} %bitcast.19), channel_id=1, source_target_pairs={{0,64},{32,96},{64,128},{96,160},{128,192},{160,224},{192,256},{22... | collective-permute-start | bytes 393224 | tf_op jit(solution)/shard_map/ppermute | solution.py:580
  32.7 4.4 %collective-permute-start.1 = (bf16[128,512]{1,0:T(8,128)(2,1)}, bf16[128,512]{1,0:T(8,128)(2,1)S(1)}, u32[]{:S(2)}, u32[]{:S(2)}) collective-permute-start(bf16[128,512]{1,0:T(8,128)(2,1)} %bitcast.20), channel_id=1, source_target_pairs={{0,32},{32,64},{64,96},{96,128},{128,160},{160,192},{192,224},{224... | collective-permute-start | bytes 393224 | tf_op jit(solution)/shard_map/ppermute | solution.py:580
  37.1 6.1 %all-to-all-done = s32[256,1,128]{2,1,0:T(1,128)S(1)} async-done(((s32[256,1,128]{2,1,0:T(1,128)}), s32[256,1,128]{2,1,0:T(1,128)S(1)}, u32[]{:S(2)}, u32[]{:S(2)}) %all-to-all-start) | async-done | bytes 131104 | tf_op jit(solution)/shard_map/all_to_all | solution.py:602
  43.2 0.0 copy-start
  43.2 2.6 %shard_map.106 = bf16[5120,128]{1,0:T(8,128)(2,1)} custom-call(s32[256,128]{1,0:T(8,128)S(1)} %bitcast.17, bf16[256,512]{1,0:T(8,128)(2,1)} %refs_1_.5), custom_call_target="tpu_custom_call" | custom-call | flops 335544320 | bytes 1703936 | tf_op jit(solution)/shard_map/pallas_call | solution.py:58
  45.8 0.0 collective-permute-done.2.refs_2_
  45.8 0.0 collective-permute-done.1.refs_3_
  45.8 0.0 copy-start.2
  45.8 0.0 copy-done
  45.9 11.3 %all-to-all-start.1 = ((bf16[256,5,4,128]{3,2,1,0:T(4,128)(2,1)}), bf16[256,5,4,128]{3,2,1,0:T(4,128)(2,1)S(1)}, u32[]{:S(2)}, u32[]{:S(2)}) async-start(bf16[256,5,4,128]{3,2,1,0:T(4,128)(2,1)} %bitcast.8), calls=%async_computation.1 | async-start | bytes 2621440 | tf_op jit(solution)/shard_map/all_to_all | solution.py:602
  57.2 0.0 copy-done.2
  57.2 5.9 %shard_map.107 = (f32[128,512]{1,0:T(8,128)}, f32[128,128]{1,0:T(8,128)}, f32[128,512]{1,0:T(8,128)}, f32[128,128]{1,0:T(8,128)}, bf16[128,512]{1,0:T(8,128)(2,1...) custom-call(s32[2]{0:T(128)S(1)} %pad_add_fusion.refs_0_, ...), custom_call_target="tpu_custom_call" | custom-call | flops 805306368 | bytes 5900360 | tf_op jit(solution)/shard_map/pallas_call | solution.py:58
  63.1 5.2 %collective-permute-start.3 = (bf16[128,512]{1,0:T(8,128)(2,1)}, bf16[128,512]{1,0:T(8,128)(2,1)S(1)}, u32[]{:S(2)}, u32[]{:S(2)}) collective-permute-start(bf16[128,512]{1,0:T(8,128)(2,1)} %get-tuple-element.39), channel_id=1, source_target_pairs={{0,32},{32,0},{1,33},{33,1},{2,34},{34,2},{3,35},{35,3},{4,36},{36... | collective-permute-start | bytes 393224 | tf_op jit(solution)/shard_map/ppermute | solution.py:584
  68.3 1.0 collective-permute-done.3
  69.3 1.8 %maximum_select_fusion.refs_4_.refs_5_ = bf16[256,512]{1,0:T(8,128)(2,1)} fusion(bf16[128,512]{1,0:T(8,128)(2,1)S(1)} %collective-permute-done.3, bf16[128,512]{1,0:T(8,128)(2,1)} %get-tuple-element.39, pred[]{:T(512)S(6)} %eq.3), kind=kLoop, calls=%fused_computation | loop fusion | flops 1179648 | bytes 524289 | tf_op jit(solution)/shard_map/jit(_where)/select_n | solution.py:605
  71.1 19.6 %all-to-all-done.1 = bf16[256,5,4,128]{3,2,1,0:T(4,128)(2,1)S(1)} async-done(((bf16[256,5,4,128]{3,2,1,0:T(4,128)(2,1)}), bf16[256,5,4,128]{3,2,1,0:T(4,128)(2,1)S(1)}, u32[]{:S(2)}, u32[]{:S(2)}) %all-to-all-start.1) | async-done | bytes 1310752 | tf_op jit(solution)/shard_map/all_to_all | solution.py:602
  90.7 2.7 %shard_map.108 = (f32[2,256]{1,0:T(2,128)S(1)}, f32[256,256]{1,0:T(8,128)}, bf16[256,512]{1,0:T(8,128)(2,1)}, bf16[256,512]{1,0:T(8,128)(2,1)}) custom-call(s32[2]{0:T(128)S(1)} %pad_add_fusion.refs_0_, bf16[5120,128]{1,0:T(8,128)(2,1)S(1)} %bitcast.15, s32[1,256]{1,0:T(1,128)} %get-tuple-element.35.refs_2_, s32[1,256]{1,0:T(1,128)} %get-tuple-element.36.refs_3_.refs_6_, ...), custom_call_target="tpu_custom_call" | custom-call | flops 201326592 | bytes 2363400 | tf_op jit(solution)/shard_map/pallas_call | solution.py:58
  93.4 6.9 %collective-permute-start.4 = (f32[2,256]{1,0:T(2,128)S(1)}, f32[2,256]{1,0:T(2,128)S(1)}, u32[]{:S(2)}, u32[]{:S(2)}) collective-permute-start(f32[2,256]{1,0:T(2,128)S(1)} %get-tuple-element.40.refs_1_), channel_id=1, source_target_pairs={{0,32},{32,0},{1,33},{33,1},{2,34},{34,2},{3,35},{35,3},{4,36},{36... | collective-permute-start | bytes 6152 | tf_op jit(solution)/shard_map/ppermute | solution.py:584
  100.4 0.8 collective-permute-done.4.refs_2_
  101.2 0.0 copy-done.1
  101.2 3.9 %shard_map.109 = (bf16[5120,128]{1,0:T(8,128)(2,1)}, f32[128,512]{1,0:T(8,128)}, f32[128,512]{1,0:T(8,128)}) custom-call(s32[2]{0:T(128)S(1)} %pad_add_fusion.refs_0_, f32[2,256]{1,0:T(2,128)S(1)} %get-tuple-element.40.refs_1_, f32[2,256]{1,0:T(2,128)S(1)} %collective-permute-done.4.refs_2_, bf16[256,512]{1,0:T(8,128)(2,1)} %get-tuple-element.41.refs_3_, ...), custom_call_target="tpu_custom_call" | custom-call | flops 268435456 | bytes 2888712 | tf_op jit(solution)/shard_map/pallas_call | solution.py:58
  105.1 0.0 copy-start.4
  105.1 9.3 %all-to-all-start.2 = ((bf16[256,5,4,128]{3,2,1,0:T(4,128)(2,1)}), bf16[256,5,4,128]{3,2,1,0:T(4,128)(2,1)S(1)}, u32[]{:S(2)}, u32[]{:S(2)}) async-start(bf16[256,5,4,128]{3,2,1,0:T(4,128)(2,1)} %bitcast.11), calls=%async_computation.2 | async-start | bytes 2621440 | tf_op jit(solution)/shard_map/all_to_all | solution.py:602
  114.5 0.0 copy-done.4
  114.5 2.2 %collective-permute-start.5 = (f32[128,512]{1,0:T(8,128)S(1)}, f32[128,512]{1,0:T(8,128)S(1)}, u32[]{:S(2)}, u32[]{:S(2)}) collective-permute-start(f32[128,512]{1,0:T(8,128)S(1)} %copy-done.4), channel_id=1, source_target_pairs={{0,32},{32,0},{1,33},{33,1},{2,34},{34,2},{3,35},{35,3},{4,36},{36... | collective-permute-start | bytes 786440 | tf_op jit(solution)/shard_map/ppermute | solution.py:584
  116.7 1.2 collective-permute-done.5.refs_3_
  117.9 0.0 copy-start.3
  117.9 0.7 copy-done.3
  118.6 7.0 %shard_map.110 = (f32[128,1024]{1,0:T(8,128)}, bf16[128,1024]{1,0:T(8,128)(2,1)}, bf16[128,1024]{1,0:T(8,128)(2,1)}, f32[128,512]{1,0:T(8,128)}, f32[128,512]{1,0:T(8,128)}) custom-call(s32[2]{0:T(128)} %copy-done.1, s32[1,16]{1,0:T(1,128)} %refs_1_.7, f32[128,512]{1,0:T(8,128)} %get-tuple-element.45.refs_2_, f32[128,512]{1,0:T(8,128)} %copy-done.3, ...), custom_call_target="tpu_custom_call" | custom-call | flops 805306368 | bytes 6946888 | tf_op jit(solution)/shard_map/pallas_call | solution.py:58
  125.6 2.2 %collective-permute-start.6 = (bf16[128,1024]{1,0:T(8,128)(2,1)}, bf16[128,1024]{1,0:T(8,128)(2,1)S(1)}, u32[]{:S(2)}, u32[]{:S(2)}) collective-permute-start(bf16[128,1024]{1,0:T(8,128)(2,1)} %get-tuple-element.56), channel_id=1, source_target_pairs={{32,0},{64,32},{96,64},{128,96},{160,128},{192,160},{224,192},{256... | collective-permute-start | bytes 786440 | tf_op jit(solution)/shard_map/ppermute | solution.py:580
  127.8 1.3 collective-permute-start.7
  129.1 19.2 %collective-permute-done.6.refs_1_ = bf16[128,1024]{1,0:T(8,128)(2,1)S(1)} collective-permute-done((bf16[128,1024]{1,0:T(8,128)(2,1)}, bf16[128,1024]{1,0:T(8,128)(2,1)S(1)}, u32[]{:S(2)}, u32[]{:S(2)}) %collective-permute-start.6) | collective-permute-done | bytes 262176 | tf_op jit(solution)/shard_map/ppermute | solution.py:580
  148.4 0.4 collective-permute-done.7.refs_2_
  148.8 2.0 %all-to-all-done.2 = bf16[256,5,4,128]{3,2,1,0:T(4,128)(2,1)S(1)} async-done(((bf16[256,5,4,128]{3,2,1,0:T(4,128)(2,1)}), bf16[256,5,4,128]{3,2,1,0:T(4,128)(2,1)S(1)}, u32[]{:S(2)}, u32[]{:S(2)}) %all-to-all-start.2) | async-done | bytes 1310752 | tf_op jit(solution)/shard_map/all_to_all | solution.py:602
  150.8 3.4 %shard_map.111 = (bf16[256,512]{1,0:T(8,128)(2,1)}, bf16[128,512]{1,0:T(8,128)(2,1)}) custom-call(bf16[5120,128]{1,0:T(8,128)(2,1)S(1)} %bitcast.16, bf16[128,1024]{1,0:T(8,128)(2,1)S(1)} %collective-permute-done.6.refs_1_, bf16[128,1024]{1,0:T(8,128)(2,1)S(1)} %collective-permute-done.7.refs_2_, s32[256,128]{1,0:T(8,128)} %bitcast.18, ...), custom_call_target="tpu_custom_call" | custom-call | flops 335544320 | bytes 6162432 | tf_op jit(solution)/shard_map/pallas_call | solution.py:58
Async XLA Ops:
  2.0 9.8 %collective-permute-start = (s32[2,128]{1,0:T(2,128)}, s32[2,128]{1,0:T(2,128)S(1)}, u32[]{:S(2)}, u32[]{:S(2)}) collective-permute-start(s32[2,128]{1,0:T(2,128)} %shard_map.104.refs_1_), channel_id=1, source_target_pairs={{0,32},{32,0},{1,33},{33,1},{2,34},{34,2},{3,35},{35,3},{4,36},{36... | collective-permute-start | bytes 3080 | tf_op jit(solution)/shard_map/ppermute | solution.py:584
  10.8 90.3 %copy-start.1 = (s32[2]{0:T(128)}, s32[2]{0:T(128)S(1)}, u32[]{:S(2)}) copy-start(s32[2]{0:T(128)S(1)} %pad_add_fusion.refs_0_) | copy-start | bytes 28
  14.0 29.2 %all-to-all-start = ((s32[256,1,128]{2,1,0:T(1,128)}), s32[256,1,128]{2,1,0:T(1,128)S(1)}, u32[]{:S(2)}, u32[]{:S(2)}) async-start(s32[256,1,128]{2,1,0:T(1,128)} %bitcast.23), calls=%async_computation | async-start | bytes 262144 | tf_op jit(solution)/shard_map/all_to_all | solution.py:602
  31.0 14.8 %collective-permute-start.2 = (bf16[128,512]{1,0:T(8,128)(2,1)}, bf16[128,512]{1,0:T(8,128)(2,1)S(1)}, u32[]{:S(2)}, u32[]{:S(2)}) collective-permute-start(bf16[128,512]{1,0:T(8,128)(2,1)} %bitcast.19), channel_id=1, source_target_pairs={{0,64},{32,96},{64,128},{96,160},{128,192},{160,224},{192,256},{22... | collective-permute-start | bytes 393224 | tf_op jit(solution)/shard_map/ppermute | solution.py:580
  32.7 13.1 %collective-permute-start.1 = (bf16[128,512]{1,0:T(8,128)(2,1)}, bf16[128,512]{1,0:T(8,128)(2,1)S(1)}, u32[]{:S(2)}, u32[]{:S(2)}) collective-permute-start(bf16[128,512]{1,0:T(8,128)(2,1)} %bitcast.20), channel_id=1, source_target_pairs={{0,32},{32,64},{64,96},{96,128},{128,160},{160,192},{192,224},{224... | collective-permute-start | bytes 393224 | tf_op jit(solution)/shard_map/ppermute | solution.py:580
  43.2 2.6 %copy-start = (s32[256,1,128]{2,1,0:T(1,128)}, s32[256,1,128]{2,1,0:T(1,128)S(1)}, u32[]{:S(2)}) copy-start(s32[256,1,128]{2,1,0:T(1,128)S(1)} %all-to-all-done) | copy-start | bytes 393220
  45.8 11.3 %copy-start.2 = (s32[1,16]{1,0:T(1,128)S(1)}, s32[1,16]{1,0:T(1,128)}, u32[]{:S(2)}) copy-start(s32[1,16]{1,0:T(1,128)} %refs_1_.7) | copy-start | bytes 196
  45.9 44.8 %all-to-all-start.1 = ((bf16[256,5,4,128]{3,2,1,0:T(4,128)(2,1)}), bf16[256,5,4,128]{3,2,1,0:T(4,128)(2,1)S(1)}, u32[]{:S(2)}, u32[]{:S(2)}) async-start(bf16[256,5,4,128]{3,2,1,0:T(4,128)(2,1)} %bitcast.8), calls=%async_computation.1 | async-start | bytes 2621440 | tf_op jit(solution)/shard_map/all_to_all | solution.py:602
  63.1 6.2 %collective-permute-start.3 = (bf16[128,512]{1,0:T(8,128)(2,1)}, bf16[128,512]{1,0:T(8,128)(2,1)S(1)}, u32[]{:S(2)}, u32[]{:S(2)}) collective-permute-start(bf16[128,512]{1,0:T(8,128)(2,1)} %get-tuple-element.39), channel_id=1, source_target_pairs={{0,32},{32,0},{1,33},{33,1},{2,34},{34,2},{3,35},{35,3},{4,36},{36... | collective-permute-start | bytes 393224 | tf_op jit(solution)/shard_map/ppermute | solution.py:584
  93.4 7.8 %collective-permute-start.4 = (f32[2,256]{1,0:T(2,128)S(1)}, f32[2,256]{1,0:T(2,128)S(1)}, u32[]{:S(2)}, u32[]{:S(2)}) collective-permute-start(f32[2,256]{1,0:T(2,128)S(1)} %get-tuple-element.40.refs_1_), channel_id=1, source_target_pairs={{0,32},{32,0},{1,33},{33,1},{2,34},{34,2},{3,35},{35,3},{4,36},{36... | collective-permute-start | bytes 6152 | tf_op jit(solution)/shard_map/ppermute | solution.py:584
  105.1 9.3 %copy-start.4 = (f32[128,512]{1,0:T(8,128)S(1)}, f32[128,512]{1,0:T(8,128)}, u32[]{:S(2)}) copy-start(f32[128,512]{1,0:T(8,128)} %get-tuple-element.46) | copy-start | bytes 786436
  105.1 45.6 %all-to-all-start.2 = ((bf16[256,5,4,128]{3,2,1,0:T(4,128)(2,1)}), bf16[256,5,4,128]{3,2,1,0:T(4,128)(2,1)S(1)}, u32[]{:S(2)}, u32[]{:S(2)}) async-start(bf16[256,5,4,128]{3,2,1,0:T(4,128)(2,1)} %bitcast.11), calls=%async_computation.2 | async-start | bytes 2621440 | tf_op jit(solution)/shard_map/all_to_all | solution.py:602
  114.5 3.4 %collective-permute-start.5 = (f32[128,512]{1,0:T(8,128)S(1)}, f32[128,512]{1,0:T(8,128)S(1)}, u32[]{:S(2)}, u32[]{:S(2)}) collective-permute-start(f32[128,512]{1,0:T(8,128)S(1)} %copy-done.4), channel_id=1, source_target_pairs={{0,32},{32,0},{1,33},{33,1},{2,34},{34,2},{3,35},{35,3},{4,36},{36... | collective-permute-start | bytes 786440 | tf_op jit(solution)/shard_map/ppermute | solution.py:584
  117.9 0.7 copy-start.3
  125.6 22.8 %collective-permute-start.6 = (bf16[128,1024]{1,0:T(8,128)(2,1)}, bf16[128,1024]{1,0:T(8,128)(2,1)S(1)}, u32[]{:S(2)}, u32[]{:S(2)}) collective-permute-start(bf16[128,1024]{1,0:T(8,128)(2,1)} %get-tuple-element.56), channel_id=1, source_target_pairs={{32,0},{64,32},{96,64},{128,96},{160,128},{192,160},{224,192},{256... | collective-permute-start | bytes 786440 | tf_op jit(solution)/shard_map/ppermute | solution.py:580
  127.8 20.9 %collective-permute-start.7 = (bf16[128,1024]{1,0:T(8,128)(2,1)}, bf16[128,1024]{1,0:T(8,128)(2,1)S(1)}, u32[]{:S(2)}, u32[]{:S(2)}) collective-permute-start(bf16[128,1024]{1,0:T(8,128)(2,1)} %get-tuple-element.57), channel_id=1, source_target_pairs={{64,0},{96,32},{128,64},{160,96},{192,128},{224,160},{256,192},{28... | collective-permute-start | bytes 786440 | tf_op jit(solution)/shard_map/ppermute | solution.py:580

commit v8 on v6

--- a/solution.py
+++ b/solution.py
@@ -528,8 +528,9 @@
 def last_kernel(
     items,
     loaded,
+    place_ref,
     returned_ref,
-    near_ref,
+    summed_ref,
     far_ref,
     asks_ref,
     own_grad_ref,
@@ -539,6 +540,7 @@
     gain_ref,
     hist_ref,
     user_grad_ref,
+    near_ref,
     table_grad_ref,
     history_grad_ref,
     wide,
@@ -562,7 +564,8 @@
     copy = pltpu.make_async_copy(held, table_grad_ref, held_sem)
     copy.start()
     loaded()
-    come = near_ref[...].astype(F32) + far_ref[...].astype(F32)
+    near = jnp.where(place_ref[1] == 0, near_ref[...].astype(F32), summed_ref[...].astype(F32))
+    come = near + far_ref[...].astype(F32)
     proj_grad = ((own_grad_ref[...] + come) * slope_ref[...]).astype(BF16)
     in_grad = (
         in_part_ref[...]
@@ -580,6 +583,12 @@
     count = lax.axis_size(axes)
     pairs = [(i, i + by) for i in range(count) if 0 <= i + by < count]
     return lax.ppermute(shard, axes, pairs)
+
+
+def from_first_core(shard, by):
+    axes = ("z", "core")
+    count = lax.axis_size(axes)
+    return lax.ppermute(shard, axes, [(i, i - by) for i in range(0, count, 2) if i >= by])
 
 
 def swapped(shard):
@@ -728,15 +737,18 @@
         ),
         2 * n * width * width * 12,
     )
-    near_back = passed_along(near_grad, -1)
-    far_back = passed_along(far_grad, -2)
+    near_chip = swapped(near_grad)
+    summed = (near_grad.astype(F32) + swapped(far_grad).astype(F32)).astype(BF16)
+    summed_back = from_first_core(summed, 1)
+    far_back = from_first_core(far_grad, 2)
     table_grad, history_grad = call(
         functools.partial(last_kernel, items),
         [shaped((rows, width), BF16), shaped((n, width), BF16)],
-        [VMEM] * 3 + [None] * 8,
+        [SMEM] + [VMEM] * 3 + [None] * 9,
         (
+            place,
             returned,
-            near_back,
+            summed_back,
             far_back,
             asks,
             own_grad,
@@ -746,6 +758,7 @@
             gain,
             own,
             user_grad,
+            near_chip,
         ),
         2 * SEATS * chips * rows * width,
         [staging[1], pltpu.VMEM((rows, width), BF16), pltpu.SemaphoreType.DMA(())],

time: 152 us -> 153 us (level)
  waiting for transfers between devices: 49 us -> 44.5 us
  starting transfers between devices: 68.7 us -> 72.1 us
    ppermute x4 -> x2, waiting for transfers between devices: 19.6 us -> 0.01 us  [passed_along(): return lax.ppermute(shard, axes, pairs)]
    ppermute x0 -> x2, waiting for transfers between devices: none -> 15.1 us  [from_first_core(): lax.ppermute(shard, axes, [(i, i - by) for i in range(0, count, 2) if i >...]
    ppermute x4 -> x6, starting transfers between devices: 15.9 us -> 20.8 us  [swapped(): return lax.ppermute(shard, 'core', [(0, 1), (1, 0)])]
    ppermute x4 -> x2, starting transfers between devices: 11.4 us -> 7.85 us  [passed_along(): return lax.ppermute(shard, axes, pairs)]
    ppermute x0 -> x2, starting transfers between devices: none -> 1.97 us  [from_first_core(): lax.ppermute(shard, axes, [(i, i - by) for i in range(0, count, 2) if i >...]
  transfers between devices with their start and end apart: 11 -> 13, of which waited for: 8 -> 7; matrix products, arithmetic and copies ran while one was open for 3% -> 4% of each run, Pallas kernels for 10% -> 10%
where the time goes in v8:
time: 153 us; the launch traced here: 152 us
  starting transfers between devices  72.1 us (47%)
  waiting for transfers between devices  44.5 us (29%)
  Pallas kernels  28.1 us (18%)
  other arithmetic  4.1 us (3%)
  local copies, waits for them, and re-layouts  2.03 us (1%)
    all_to_all x3, starting transfers between devices, exchange(): lax.all_to_all(split, axes, split_axis=0, concat_axis=0, tiled=True)  41.5 us
    pallas_call x7, Pallas kernels, call(): pl.pallas_call(body, out_shape=tuple(outs), in_specs=[HBM if spec is None...  28.1 us
    all_to_all x3, waiting for transfers between devices, exchange(): lax.all_to_all(split, axes, split_axis=0, concat_axis=0, tiled=True)  27.3 us
    ppermute x6, starting transfers between devices, swapped(): return lax.ppermute(shard, 'core', [(0, 1), (1, 0)])  20.8 us
    ppermute x2, waiting for transfers between devices, from_first_core(): lax.ppermute(shard, axes, [(i, i - by) for i in range(0, count, 2) if i >...  15.1 us
    ppermute x2, starting transfers between devices, passed_along(): return lax.ppermute(shard, axes, pairs)  7.85 us
  transfers between devices with their start and end apart: 13, of which 7 were waited for; matrix products, arithmetic and copies ran while one was open for 4% of the time, Pallas kernels for 10%

profile of v8, /device:TPU:1, one launch (start us, length us, event | category | flops | bytes accessed | tf_op | source)
XLA Modules:
  0.0 151.8 jit_solution(1135305805139548740)
XLA Ops:
  0.6 1.7 %shard_map.104 = (s32[512,128]{1,0:T(8,128)}, s32[1,128]{1,0:T(1,128)}, s32[128,1]{1,0:T(8,128)}) custom-call(s32[1,128]{1,0:T(1,128)} %bitcast.33, s32[1,128]{1,0:T(1,128)} %refs_1_.4, s32[1,512]{1,0:T(1,128)} %bitcast.31), custom_call_target="tpu_custom_call" | custom-call | flops 33554432 | bytes 266240 | tf_op jit(solution)/shard_map/pallas_call | solution.py:59
  2.4 22.2 %all-to-all-start = ((s32[512,1,128]{2,1,0:T(1,128)}), s32[512,1,128]{2,1,0:T(1,128)S(1)}, u32[]{:S(2)}, u32[]{:S(2)}) async-start(s32[512,1,128]{2,1,0:T(1,128)} %bitcast.27), calls=%async_computation | async-start | bytes 524288 | tf_op jit(solution)/shard_map/all_to_all | solution.py:613
  24.5 3.7 %collective-permute-start.1 = (bf16[128,512]{1,0:T(8,128)(2,1)}, bf16[128,512]{1,0:T(8,128)(2,1)S(1)}, u32[]{:S(2)}, u32[]{:S(2)}) collective-permute-start(bf16[128,512]{1,0:T(8,128)(2,1)} %bitcast.23), channel_id=1, source_target_pairs={{0,64},{32,96},{64,128},{96,160},{128,192},{160,224},{192,256},{22... | collective-permute-start | bytes 393224 | tf_op jit(solution)/shard_map/ppermute | solution.py:585
  28.2 4.2 %collective-permute-start = (bf16[128,512]{1,0:T(8,128)(2,1)}, bf16[128,512]{1,0:T(8,128)(2,1)S(1)}, u32[]{:S(2)}, u32[]{:S(2)}) collective-permute-start(bf16[128,512]{1,0:T(8,128)(2,1)} %bitcast.24), channel_id=1, source_target_pairs={{0,32},{32,64},{64,96},{96,128},{128,160},{160,192},{192,224},{224... | collective-permute-start | bytes 393224 | tf_op jit(solution)/shard_map/ppermute | solution.py:585
  32.4 8.9 %all-to-all-done = s32[512,1,128]{2,1,0:T(1,128)S(1)} async-done(((s32[512,1,128]{2,1,0:T(1,128)}), s32[512,1,128]{2,1,0:T(1,128)S(1)}, u32[]{:S(2)}, u32[]{:S(2)}) %all-to-all-start) | async-done | bytes 262176 | tf_op jit(solution)/shard_map/all_to_all | solution.py:613
  41.3 2.6 %shard_map.105 = bf16[5120,128]{1,0:T(8,128)(2,1)} custom-call(s32[512,128]{1,0:T(8,128)S(1)} %bitcast.21, bf16[256,512]{1,0:T(8,128)(2,1)} %refs_1_.5), custom_call_target="tpu_custom_call" | custom-call | flops 335544320 | bytes 1835008 | tf_op jit(solution)/shard_map/pallas_call | solution.py:59
  43.9 0.0 collective-permute-done.1.refs_2_
  43.9 0.0 collective-permute-done.refs_3_
  43.9 0.0 copy-start.7
  43.9 0.0 copy-start.6
  44.0 0.0 copy-start.3
  44.0 10.0 %all-to-all-start.1 = ((bf16[256,5,4,128]{3,2,1,0:T(4,128)(2,1)}), bf16[256,5,4,128]{3,2,1,0:T(4,128)(2,1)S(1)}, u32[]{:S(2)}, u32[]{:S(2)}) async-start(bf16[256,5,4,128]{3,2,1,0:T(4,128)(2,1)} %bitcast.8), calls=%async_computation.1 | async-start | bytes 2621440 | tf_op jit(solution)/shard_map/all_to_all | solution.py:613
  54.0 4.7 %collective-permute-start.2 = (s32[1,128]{1,0:T(1,128)S(1)}, s32[1,128]{1,0:T(1,128)S(1)}, u32[]{:S(2)}, u32[]{:S(2)}) collective-permute-start(s32[1,128]{1,0:T(1,128)S(1)} %copy-done.7), channel_id=1, source_target_pairs={{0,32},{32,0},{1,33},{33,1},{2,34},{34,2},{3,35},{35,3},{4,36},{36... | collective-permute-start | bytes 1544 | tf_op jit(solution)/shard_map/ppermute | solution.py:595
  58.7 0.5 broadcast.11
  59.2 0.0 copy-done.6
  59.2 0.7 reduce.3
  59.9 0.1 reshape.96
  60.0 0.1 pad_add_fusion.refs_0_
  60.1 5.9 %shard_map.106 = (f32[128,512]{1,0:T(8,128)}, f32[128,128]{1,0:T(8,128)}, f32[128,512]{1,0:T(8,128)}, f32[128,128]{1,0:T(8,128)}, bf16[128,512]{1,0:T(8,128)(2,1...) custom-call(s32[2]{0:T(128)S(1)} %pad_add_fusion.refs_0_, ...), custom_call_target="tpu_custom_call" | custom-call | flops 805306368 | bytes 5900360 | tf_op jit(solution)/shard_map/pallas_call | solution.py:59
  65.9 1.9 %collective-permute-start.3 = (bf16[128,512]{1,0:T(8,128)(2,1)}, bf16[128,512]{1,0:T(8,128)(2,1)S(1)}, u32[]{:S(2)}, u32[]{:S(2)}) collective-permute-start(bf16[128,512]{1,0:T(8,128)(2,1)} %get-tuple-element.37), channel_id=1, source_target_pairs={{0,32},{32,0},{1,33},{33,1},{2,34},{34,2},{3,35},{35,3},{4,36},{36... | collective-permute-start | bytes 393224 | tf_op jit(solution)/shard_map/ppermute | solution.py:595
  67.9 0.7 reshape.97.refs_2_
  68.5 0.0 collective-permute-done.2
  68.5 0.6 broadcast_select_fusion.refs_3_.refs_6_
  69.1 0.2 collective-permute-done.3
  69.4 1.8 %maximum_select_fusion.refs_4_.refs_5_ = bf16[256,512]{1,0:T(8,128)(2,1)} fusion(bf16[128,512]{1,0:T(8,128)(2,1)S(1)} %collective-permute-done.3, bf16[128,512]{1,0:T(8,128)(2,1)} %get-tuple-element.37, pred[]{:T(512)S(6)} %eq.4), kind=kLoop, calls=%fused_computation.1 | loop fusion | flops 1179648 | bytes 524289 | tf_op jit(solution)/shard_map/jit(_where)/select_n | solution.py:616
  71.1 16.5 %all-to-all-done.1 = bf16[256,5,4,128]{3,2,1,0:T(4,128)(2,1)S(1)} async-done(((bf16[256,5,4,128]{3,2,1,0:T(4,128)(2,1)}), bf16[256,5,4,128]{3,2,1,0:T(4,128)(2,1)S(1)}, u32[]{:S(2)}, u32[]{:S(2)}) %all-to-all-start.1) | async-done | bytes 1310752 | tf_op jit(solution)/shard_map/all_to_all | solution.py:613
  87.6 2.7 %shard_map.107 = (f32[2,256]{1,0:T(2,128)S(1)}, f32[256,256]{1,0:T(8,128)}, bf16[256,512]{1,0:T(8,128)(2,1)}, bf16[256,512]{1,0:T(8,128)(2,1)}) custom-call(s32[2]{0:T(128)S(1)} %pad_add_fusion.refs_0_, bf16[5120,128]{1,0:T(8,128)(2,1)S(1)} %bitcast.19, s32[1,256]{1,0:T(1,128)} %reshape.97.refs_2_, s32[1,256]{1,0:T(1,128)} %broadcast_select_fusion.refs_3_.refs_6_, ...), custom_call_target="tpu_custom_call" | custom-call | flops 201326592 | bytes 2363400 | tf_op jit(solution)/shard_map/pallas_call | solution.py:59
  90.3 7.0 %collective-permute-start.4 = (f32[2,256]{1,0:T(2,128)S(1)}, f32[2,256]{1,0:T(2,128)S(1)}, u32[]{:S(2)}, u32[]{:S(2)}) collective-permute-start(f32[2,256]{1,0:T(2,128)S(1)} %get-tuple-element.38.refs_1_), channel_id=1, source_target_pairs={{0,32},{32,0},{1,33},{33,1},{2,34},{34,2},{3,35},{35,3},{4,36},{36... | collective-permute-start | bytes 6152 | tf_op jit(solution)/shard_map/ppermute | solution.py:595
  97.3 0.6 collective-permute-done.4.refs_2_
  98.0 0.0 copy-done.1
  98.0 4.0 %shard_map.108 = (bf16[5120,128]{1,0:T(8,128)(2,1)}, f32[128,512]{1,0:T(8,128)}, f32[128,512]{1,0:T(8,128)}) custom-call(s32[2]{0:T(128)S(1)} %pad_add_fusion.refs_0_, f32[2,256]{1,0:T(2,128)S(1)} %get-tuple-element.38.refs_1_, f32[2,256]{1,0:T(2,128)S(1)} %collective-permute-done.4.refs_2_, bf16[256,512]{1,0:T(8,128)(2,1)} %get-tuple-element.39.refs_3_, ...), custom_call_target="tpu_custom_call" | custom-call | flops 268435456 | bytes 2888712 | tf_op jit(solution)/shard_map/pallas_call | solution.py:59
  101.9 9.3 %all-to-all-start.2 = ((bf16[256,5,4,128]{3,2,1,0:T(4,128)(2,1)}), bf16[256,5,4,128]{3,2,1,0:T(4,128)(2,1)S(1)}, u32[]{:S(2)}, u32[]{:S(2)}) async-start(bf16[256,5,4,128]{3,2,1,0:T(4,128)(2,1)} %bitcast.11), calls=%async_computation.2 | async-start | bytes 2621440 | tf_op jit(solution)/shard_map/all_to_all | solution.py:613
  111.3 2.2 %collective-permute-start.5 = (f32[128,512]{1,0:T(8,128)S(1)}, f32[128,512]{1,0:T(8,128)S(1)}, u32[]{:S(2)}, u32[]{:S(2)}) collective-permute-start(f32[128,512]{1,0:T(8,128)S(1)} %copy-done.8), channel_id=1, source_target_pairs={{0,32},{32,0},{1,33},{33,1},{2,34},{34,2},{3,35},{35,3},{4,36},{36... | collective-permute-start | bytes 786440 | tf_op jit(solution)/shard_map/ppermute | solution.py:595
  113.5 1.2 collective-permute-done.5.refs_3_
  114.7 0.7 copy-done.5
  115.4 7.1 %shard_map.109 = (f32[128,1024]{1,0:T(8,128)}, bf16[128,1024]{1,0:T(8,128)(2,1)}, bf16[128,1024]{1,0:T(8,128)(2,1)}, f32[128,512]{1,0:T(8,128)}, f32[128,512]{1,0:T(8,128)}) custom-call(s32[2]{0:T(128)} %copy-done.1, s32[1,16]{1,0:T(1,128)} %refs_1_.7, f32[128,512]{1,0:T(8,128)} %get-tuple-element.43.refs_2_, f32[128,512]{1,0:T(8,128)} %copy-done.5, ...), custom_call_target="tpu_custom_call" | custom-call | flops 805306368 | bytes 6946888 | tf_op jit(solution)/shard_map/pallas_call | solution.py:59
  122.5 2.2 %collective-permute-start.6 = (bf16[128,1024]{1,0:T(8,128)(2,1)}, bf16[128,1024]{1,0:T(8,128)(2,1)S(1)}, u32[]{:S(2)}, u32[]{:S(2)}) collective-permute-start(bf16[128,1024]{1,0:T(8,128)(2,1)} %get-tuple-element.55), channel_id=1, source_target_pairs={{0,32},{32,0},{1,33},{33,1},{2,34},{34,2},{3,35},{35,3},{4,36},{36... | collective-permute-start | bytes 786440 | tf_op jit(solution)/shard_map/ppermute | solution.py:595
  124.8 0.7 collective-permute-start.8
  125.5 2.7 %collective-permute-start.9 = (bf16[128,1024]{1,0:T(8,128)(2,1)}, bf16[128,1024]{1,0:T(8,128)(2,1)S(1)}, u32[]{:S(2)}, u32[]{:S(2)}) collective-permute-start(bf16[128,1024]{1,0:T(8,128)(2,1)} %get-tuple-element.54), channel_id=1, source_target_pairs={{0,32},{32,0},{1,33},{33,1},{2,34},{34,2},{3,35},{35,3},{4,36},{36... | collective-permute-start | bytes 786440 | tf_op jit(solution)/shard_map/ppermute | solution.py:595
  128.2 0.0 collective-permute-done.6
  128.2 1.0 add_convert_fusion
  129.2 1.3 collective-permute-start.7
  130.5 0.0 collective-permute-done.9.refs_12_
  130.5 0.0 collective-permute-done.8.refs_3_
  130.5 15.1 %collective-permute-done.7.refs_2_ = bf16[128,1024]{1,0:T(8,128)(2,1)S(1)} collective-permute-done((bf16[128,1024]{1,0:T(8,128)(2,1)S(1)}, bf16[128,1024]{1,0:T(8,128)(2,1)S(1)}, u32[]{:S(2)}, u32[]{:S(2)}) %collective-permute-start.7) | collective-permute-done | bytes 262176 | tf_op jit(solution)/shard_map/ppermute | solution.py:591
  145.6 1.9 %all-to-all-done.2 = bf16[256,5,4,128]{3,2,1,0:T(4,128)(2,1)S(1)} async-done(((bf16[256,5,4,128]{3,2,1,0:T(4,128)(2,1)}), bf16[256,5,4,128]{3,2,1,0:T(4,128)(2,1)S(1)}, u32[]{:S(2)}, u32[]{:S(2)}) %all-to-all-start.2) | async-done | bytes 1310752 | tf_op jit(solution)/shard_map/all_to_all | solution.py:613
  147.6 0.0 copy-done.4
  147.6 4.1 %shard_map.110 = (bf16[256,512]{1,0:T(8,128)(2,1)}, bf16[128,512]{1,0:T(8,128)(2,1)}) custom-call(s32[2]{0:T(128)S(1)} %copy-done.2, bf16[5120,128]{1,0:T(8,128)(2,1)S(1)} %bitcast.20, bf16[128,1024]{1,0:T(8,128)(2,1)S(1)} %collective-permute-done.7.refs_2_, bf16[128,1024]{1,0:T(8,128)(2,1)S(1)} %collective-permute-done.8.refs_3_, s32[512,128]{1,0:T(8,128)} %bitcast.22, ...), custom_call_target="tpu_custom_call" | custom-call | flops 335544320 | bytes 6555656 | tf_op jit(solution)/shard_map/pallas_call | solution.py:59
  (12 shorter events, 0.0 us)
Async XLA Ops:
  2.4 38.9 %all-to-all-start = ((s32[512,1,128]{2,1,0:T(1,128)}), s32[512,1,128]{2,1,0:T(1,128)S(1)}, u32[]{:S(2)}, u32[]{:S(2)}) async-start(s32[512,1,128]{2,1,0:T(1,128)} %bitcast.27), calls=%async_computation | async-start | bytes 524288 | tf_op jit(solution)/shard_map/all_to_all | solution.py:613
  24.5 19.4 %collective-permute-start.1 = (bf16[128,512]{1,0:T(8,128)(2,1)}, bf16[128,512]{1,0:T(8,128)(2,1)S(1)}, u32[]{:S(2)}, u32[]{:S(2)}) collective-permute-start(bf16[128,512]{1,0:T(8,128)(2,1)} %bitcast.23), channel_id=1, source_target_pairs={{0,64},{32,96},{64,128},{96,160},{128,192},{160,224},{192,256},{22... | collective-permute-start | bytes 393224 | tf_op jit(solution)/shard_map/ppermute | solution.py:585
  28.2 15.7 %collective-permute-start = (bf16[128,512]{1,0:T(8,128)(2,1)}, bf16[128,512]{1,0:T(8,128)(2,1)S(1)}, u32[]{:S(2)}, u32[]{:S(2)}) collective-permute-start(bf16[128,512]{1,0:T(8,128)(2,1)} %bitcast.24), channel_id=1, source_target_pairs={{0,32},{32,64},{64,96},{96,128},{128,160},{160,192},{192,224},{224... | collective-permute-start | bytes 393224 | tf_op jit(solution)/shard_map/ppermute | solution.py:585
  41.3 2.7 %copy-start = (s32[512,1,128]{2,1,0:T(1,128)}, s32[512,1,128]{2,1,0:T(1,128)S(1)}, u32[]{:S(2)}) copy-start(s32[512,1,128]{2,1,0:T(1,128)S(1)} %all-to-all-done) | copy-start | bytes 786436
  43.9 10.1 %copy-start.7 = (s32[1,128]{1,0:T(1,128)S(1)}, s32[1,128]{1,0:T(1,128)}, u32[]{:S(2)}) copy-start(s32[1,128]{1,0:T(1,128)} %get-tuple-element.34) | copy-start | bytes 1540
  43.9 15.3 %copy-start.6 = (s32[1,512,1]{1,2,0:T(1,128)S(1)}, s32[1,512,1]{1,2,0:T(1,128)}, u32[]{:S(2)}) copy-start(s32[1,512,1]{1,2,0:T(1,128)} %param.17) | copy-start | bytes 6148
  44.0 16.1 %copy-start.3 = (s32[1,16]{1,0:T(1,128)S(1)}, s32[1,16]{1,0:T(1,128)}, u32[]{:S(2)}) copy-start(s32[1,16]{1,0:T(1,128)} %refs_1_.7) | copy-start | bytes 196
  44.0 43.6 %all-to-all-start.1 = ((bf16[256,5,4,128]{3,2,1,0:T(4,128)(2,1)}), bf16[256,5,4,128]{3,2,1,0:T(4,128)(2,1)S(1)}, u32[]{:S(2)}, u32[]{:S(2)}) async-start(bf16[256,5,4,128]{3,2,1,0:T(4,128)(2,1)} %bitcast.8), calls=%async_computation.1 | async-start | bytes 2621440 | tf_op jit(solution)/shard_map/all_to_all | solution.py:613
  54.0 14.5 %collective-permute-start.2 = (s32[1,128]{1,0:T(1,128)S(1)}, s32[1,128]{1,0:T(1,128)S(1)}, u32[]{:S(2)}, u32[]{:S(2)}) collective-permute-start(s32[1,128]{1,0:T(1,128)S(1)} %copy-done.7), channel_id=1, source_target_pairs={{0,32},{32,0},{1,33},{33,1},{2,34},{34,2},{3,35},{35,3},{4,36},{36... | collective-permute-start | bytes 1544 | tf_op jit(solution)/shard_map/ppermute | solution.py:595
  60.1 37.9 %copy-start.1 = (s32[2]{0:T(128)}, s32[2]{0:T(128)S(1)}, u32[]{:S(2)}) copy-start(s32[2]{0:T(128)S(1)} %pad_add_fusion.refs_0_) | copy-start | bytes 28
  65.9 3.5 %collective-permute-start.3 = (bf16[128,512]{1,0:T(8,128)(2,1)}, bf16[128,512]{1,0:T(8,128)(2,1)S(1)}, u32[]{:S(2)}, u32[]{:S(2)}) collective-permute-start(bf16[128,512]{1,0:T(8,128)(2,1)} %get-tuple-element.37), channel_id=1, source_target_pairs={{0,32},{32,0},{1,33},{33,1},{2,34},{34,2},{3,35},{35,3},{4,36},{36... | collective-permute-start | bytes 393224 | tf_op jit(solution)/shard_map/ppermute | solution.py:595
  90.3 7.6 %collective-permute-start.4 = (f32[2,256]{1,0:T(2,128)S(1)}, f32[2,256]{1,0:T(2,128)S(1)}, u32[]{:S(2)}, u32[]{:S(2)}) collective-permute-start(f32[2,256]{1,0:T(2,128)S(1)} %get-tuple-element.38.refs_1_), channel_id=1, source_target_pairs={{0,32},{32,0},{1,33},{33,1},{2,34},{34,2},{3,35},{35,3},{4,36},{36... | collective-permute-start | bytes 6152 | tf_op jit(solution)/shard_map/ppermute | solution.py:595
  101.9 9.3 %copy-start.8 = (f32[128,512]{1,0:T(8,128)S(1)}, f32[128,512]{1,0:T(8,128)}, u32[]{:S(2)}) copy-start(f32[128,512]{1,0:T(8,128)} %get-tuple-element.44) | copy-start | bytes 786436
  101.9 45.6 %all-to-all-start.2 = ((bf16[256,5,4,128]{3,2,1,0:T(4,128)(2,1)}), bf16[256,5,4,128]{3,2,1,0:T(4,128)(2,1)S(1)}, u32[]{:S(2)}, u32[]{:S(2)}) async-start(bf16[256,5,4,128]{3,2,1,0:T(4,128)(2,1)} %bitcast.11), calls=%async_computation.2 | async-start | bytes 2621440 | tf_op jit(solution)/shard_map/all_to_all | solution.py:613
  111.3 3.4 %collective-permute-start.5 = (f32[128,512]{1,0:T(8,128)S(1)}, f32[128,512]{1,0:T(8,128)S(1)}, u32[]{:S(2)}, u32[]{:S(2)}) collective-permute-start(f32[128,512]{1,0:T(8,128)S(1)} %copy-done.8), channel_id=1, source_target_pairs={{0,32},{32,0},{1,33},{33,1},{2,34},{34,2},{3,35},{35,3},{4,36},{36... | collective-permute-start | bytes 786440 | tf_op jit(solution)/shard_map/ppermute | solution.py:595
  114.7 0.7 copy-start.5
  115.4 32.1 %copy-start.2 = (s32[2]{0:T(128)S(1)}, s32[2]{0:T(128)}, u32[]{:S(2)}) copy-start(s32[2]{0:T(128)} %copy-done.1) | copy-start | bytes 28
  122.5 5.6 %collective-permute-start.6 = (bf16[128,1024]{1,0:T(8,128)(2,1)}, bf16[128,1024]{1,0:T(8,128)(2,1)S(1)}, u32[]{:S(2)}, u32[]{:S(2)}) collective-permute-start(bf16[128,1024]{1,0:T(8,128)(2,1)} %get-tuple-element.55), channel_id=1, source_target_pairs={{0,32},{32,0},{1,33},{33,1},{2,34},{34,2},{3,35},{35,3},{4,36},{36... | collective-permute-start | bytes 786440 | tf_op jit(solution)/shard_map/ppermute | solution.py:595
  124.8 5.7 %collective-permute-start.8 = (bf16[128,1024]{1,0:T(8,128)(2,1)}, bf16[128,1024]{1,0:T(8,128)(2,1)S(1)}, u32[]{:S(2)}, u32[]{:S(2)}) collective-permute-start(bf16[128,1024]{1,0:T(8,128)(2,1)} %get-tuple-element.55), channel_id=1, source_target_pairs={{64,0},{128,64},{192,128},{256,192},{320,256},{384,320},{448,384},... | collective-permute-start | bytes 786440 | tf_op jit(solution)/shard_map/ppermute | solution.py:591
  125.5 5.0 %collective-permute-start.9 = (bf16[128,1024]{1,0:T(8,128)(2,1)}, bf16[128,1024]{1,0:T(8,128)(2,1)S(1)}, u32[]{:S(2)}, u32[]{:S(2)}) collective-permute-start(bf16[128,1024]{1,0:T(8,128)(2,1)} %get-tuple-element.54), channel_id=1, source_target_pairs={{0,32},{32,0},{1,33},{33,1},{2,34},{34,2},{3,35},{35,3},{4,36},{36... | collective-permute-start | bytes 786440 | tf_op jit(solution)/shard_map/ppermute | solution.py:595
  129.2 16.4 %collective-permute-start.7 = (bf16[128,1024]{1,0:T(8,128)(2,1)S(1)}, bf16[128,1024]{1,0:T(8,128)(2,1)S(1)}, u32[]{:S(2)}, u32[]{:S(2)}) collective-permute-start(bf16[128,1024]{1,0:T(8,128)(2,1)S(1)} %add_convert_fusion), channel_id=1, source_target_pairs={{64,32},{128,96},{192,160},{256,224},{320,288},{384,352},{448,416}... | collective-permute-start | bytes 786440 | tf_op jit(solution)/shard_map/ppermute | solution.py:591
  130.5 17.1 %copy-start.4 = (bf16[128,1024]{1,0:T(8,128)(2,1)}, bf16[128,1024]{1,0:T(8,128)(2,1)S(1)}, u32[]{:S(2)}) copy-start(bf16[128,1024]{1,0:T(8,128)(2,1)S(1)} %collective-permute-done.9.refs_12_) | copy-start | bytes 786436
